TPU v7x, 32 devices: a whole 2x2x4 slice. The times are simulated.
32 devices in a mesh: tile: 8 (over z, x), batch: 4 (over y, core).
Axes of the slice: x: 2, y: 2, z: 4, core: 2. Of those that a mesh axis runs over, the one named last changes fastest.
Arguments:
- object_slices: float32 [8, 2, 2, 256, 256], P('tile'), may hold values from -1 to 1
- probe: float32 [2, 2, 128, 128], replicated, may hold values from -6 to 6
- prop_phase: float32 [128, 128], replicated, may hold values from -3.140625 to 3.140625
- scan_offsets: int32 [8, 4, 2], P('tile', 'batch'), may hold values from 0 to 255, as said below
- measured: float32 [8, 4, 128, 128], P('tile', 'batch'), may hold values from 0 to 2
Outputs:
- object_grad: float32 [8, 2, 2, 256, 256], P('tile', None, None, 'batch')
- probe_step: float32 [2, 2, 128, 128], replicated
Inputs may be any that keep to these rules, and one draw needn't show every extreme that they name: `scan_offsets`: offsets are relative to the tile that holds the position. A window never leaves the object: in the last row of the tile grid the row offset is at most 128, in the last column of the tile grid the column offset is at most 128.
All inputs are finite; a program needn't handle non-finite values.
Results may differ from a plain program's by a relative error of at most 0.00012.
Values sent between devices are 32-bit elements; how exact they have to be, the bound alone decides.
No kernel may reach another device: no remote copies, remote signals or barrier semaphores. Data moves between devices by JAX's collectives and lax.ppermute only.
A program may use at most 64 MiB of HBM per device.

v0:
```python
import math

import jax
import jax.numpy as jnp
from jax import lax
from jax.sharding import PartitionSpec as P

TGX = 8


LOSS_SCALE = 0.05


def passed_along(block, axis, distance):
    devices = range(lax.axis_size(axis))
    route = [(i - distance, i) for i in devices if i - distance in devices]
    return lax.ppermute(block, axis, route)


def fourier_tables(extent):
    indices = jnp.arange(extent, dtype=jnp.int32)
    phases = (indices[:, None] * indices[None, :] % extent).astype(jnp.float32) * (
        2.0 * math.pi / extent
    )
    scaling = 1.0 / math.sqrt(extent)
    return (jnp.cos(phases) * scaling, -jnp.sin(phases) * scaling)


def complex_product(left_op, right_op):
    return (
        left_op[0] * right_op[0] - left_op[1] * right_op[1],
        left_op[0] * right_op[1] + left_op[1] * right_op[0],
    )


def transform(fields, table_real, table_imag):
    highest = lax.Precision.HIGHEST
    left_real = jnp.einsum("jk,bkl->bjl", table_real, fields[0], precision=highest) - jnp.einsum(
        "jk,bkl->bjl", table_imag, fields[1], precision=highest
    )
    left_imag = jnp.einsum("jk,bkl->bjl", table_real, fields[1], precision=highest) + jnp.einsum(
        "jk,bkl->bjl", table_imag, fields[0], precision=highest
    )
    out_real = jnp.einsum("bjk,kl->bjl", left_real, table_real, precision=highest) - jnp.einsum(
        "bjk,kl->bjl", left_imag, table_imag, precision=highest
    )
    out_imag = jnp.einsum("bjk,kl->bjl", left_real, table_imag, precision=highest) + jnp.einsum(
        "bjk,kl->bjl", left_imag, table_real, precision=highest
    )
    return (out_real, out_imag)


def window_loss(windows, probe, prop_real, prop_imag, target):
    positions = windows.shape[0]
    layers = windows.shape[1]
    mode_count = probe.shape[0]
    extent = probe.shape[-1]
    table_real, table_imag = fourier_tables(extent)
    shape_full = (positions, mode_count, extent, extent)
    shape_flat = (positions * mode_count, extent, extent)
    wavefield = (probe[None, :, 0], probe[None, :, 1])
    for slab_index in range(layers):
        if slab_index > 0:
            flattened = (wavefield[0].reshape(shape_flat), wavefield[1].reshape(shape_flat))
            spectrum = complex_product(
                transform(flattened, table_real, table_imag), (prop_real, prop_imag)
            )
            flattened = transform(spectrum, table_real, -table_imag)
            wavefield = (flattened[0].reshape(shape_full), flattened[1].reshape(shape_full))
        slab_now = (windows[:, slab_index, 0][:, None], windows[:, slab_index, 1][:, None])
        wavefield = complex_product(wavefield, slab_now)
    far_field = transform(
        (wavefield[0].reshape(shape_flat), wavefield[1].reshape(shape_flat)), table_real, table_imag
    )
    intensity = jnp.sum(
        (far_field[0] * far_field[0] + far_field[1] * far_field[1]).reshape(shape_full), axis=1
    )
    return LOSS_SCALE * jnp.sum((intensity - target) ** 2)


def local(object_slices, probe, prop_phase, scan_offsets, measured):
    own_tile = object_slices[0]
    layers = own_tile.shape[0]
    tile_side = own_tile.shape[-1]
    extent = probe.shape[-1]
    prop_real = jnp.cos(prop_phase)
    prop_imag = jnp.sin(prop_phase)
    outgoing = (
        (-1, own_tile[:, :, :, :extent]),
        (-TGX, own_tile[:, :, :extent, :]),
        (-TGX - 1, own_tile[:, :, :extent, :extent]),
    )
    arrived = []
    for offset, rim_piece in outgoing:
        arrived.append(passed_along(rim_piece, "tile", offset))
    upper_rows = jnp.concatenate([own_tile, arrived[0]], axis=3)
    lower_rows = jnp.concatenate([arrived[1], arrived[2]], axis=3)
    extended = jnp.concatenate([upper_rows, lower_rows], axis=2)
    offsets = scan_offsets[0]
    target = measured[0]
    slot_count = offsets.shape[0]
    zero_index = jnp.zeros((), jnp.int32)

    def local_loss(ext_field, probe_field):

        def cut_window(row_at, col_at):
            return lax.dynamic_slice(
                ext_field, (zero_index, zero_index, row_at, col_at), (layers, 2, extent, extent)
            )

        windows = jax.vmap(cut_window)(offsets[:, 0], offsets[:, 1])
        return window_loss(windows, probe_field, prop_real, prop_imag, target)

    ext_grad, probe_grad = jax.grad(local_loss, argnums=(0, 1))(extended, probe)
    core_grad = ext_grad[:, :, :tile_side, :tile_side]
    right_part = ext_grad[:, :, :tile_side, tile_side:]
    lower_part = ext_grad[:, :, tile_side:, :tile_side]
    corner_part = ext_grad[:, :, tile_side:, tile_side:]
    for offset, rim_piece in ((1, right_part), (TGX, lower_part), (TGX + 1, corner_part)):
        landed = passed_along(rim_piece, "tile", offset)
        core_grad = core_grad.at[:, :, : landed.shape[2], : landed.shape[3]].add(landed)
    row_share = lax.psum_scatter(core_grad, "batch", scatter_dimension=2, tiled=True)
    probe_total = lax.psum(probe_grad, ("tile", "batch"))
    positions = lax.axis_size("tile") * lax.axis_size("batch") * slot_count
    return (row_share[None], probe_total / positions)


def solution(mesh):
    in_specs = (
        P("tile", None, None, None, None),
        P(),
        P(),
        P("tile", "batch", None),
        P("tile", "batch", None, None),
    )
    out_specs = (P("tile", None, None, "batch", None), P())
    return jax.shard_map(local, mesh=mesh, in_specs=in_specs, out_specs=out_specs, check_vma=False)
```

profile of v0, /device:TPU:0, one launch (start us, length us, event | category | flops | bytes accessed | tf_op | source)
XLA Modules:
  0.0 207.2 jit_solution(9234972377841362507)
XLA Ops:
  8.1 1.2 slice.227
  9.3 1.3 collective-permute-start
  10.6 1.1 slice.228
  12.4 1.7 slice.229
  14.0 1.3 collective-permute-start.2
  20.6 3.3 %and_reduce_fusion = pred[]{:T(512)} fusion(s32[4]{0:T(128)S(1)} %copy-done.7, s32[1]{0:T(128)} %bitcast.8, s32[1]{0:T(128)} %bitcast.7, s32[1]{0:T(128)} %bitcast.6, s32[1]{0:T(128)} %bitcast.5), kind=kLoop, calls=%fused_computation.200 | loop fusion | flops 27 | bytes 33 | tf_op jit(solution)/shard_map/reduce.4
  24.1 1.1 fusion.374
  25.2 0.9 collective-permute-done
  38.4 0.7 fusion.12
  52.2 0.8 fusion
  53.0 1.3 add_bitcast_fusion.1
  55.4 4.6 %scatter-add.14 = f32[2,2,384,384]{3,2,1,0:T(8,128)S(1)} dynamic-update-slice(f32[2,2,384,384]{3,2,1,0:T(8,128)S(1)} %broadcast_in_dim.15, f32[2,2,128,128]{3,2,1,0:T(8,128)S(1)} %select_bitcast_fusion, s32[]{:T(128)} %constant.133.clone.1, s32[]{:T(128)} %constant.133.clone.1, s32[]{:T(128)} %bitcast.46, s32[]{:T(128)} %bitcast.47) | dynamic-update-slice | bytes 524292 | tf_op jit(solution)/shard_map/transpose(jvp(vmap()))/scatter-add | solution.py:107
  60.0 0.8 slice.236
  60.8 5.5 %collective-permute-start.3 = (f32[2,2,256,128]{3,2,1,0:T(8,128)}, f32[2,2,256,128]{3,2,1,0:T(8,128)}, u32[]{:S(2)}, u32[]{:S(2)}) collective-permute-start(f32[2,2,256,128]{3,2,1,0:T(8,128)} %slice.236), channel_id=1, source_target_pairs={{0,4},{4,8},{8,12},{12,16},{16,20},{20,24},{24,28},{1,5},{5,9},{9,... | collective-permute-start | bytes 1572872 | tf_op jit(solution)/shard_map/ppermute | solution.py:17
  66.3 0.9 slice.238
  67.2 1.5 collective-permute-start.4
  68.7 0.7 slice.240
  70.9 6.2 %collective-permute-done.3 = f32[2,2,256,128]{3,2,1,0:T(8,128)} collective-permute-done((f32[2,2,256,128]{3,2,1,0:T(8,128)}, f32[2,2,256,128]{3,2,1,0:T(8,128)}, u32[]{:S(2)}, u32[]{:S(2)}) %collective-permute-start.3) | collective-permute-done | bytes 524320 | tf_op jit(solution)/shard_map/ppermute | solution.py:17
  77.1 1.1 fusion.18
  78.3 1.2 constant_dynamic-update-slice_fusion
  79.6 1.0 copy-done
  80.6 117.4 %all-reduce.8.cloned.1.call-done = f32[2,2,128,128]{2,3,0,1:T(8,128)} async-done(((f32[2,2,128,128]{2,3,0,1:T(8,128)}), f32[2,2,128,128]{2,3,0,1:T(8,128)}) %all-reduce.8.cloned.1.call-update) | async-done | bytes 262160 | tf_op jit(solution)/shard_map/psum | solution.py:123
  197.9 1.0 broadcast_multiply_fusion
  198.9 0.8 copy.146
  (94 shorter events, 30.0 us)
Async XLA Ops:
  8.0 11.8 %copy-start.6 = (s32[1,4]{1,0:T(1,128)S(1)}, s32[1,4]{1,0:T(1,128)}, u32[]{:S(2)}) copy-start(s32[1,4]{1,0:T(1,128)} %constant.136.clone.1) | copy-start | bytes 52
  8.0 12.6 %copy-start.7 = (s32[4]{0:T(128)S(1)}, s32[4]{0:T(128)}, u32[]{:S(2)}) copy-start(s32[4]{0:T(128)} %constant.137.clone.1) | copy-start | bytes 52
  8.0 18.0 %copy-start.1 = (f32[1,2,2,256,256]{4,3,2,1,0:T(8,128)S(1)}, f32[1,2,2,256,256]{4,3,2,1,0:T(8,128)}, u32[]{:S(2)}) copy-start(f32[1,2,2,256,256]{4,3,2,1,0:T(8,128)} %param.13) | copy-start | bytes 3145732
  8.0 7.4 %copy-start.5 = (s32[1,1,2]{2,1,0:T(1,128)S(1)}, s32[1,1,2]{2,1,0:T(1,128)}, u32[]{:S(2)}) copy-start(s32[1,1,2]{2,1,0:T(1,128)} %param.16) | copy-start | bytes 28
  8.0 189.9 %all-reduce.8.cloned.1.call-start = ((), (), s32[]{:S(2)}) async-start(), calls=%async_computation.2 | async-start | bytes 524288 | tf_op jit(solution)/shard_map/psum | solution.py:123
  8.1 12.5 %copy-start.3 = (f32[2,2,128,128]{3,2,1,0:T(8,128)S(1)}, f32[2,2,128,128]{3,2,1,0:T(8,128)}, u32[]{:S(2)}) copy-start(f32[2,2,128,128]{3,2,1,0:T(8,128)} %param.14) | copy-start | bytes 786436
  9.3 16.8 %collective-permute-start = (f32[2,2,256,128]{3,2,1,0:T(8,128)S(1)}, f32[2,2,256,128]{3,2,1,0:T(8,128)S(1)}, u32[]{:S(2)}, u32[]{:S(2)}) collective-permute-start(f32[2,2,256,128]{3,2,1,0:T(8,128)S(1)} %slice.227), channel_id=1, source_target_pairs={{4,0},{8,4},{12,8},{16,12},{20,16},{24,20},{28,24},{5,1},{9,5},{13... | collective-permute-start | bytes 1572872 | tf_op jit(solution)/shard_map/ppermute | solution.py:17
  11.7 14.4 %collective-permute-start.1 = (f32[2,2,128,256]{3,2,1,0:T(8,128)S(1)}, f32[2,2,128,256]{3,2,1,0:T(8,128)S(1)}, u32[]{:S(2)}, u32[]{:S(2)}) collective-permute-start(f32[2,2,128,256]{3,2,1,0:T(8,128)S(1)} %slice.228), channel_id=1, source_target_pairs={} | collective-permute-start | bytes 1572872 | tf_op jit(solution)/shard_map/ppermute | solution.py:17
  14.0 11.1 %collective-permute-start.2 = (f32[2,2,128,128]{3,2,1,0:T(8,128)}, f32[2,2,128,128]{3,2,1,0:T(8,128)}, u32[]{:S(2)}, u32[]{:S(2)}) collective-permute-start(f32[2,2,128,128]{3,2,1,0:T(8,128)} %slice.229), channel_id=1, source_target_pairs={} | collective-permute-start | bytes 786440 | tf_op jit(solution)/shard_map/ppermute | solution.py:17
  34.4 5.8 %copy-start.4 = (f32[1,1,128,128]{3,2,1,0:T(8,128)S(1)}, f32[1,1,128,128]{3,2,1,0:T(8,128)}, u32[]{:S(2)}) copy-start(f32[1,1,128,128]{3,2,1,0:T(8,128)} %param.17) | copy-start | bytes 196612
  60.0 9.5 %copy-start.2 = (f32[2,1,128,128]{2,3,0,1:T(8,128)S(1)}, f32[2,1,128,128]{2,3,0,1:T(8,128)}, u32[]{:S(2)}) copy-start(f32[2,1,128,128]{2,3,0,1:T(8,128)} %get-tuple-element.78) | copy-start | bytes 393220
  60.8 16.3 %collective-permute-start.3 = (f32[2,2,256,128]{3,2,1,0:T(8,128)}, f32[2,2,256,128]{3,2,1,0:T(8,128)}, u32[]{:S(2)}, u32[]{:S(2)}) collective-permute-start(f32[2,2,256,128]{3,2,1,0:T(8,128)} %slice.236), channel_id=1, source_target_pairs={{0,4},{4,8},{8,12},{12,16},{16,20},{20,24},{24,28},{1,5},{5,9},{9,... | collective-permute-start | bytes 1572872 | tf_op jit(solution)/shard_map/ppermute | solution.py:17
  67.2 11.1 %collective-permute-start.4 = (f32[2,2,128,256]{3,2,1,0:T(8,128)}, f32[2,2,128,256]{3,2,1,0:T(8,128)}, u32[]{:S(2)}, u32[]{:S(2)}) collective-permute-start(f32[2,2,128,256]{3,2,1,0:T(8,128)} %slice.238), channel_id=1, source_target_pairs={} | collective-permute-start | bytes 1572872 | tf_op jit(solution)/shard_map/ppermute | solution.py:17
  70.2 129.5 %reduce-scatter.2.cloned.1.call-start = ((), (), s32[]{:S(2)}) async-start(), calls=%async_computation.1 | async-start | bytes 1310720 | tf_op jit(solution)/shard_map/reduce_scatter | solution.py:122
  70.2 9.3 %collective-permute-start.5 = (f32[2,2,128,128]{3,2,1,0:T(8,128)}, f32[2,2,128,128]{3,2,1,0:T(8,128)S(1)}, u32[]{:S(2)}, u32[]{:S(2)}) collective-permute-start(f32[2,2,128,128]{3,2,1,0:T(8,128)} %slice.240), channel_id=1, source_target_pairs={} | collective-permute-start | bytes 786440 | tf_op jit(solution)/shard_map/ppermute | solution.py:17
  79.5 1.0 copy-start
Sparse Core Ops, SparseCore 0:
  70.3 127.5 all-reduce.7
Sparse Core Ops, SparseCore 1:
  80.6 28.2 reduce-scatter.1
where the time goes:
time: 208 us; the launch traced here: 207 us
  waiting for transfers between devices  124 us (60%)
  matrix products  27.2 us (13%)
  between operations  20 us (10%)
  local copies, waits for them, and re-layouts  16.1 us (8%)
  starting transfers between devices  11 us (5%)
  other arithmetic  8.39 us (4%)
    psum x1, waiting for transfers between devices, local(): probe_total = lax.psum(probe_grad, ('tile', 'batch'))  117 us
    ppermute x6, starting transfers between devices, passed_along(): return lax.ppermute(block, axis, route)  10.9 us
    ppermute x6, waiting for transfers between devices, passed_along(): return lax.ppermute(block, axis, route)  7.09 us
    scatter-add x1, local copies, waits for them, and re-layouts, cut_window(): lax.dynamic_slice(ext_field, (zero_index, zero_index, row_at, col_at), (l...  4.59 us
  transfers between devices with their start and end apart: 8, of which 3 were waited for; matrix products, arithmetic and copies ran while one was open for 7% of the time, Pallas kernels for 0%

commit v1 on v0

v1 whole, which is shorter than its diff:
```python
import functools
import math

import jax
import jax.numpy as jnp
import numpy as np
from jax import lax
from jax.experimental import pallas as pl
from jax.experimental.pallas import tpu as pltpu
from jax.sharding import PartitionSpec as P

TGX = 8


LOSS_SCALE = 0.05

F32 = jnp.float32
BF16 = jnp.bfloat16
ROWS = 8


def passed_along(block, axis, distance):
    devices = range(lax.axis_size(axis))
    route = [(i - distance, i) for i in devices if i - distance in devices]
    return lax.ppermute(block, axis, route)


def exchanged(block, axis, bit):
    return lax.ppermute(block, axis, [(i, i ^ bit) for i in range(lax.axis_size(axis))])


def fourier_tables(extent):
    indices = np.arange(extent)
    phases = (indices[:, None] * indices[None, :] % extent) * (2.0 * math.pi / extent)
    tables = np.stack([np.cos(phases), -np.sin(phases)]).astype(np.float32) / np.float32(math.sqrt(extent))
    high = tables.astype(BF16)
    low = (tables - high.astype(np.float32)).astype(BF16)
    return jnp.asarray(np.stack([high, low]))


def split(value):
    high = value.astype(BF16)
    return high, (value - high.astype(F32)).astype(BF16)


def product(left_op, right_op):
    dot = functools.partial(jnp.dot, preferred_element_type=F32)
    return dot(left_op[0], right_op[0]) + (dot(left_op[0], right_op[1]) + dot(left_op[1], right_op[0]))


def block_matrix(cos_part, sin_part):
    return jnp.concatenate(
        [jnp.concatenate([cos_part, sin_part], 1), jnp.concatenate([-sin_part, cos_part], 1)], 0
    )


def transform(fields, on_left, on_right):
    extent = fields[0][0].shape[0]
    stacked = jnp.concatenate(
        [jnp.concatenate([f[part] for f in fields], 1) for part in range(2)], 0
    )
    left = product(on_left, split(stacked))
    stacked = jnp.concatenate(
        [
            jnp.concatenate(
                [left[part * extent : (part + 1) * extent, m * extent : (m + 1) * extent] for part in range(2)], 1
            )
            for m in range(len(fields))
        ],
        0,
    )
    out = product(split(stacked), on_right)
    return [
        tuple(
            out[m * extent : (m + 1) * extent, part * extent : (part + 1) * extent] for part in range(2)
        )
        for m in range(len(fields))
    ]


def times(a, b):
    return (a[0] * b[0] - a[1] * b[1], a[0] * b[1] + a[1] * b[0])


def times_conj(a, b):
    return (a[0] * b[0] + a[1] * b[1], a[1] * b[0] - a[0] * b[1])


def placed(place_ref, first, extent):
    rows = pl.ds(pl.multiple_of(place_ref[first] * ROWS, ROWS), extent + ROWS)
    cols = pl.ds(pl.multiple_of(place_ref[first + 2] * extent, extent), 2 * extent)
    return rows, cols, place_ref[first + 1], place_ref[first + 3]


def wave_kernel(layers, place_ref, *refs):
    pieces, (probe_ref, prop_ref, measured_ref, table_ref, grad_ref, keep_ref, send_ref, frame_ref) = (
        refs[:-8],
        refs[-8:],
    )
    extent = probe_ref.shape[-1]
    mode_count = probe_ref.shape[0]
    tile_side = pieces[0].shape[-1]
    frame_ref[:, :, :tile_side, :tile_side] = pieces[0][...]
    frame_ref[:, :, :tile_side, tile_side:] = pieces[1][...]
    if len(pieces) > 2:
        below = pl.ds(tile_side, extent)
        frame_ref[:, :, below, :tile_side] = pieces[2][...]
        frame_ref[:, :, below, tile_side:] = pieces[3][...]
    rows, cols, row_shift, col_shift = placed(place_ref, 0, extent)

    def window(layer, part):
        wide = frame_ref[layer, part, rows, cols]
        tall = pltpu.roll(wide, lax.rem(2 * extent - col_shift, 2 * extent), 1)[:, :extent]
        return pltpu.roll(tall, lax.rem(extent + ROWS - row_shift, extent + ROWS), 0)[:extent]

    windows = [tuple(window(layer, part) for part in range(2)) for layer in range(layers)]
    probe = [tuple(probe_ref[m, part] for part in range(2)) for m in range(mode_count)]
    prop = (prop_ref[0], prop_ref[1])
    forward = tuple(block_matrix(table_ref[k, 0], table_ref[k, 1]) for k in range(2))
    backward = tuple(block_matrix(table_ref[k, 0], -table_ref[k, 1]) for k in range(2))

    fields = [times(p, windows[0]) for p in probe]
    entering = [probe]
    for layer in range(1, layers):
        fields = transform(fields, backward, forward)
        fields = [times(f, prop) for f in fields]
        fields = transform(fields, forward, backward)
        entering.append(fields)
        fields = [times(f, windows[layer]) for f in fields]
    fields = transform(fields, backward, forward)
    intensity = sum(f[0] * f[0] + f[1] * f[1] for f in fields)
    slope = (4.0 * LOSS_SCALE) * (intensity - measured_ref[...])
    fields = [(slope * f[0], slope * f[1]) for f in fields]
    fields = transform(fields, forward, backward)
    for layer in reversed(range(layers)):
        parts = [times_conj(f, e) for f, e in zip(fields, entering[layer])]
        for part in range(2):
            grad_ref[layer, part] = sum(p[part] for p in parts)
        fields = [times_conj(f, windows[layer]) for f in fields]
        if layer > 0:
            fields = transform(fields, backward, forward)
            fields = [times_conj(f, prop) for f in fields]
            fields = transform(fields, forward, backward)
    core = place_ref[4]
    for m in range(mode_count):
        keep_ref[m] = jnp.where(core == 0, fields[m][0], fields[m][1])
        send_ref[m] = jnp.where(core == 0, fields[m][1], fields[m][0])


VMEM = pl.BlockSpec(memory_space=pltpu.VMEM)
SMEM = pl.BlockSpec(memory_space=pltpu.SMEM)


def wave_gradients(place, pieces, probe, prop, measured, layers):
    extent = probe.shape[-1]
    tile_side = pieces[0].shape[-1]
    rows = tile_side + ROWS + (extent if len(pieces) > 2 else 0)
    return pl.pallas_call(
        functools.partial(wave_kernel, layers),
        out_shape=(
            jax.ShapeDtypeStruct((layers, 2, extent, extent), F32),
            jax.ShapeDtypeStruct((probe.shape[0], extent, extent), F32),
            jax.ShapeDtypeStruct((probe.shape[0], extent, extent), F32),
        ),
        in_specs=[SMEM] + [VMEM] * (len(pieces) + 4),
        out_specs=(VMEM, VMEM, VMEM),
        scratch_shapes=[pltpu.VMEM((layers, 2, rows, tile_side + extent), F32)],
        compiler_params=pltpu.CompilerParams(vmem_limit_bytes=24 << 20),
        name="wave_gradients",
    )(place, *pieces, probe, prop, measured, fourier_tables(extent))


def spread_kernel(count, place_ref, *refs):
    number = len(refs) - 1 - count
    windows, outs, frame_ref = refs[:number], refs[number:-1], refs[-1]
    extent = windows[0].shape[-1]
    frame_ref[...] = jnp.zeros_like(frame_ref)
    for w, window_ref in enumerate(windows):
        rows, cols, row_shift, col_shift = placed(place_ref, 5 * w, extent)
        for layer in range(window_ref.shape[0]):
            for part in range(2):
                block = jnp.concatenate([window_ref[layer, part], jnp.zeros((ROWS, extent), F32)], 0)
                block = pltpu.roll(block, row_shift, 0)
                wide = pltpu.roll(jnp.concatenate([block, jnp.zeros_like(block)], 1), col_shift, 1)
                at = (layer, part, rows, cols)
                frame_ref[at] = wide if w == 0 else wide + frame_ref[at]
    for k, out_ref in enumerate(outs):
        rows = out_ref.shape[2]
        first = pl.multiple_of(place_ref[5 * number + k] * rows, rows)
        out_ref[...] = frame_ref[:, :, pl.ds(first, rows), :]


def spread(place, windows, frame_rows, frame_cols, share_rows, count):
    layers = windows[0].shape[0]
    return pl.pallas_call(
        functools.partial(spread_kernel, count),
        out_shape=[jax.ShapeDtypeStruct((layers, 2, share_rows, frame_cols), F32)] * count,
        in_specs=[SMEM] + [VMEM] * len(windows),
        out_specs=[VMEM] * count,
        scratch_shapes=[pltpu.VMEM((layers, 2, frame_rows + ROWS, frame_cols), F32)],
        compiler_params=pltpu.CompilerParams(vmem_limit_bytes=24 << 20),
        name="spread_windows",
    )(place, *windows)


def local(object_slices, probe, prop_phase, scan_offsets, measured):
    own_tile = object_slices[0]
    layers = own_tile.shape[0]
    tile_side = own_tile.shape[-1]
    extent = probe.shape[-1]
    tiles = lax.axis_size("tile")
    shares = lax.axis_size("batch")
    tall = tiles > TGX
    share = lax.axis_index("batch")
    core = lax.rem(share, 2)
    half = tile_side // 2

    offset = scan_offsets[0, 0]
    place = jnp.stack([offset[0] // ROWS, offset[0] % ROWS, offset[1] // extent, offset[1] % extent, core])
    prop = jnp.stack([jnp.cos(prop_phase), jnp.sin(prop_phase)])
    strip = lax.dynamic_slice(own_tile, (0, 0, core * half, 0), (layers, 2, half, extent))
    strip = passed_along(strip, "tile", -1)
    other = exchanged(strip, "batch", 1)
    upper = jnp.where(core == 0, strip, other)
    lower = jnp.where(core == 0, other, strip)
    pieces = [own_tile, jnp.concatenate([upper, lower], 2)]
    if tall:
        pieces.append(passed_along(own_tile[:, :, :extent, :], "tile", -TGX))
        pieces.append(passed_along(own_tile[:, :, :extent, :extent], "tile", -TGX - 1))

    window_grad, probe_keep, probe_send = wave_gradients(
        place, pieces, probe, prop, measured[0, 0], layers
    )
    frame_cols = tile_side + extent
    if tall or shares != 4:
        frame_rows = tile_side + (extent if tall else 0)
        (frame,) = spread(
            jnp.concatenate([place, jnp.zeros((1,), jnp.int32)]),
            [window_grad], frame_rows, frame_cols, frame_rows, 1,
        )
        core_grad = frame[:, :, :tile_side, :tile_side]
        parts = [(1, frame[:, :, :tile_side, tile_side:])]
        if tall:
            parts.append((TGX, frame[:, :, tile_side:, :tile_side]))
            parts.append((TGX + 1, frame[:, :, tile_side:, tile_side:]))
        for distance, part in parts:
            landed = passed_along(part, "tile", distance)
            core_grad = core_grad.at[:, :, : landed.shape[2], : landed.shape[3]].add(landed)
        object_share = lax.psum_scatter(core_grad, "batch", scatter_dimension=2, tiled=True)
    else:
        place_across = exchanged(place, "batch", 2)
        across = exchanged(window_grad, "batch", 2)
        kept, given = spread(
            jnp.concatenate([place, place_across, jnp.stack([share, share ^ 1])]),
            [window_grad, across], tile_side, frame_cols, tile_side // shares, 2,
        )
        summed = kept + exchanged(given, "batch", 1)
        landed = passed_along(summed[:, :, :, tile_side:], "tile", 1)
        object_share = summed[:, :, :, :tile_side].at[:, :, :, :extent].add(landed)

    total = probe_keep + exchanged(probe_send, "batch", 1)
    for axis, size, first in (("batch", shares, 2), ("tile", tiles, 1)):
        bit = first
        while bit < size:
            total = total + exchanged(total, axis, bit)
            bit *= 2
    total = total / (tiles * shares)
    other = exchanged(total, "batch", 1)
    probe_step = jnp.stack([jnp.where(core == 0, total, other), jnp.where(core == 0, other, total)], 1)
    return (object_share[None], probe_step)


def solution(mesh):
    in_specs = (
        P("tile", None, None, None, None),
        P(),
        P(),
        P("tile", "batch", None),
        P("tile", "batch", None, None),
    )
    out_specs = (P("tile", None, None, "batch", None), P())
    return jax.shard_map(local, mesh=mesh, in_specs=in_specs, out_specs=out_specs, check_vma=False)
```

time: 208 us -> 58.1 us (0.28)
  waiting for transfers between devices: 124 us -> 25.4 us
  matrix products: 27.2 us -> 0 us
  between operations: 20 us -> 6.08 us
  local copies, waits for them, and re-layouts: 16.1 us -> 4.35 us
  other arithmetic: 8.39 us -> 0.29 us
  Pallas kernels: 0 us -> 5.56 us
  starting transfers between devices: 11 us -> 16.1 us
    psum x1 -> x0, waiting for transfers between devices: 117 us -> none  [local(): probe_total = lax.psum(probe_grad, ('tile', 'batch'))]
    dot_general x48 -> x0, matrix products: 27.2 us -> none  [the longest x6 4.02 us: transform(): jnp.einsum('jk,bkl->bjl', table_imag, fields[1], precision=highest)]
    ppermute x0 -> x10, waiting for transfers between devices: none -> 18.9 us  [exchanged(): lax.ppermute(block, axis, [(i, i ^ bit) for i in range(lax.axis_size(axis...]
    ppermute x0 -> x10, starting transfers between devices: none -> 10.7 us  [exchanged(): lax.ppermute(block, axis, [(i, i ^ bit) for i in range(lax.axis_size(axis...]
    slice x9 -> x2, local copies, waits for them, and re-layouts: 7.02 us -> 0.59 us  [the longest x1 0.58 us: local(): offset[1] // extent]
    ppermute x6 -> x2, starting transfers between devices: 10.9 us -> 5.36 us  [passed_along(): return lax.ppermute(block, axis, route)]
    pallas_call x0 -> x2, Pallas kernels: none -> 5.56 us  [the longest x1 4.62 us: wave_gradients(): pl.pallas_call(functools.partial(wave_kernel, layers), out_shape=(jax.Sha...]
    scatter-add x1 -> x0, local copies, waits for them, and re-layouts: 4.59 us -> none  [cut_window(): lax.dynamic_slice(ext_field, (zero_index, zero_index, row_at, col_at), (l...]
  transfers between devices with their start and end apart: 8 -> 12, of which waited for: 3 -> 8; matrix products, arithmetic and copies ran while one was open for 7% -> 3% of each run, Pallas kernels for 0% -> 2%
where the time goes in v1:
time: 58.1 us; the launch traced here: 57.8 us
  waiting for transfers between devices  25.4 us (44%)
  starting transfers between devices  16.1 us (28%)
  between operations  6.08 us (10%)
  Pallas kernels  5.56 us (10%)
  local copies, waits for them, and re-layouts  4.35 us (7%)
    ppermute x10, waiting for transfers between devices, exchanged(): lax.ppermute(block, axis, [(i, i ^ bit) for i in range(lax.axis_size(axis...  18.9 us
    ppermute x10, starting transfers between devices, exchanged(): lax.ppermute(block, axis, [(i, i ^ bit) for i in range(lax.axis_size(axis...  10.7 us
    ppermute x2, waiting for transfers between devices, passed_along(): return lax.ppermute(block, axis, route)  6.46 us
    ppermute x2, starting transfers between devices, passed_along(): return lax.ppermute(block, axis, route)  5.36 us
    pallas_call x1, Pallas kernels, wave_gradients(): pl.pallas_call(functools.partial(wave_kernel, layers), out_shape=(jax.Sha...  4.62 us
    unnamed x15, local copies, waits for them, and re-layouts  2.34 us
  transfers between devices with their start and end apart: 12, of which 8 were waited for; matrix products, arithmetic and copies ran while one was open for 3% of the time, Pallas kernels for 2%

profile of v1, /device:TPU:0, one launch (start us, length us, event | category | flops | bytes accessed | tf_op | source)
XLA Modules:
  0.0 57.8 jit_solution(3050832096599865165)
XLA Ops:
  0.7 1.0 %dynamic-slice_bitcast_fusion = f32[2,2,128,128]{3,2,1,0:T(8,128)S(1)} fusion(f32[1,2,2,256,256]{4,3,2,1,0:T(8,128)} %param.8, s32[]{:T(128)S(6)} %select_n.50), kind=kLoop, calls=%fused_computation.3 | loop fusion | bytes 524292 | tf_op jit(solution)/shard_map/dynamic_slice | solution.py:221
  1.7 1.4 %collective-permute-start.1 = (f32[2,2,128,128]{3,2,1,0:T(8,128)S(1)}, f32[2,2,128,128]{3,2,1,0:T(8,128)S(1)}, u32[]{:S(2)}, u32[]{:S(2)}) collective-permute-start(f32[2,2,128,128]{3,2,1,0:T(8,128)S(1)} %dynamic-slice_bitcast_fusion), channel_id=1, source_target_pairs={{4,0},{8,4},{12,8},{16,12},{20,16},{24,20},{28,24},{5,1},{9,5},{13... | collective-permute-start | bytes 786440 | tf_op jit(solution)/shard_map/ppermute | solution.py:25
  3.1 0.6 %fusion.2 = (s32[1,1,1]{2,1,0:T(1,128)}, s32[1,1,1]{2,1,0:T(1,128)}) fusion(s32[1,1,2]{2,1,0:T(1,128)S(1)} %copy-done.6), kind=kLoop, calls=%fused_computation.15 | loop fusion | bytes 16 | tf_op jit(solution)/shard_map/slice | solution.py:219
  9.0 3.9 %collective-permute-done.1 = f32[2,2,128,128]{3,2,1,0:T(8,128)S(1)} collective-permute-done((f32[2,2,128,128]{3,2,1,0:T(8,128)S(1)}, f32[2,2,128,128]{3,2,1,0:T(8,128)S(1)}, u32[]{:S(2)}, u32[]{:S(2)}) %collective-permute-start.1) | collective-permute-done | bytes 262176 | tf_op jit(solution)/shard_map/ppermute | solution.py:25
  13.2 1.3 %collective-permute-done.2 = f32[2,2,128,128]{3,2,1,0:T(8,128)S(1)} collective-permute-done((f32[2,2,128,128]{3,2,1,0:T(8,128)S(1)}, f32[2,2,128,128]{3,2,1,0:T(8,128)S(1)}, u32[]{:S(2)}, u32[]{:S(2)}) %collective-permute-start.2) | collective-permute-done | bytes 262176 | tf_op jit(solution)/shard_map/ppermute | solution.py:29
  14.6 0.9 %copy-done.1 = f32[2,2,128,128]{3,2,1,0:T(8,128)S(1)} copy-done((f32[2,2,128,128]{3,2,1,0:T(8,128)S(1)}, f32[2,2,128,128]{3,2,1,0:T(8,128)}, u32[]{:S(2)}) %copy-start.1) | copy-done | bytes 262168
  15.5 4.6 %wave_gradients.1 = (f32[2,2,128,128]{3,2,1,0:T(8,128)S(1)}, f32[2,128,128]{2,1,0:T(8,128)S(1)}, f32[2,128,128]{2,1,0:T(8,128)S(1)}) custom-call(s32[5]{0:T(128)S(1)} %stack.47.place_ref, f32[2,2,256,256]{3,2,1,0:T(8,128)S(1)} %bitcast.27, f32[2,2,256,128]{3,2,1,0:T(8,128)S(1)} %pad_maximum_fusion.refs_1_, f32[2,2,128,128]{3,2,1,0:T(8,128)S(1)} %copy-done.1, ...), custom_call_target="tpu_custom_call" | custom-call | tf_op jit(solution)/shard_map/wave_gradients/pallas_call | solution.py:158
  20.1 0.3 collective-permute-start.6
  20.4 1.1 %collective-permute-done.6 = f32[2,128,128]{2,1,0:T(8,128)S(1)} collective-permute-done((f32[2,128,128]{2,1,0:T(8,128)S(1)}, f32[2,128,128]{2,1,0:T(8,128)S(1)}, u32[]{:S(2)}, u32[]{:S(2)}) %collective-permute-start.6) | collective-permute-done | bytes 131104 | tf_op jit(solution)/shard_map/ppermute | solution.py:29
  21.6 1.8 %collective-permute-start.7 = (f32[2,128,128]{2,1,0:T(8,128)S(1)}, f32[2,128,128]{2,1,0:T(8,128)S(1)}, u32[]{:S(2)}, u32[]{:S(2)}) collective-permute-start(f32[2,128,128]{2,1,0:T(8,128)S(1)} %add.42), channel_id=1, source_target_pairs={{0,2},{1,3},{2,0},{3,1},{4,6},{5,7},{6,4},{7,5},{8,10},{9,11},{10,... | collective-permute-start | bytes 393224 | tf_op jit(solution)/shard_map/ppermute | solution.py:29
  23.4 0.3 collective-permute-start.3
  23.7 4.3 %collective-permute-done.7 = f32[2,128,128]{2,1,0:T(8,128)S(1)} collective-permute-done((f32[2,128,128]{2,1,0:T(8,128)S(1)}, f32[2,128,128]{2,1,0:T(8,128)S(1)}, u32[]{:S(2)}, u32[]{:S(2)}) %collective-permute-start.7) | collective-permute-done | bytes 131104 | tf_op jit(solution)/shard_map/ppermute | solution.py:29
  28.0 2.7 %collective-permute-start.8 = (f32[2,128,128]{2,1,0:T(8,128)S(1)}, f32[2,128,128]{2,1,0:T(8,128)S(1)}, u32[]{:S(2)}, u32[]{:S(2)}) collective-permute-start(f32[2,128,128]{2,1,0:T(8,128)S(1)} %add.43), channel_id=1, source_target_pairs={{0,4},{4,0},{8,12},{12,8},{16,20},{20,16},{24,28},{28,24},{1,5},{5... | collective-permute-start | bytes 393224 | tf_op jit(solution)/shard_map/ppermute | solution.py:29
  30.7 2.9 %collective-permute-done.8 = f32[2,128,128]{2,1,0:T(8,128)S(1)} collective-permute-done((f32[2,128,128]{2,1,0:T(8,128)S(1)}, f32[2,128,128]{2,1,0:T(8,128)S(1)}, u32[]{:S(2)}, u32[]{:S(2)}) %collective-permute-start.8) | collective-permute-done | bytes 131104 | tf_op jit(solution)/shard_map/ppermute | solution.py:29
  33.7 1.6 %collective-permute-start.9 = (f32[2,128,128]{2,1,0:T(8,128)S(1)}, f32[2,128,128]{2,1,0:T(8,128)S(1)}, u32[]{:S(2)}, u32[]{:S(2)}) collective-permute-start(f32[2,128,128]{2,1,0:T(8,128)S(1)} %add.44), channel_id=1, source_target_pairs={{0,8},{4,12},{8,0},{12,4},{16,24},{20,28},{24,16},{28,20},{1,9},{5... | collective-permute-start | bytes 393224 | tf_op jit(solution)/shard_map/ppermute | solution.py:29
  35.3 1.5 %collective-permute-start = (s32[5]{0:T(128)S(1)}, s32[5]{0:T(128)S(1)}, u32[]{:S(2)}, u32[]{:S(2)}) collective-permute-start(s32[5]{0:T(128)S(1)} %stack.47.place_ref), channel_id=1, source_target_pairs={{0,2},{1,3},{2,0},{3,1},{4,6},{5,7},{6,4},{7,5},{8,10},{9,11},{10,... | collective-permute-start | bytes 68 | tf_op jit(solution)/shard_map/ppermute | solution.py:29
  36.8 2.0 %collective-permute-done = s32[5]{0:T(128)S(1)} collective-permute-done((s32[5]{0:T(128)S(1)}, s32[5]{0:T(128)S(1)}, u32[]{:S(2)}, u32[]{:S(2)}) %collective-permute-start) | collective-permute-done | bytes 52 | tf_op jit(solution)/shard_map/ppermute | solution.py:29
  38.9 0.9 %spread_windows.1 = (f32[2,2,64,384]{3,2,1,0:T(8,128)S(1)}, f32[2,2,64,384]{3,2,1,0:T(8,128)S(1)}) custom-call(s32[12]{0:T(128)S(1)} %concatenate.9.place_ref, f32[2,2,128,128]{3,2,1,0:T(8,128)S(1)} %get-tuple-element.19.refs_0_, f32[2,2,128,128]{3,2,1,0:T(8,128)S(1)} %collective-permute-done.3.refs_1_), custom_call_target="tpu_custom_call" | custom-call | tf_op jit(solution)/shard_map/spread_windows/pallas_call | solution.py:195
  40.0 2.3 %collective-permute-start.10 = (f32[2,128,128]{2,1,0:T(8,128)S(1)}, f32[2,128,128]{2,1,0:T(8,128)S(1)}, u32[]{:S(2)}, u32[]{:S(2)}) collective-permute-start(f32[2,128,128]{2,1,0:T(8,128)S(1)} %add.45), channel_id=1, source_target_pairs={{0,16},{4,20},{8,24},{12,28},{16,0},{20,4},{24,8},{28,12},{1,17},{... | collective-permute-start | bytes 393224 | tf_op jit(solution)/shard_map/ppermute | solution.py:29
  42.3 7.3 %collective-permute-done.10 = f32[2,128,128]{2,1,0:T(8,128)S(1)} collective-permute-done((f32[2,128,128]{2,1,0:T(8,128)S(1)}, f32[2,128,128]{2,1,0:T(8,128)S(1)}, u32[]{:S(2)}, u32[]{:S(2)}) %collective-permute-start.10) | collective-permute-done | bytes 131104 | tf_op jit(solution)/shard_map/ppermute | solution.py:29
  49.8 3.9 %collective-permute-start.5 = (f32[2,2,64,128]{3,2,1,0:T(8,128)S(1)}, f32[2,2,64,128]{3,2,1,0:T(8,128)S(1)}, u32[]{:S(2)}, u32[]{:S(2)}) collective-permute-start(f32[2,2,64,128]{3,2,1,0:T(8,128)S(1)} %slice.53), channel_id=1, source_target_pairs={{0,4},{4,8},{8,12},{12,16},{16,20},{20,24},{24,28},{1,5},{5,9},{9,... | collective-permute-start | bytes 393224 | tf_op jit(solution)/shard_map/ppermute | solution.py:25
  53.8 0.7 %copy.8 = f32[2,2,128,128]{3,2,1,0:T(8,128)} copy(f32[2,2,128,128]{3,2,0,1:T(8,128)S(1)} %pad_maximum_fusion.1) | data formatting | bytes 524288
  54.5 2.5 %collective-permute-done.5 = f32[2,2,64,128]{3,2,1,0:T(8,128)S(1)} collective-permute-done((f32[2,2,64,128]{3,2,1,0:T(8,128)S(1)}, f32[2,2,64,128]{3,2,1,0:T(8,128)S(1)}, u32[]{:S(2)}, u32[]{:S(2)}) %collective-permute-start.5) | collective-permute-done | bytes 131104 | tf_op jit(solution)/shard_map/ppermute | solution.py:25
  57.1 0.7 %copy-done.4 = f32[1,2,2,64,256]{4,3,2,1,0:T(8,128)} copy-done((f32[1,2,2,64,256]{4,3,2,1,0:T(8,128)}, f32[1,2,2,64,256]{4,3,2,1,0:T(8,128)S(1)}, u32[]{:S(2)}) %copy-start.4) | copy-done | bytes 262168
  (36 shorter events, 1.0 us)
Async XLA Ops:
  0.6 2.5 %copy-start.6 = (s32[1,1,2]{2,1,0:T(1,128)S(1)}, s32[1,1,2]{2,1,0:T(1,128)}, u32[]{:S(2)}) copy-start(s32[1,1,2]{2,1,0:T(1,128)} %param.11) | copy-start | bytes 28
  1.6 11.3 %copy-start.5 = (f32[128,128]{1,0:T(8,128)S(1)}, f32[128,128]{1,0:T(8,128)}, u32[]{:S(2)}) copy-start(f32[128,128]{1,0:T(8,128)} %param.10) | copy-start | bytes 196612
  1.7 11.3 %collective-permute-start.1 = (f32[2,2,128,128]{3,2,1,0:T(8,128)S(1)}, f32[2,2,128,128]{3,2,1,0:T(8,128)S(1)}, u32[]{:S(2)}, u32[]{:S(2)}) collective-permute-start(f32[2,2,128,128]{3,2,1,0:T(8,128)S(1)} %dynamic-slice_bitcast_fusion), channel_id=1, source_target_pairs={{4,0},{8,4},{12,8},{16,12},{20,16},{24,20},{28,24},{5,1},{9,5},{13... | collective-permute-start | bytes 786440 | tf_op jit(solution)/shard_map/ppermute | solution.py:25
  12.9 1.5 %collective-permute-start.2 = (f32[2,2,128,128]{3,2,1,0:T(8,128)S(1)}, f32[2,2,128,128]{3,2,1,0:T(8,128)S(1)}, u32[]{:S(2)}, u32[]{:S(2)}) collective-permute-start(f32[2,2,128,128]{3,2,1,0:T(8,128)S(1)} %collective-permute-done.1), channel_id=1, source_target_pairs={{0,1},{1,0},{2,3},{3,2},{4,5},{5,4},{6,7},{7,6},{8,9},{9,8},{10,11... | collective-permute-start | bytes 786440 | tf_op jit(solution)/shard_map/ppermute | solution.py:29
  13.2 1.4 %copy-start = (f32[1,2,2,256,256]{4,3,2,1,0:T(8,128)S(1)}, f32[1,2,2,256,256]{4,3,2,1,0:T(8,128)}, u32[]{:S(2)}) copy-start(f32[1,2,2,256,256]{4,3,2,1,0:T(8,128)} %param.8) | copy-start | bytes 3145732
  14.5 1.0 %copy-start.1 = (f32[2,2,128,128]{3,2,1,0:T(8,128)S(1)}, f32[2,2,128,128]{3,2,1,0:T(8,128)}, u32[]{:S(2)}) copy-start(f32[2,2,128,128]{3,2,1,0:T(8,128)} %refs_2_.1) | copy-start | bytes 786436
  14.5 1.0 %copy-start.2 = (bf16[2,2,128,128]{3,2,1,0:T(8,128)(2,1)S(1)}, bf16[2,2,128,128]{3,2,1,0:T(8,128)(2,1)}, u32[]{:S(2)}) copy-start(bf16[2,2,128,128]{3,2,1,0:T(8,128)(2,1)} %constant.88.clone.refs_5_) | copy-start | bytes 393220
  14.5 1.0 %copy-start.3 = (f32[1,1,128,128]{3,2,1,0:T(8,128)S(1)}, f32[1,1,128,128]{3,2,1,0:T(8,128)}, u32[]{:S(2)}) copy-start(f32[1,1,128,128]{3,2,1,0:T(8,128)} %param.12) | copy-start | bytes 196612
  20.1 1.4 %collective-permute-start.6 = (f32[2,128,128]{2,1,0:T(8,128)S(1)}, f32[2,128,128]{2,1,0:T(8,128)S(1)}, u32[]{:S(2)}, u32[]{:S(2)}) collective-permute-start(f32[2,128,128]{2,1,0:T(8,128)S(1)} %get-tuple-element.23), channel_id=1, source_target_pairs={{0,1},{1,0},{2,3},{3,2},{4,5},{5,4},{6,7},{7,6},{8,9},{9,8},{10,11... | collective-permute-start | bytes 393224 | tf_op jit(solution)/shard_map/ppermute | solution.py:29
  21.6 6.4 %collective-permute-start.7 = (f32[2,128,128]{2,1,0:T(8,128)S(1)}, f32[2,128,128]{2,1,0:T(8,128)S(1)}, u32[]{:S(2)}, u32[]{:S(2)}) collective-permute-start(f32[2,128,128]{2,1,0:T(8,128)S(1)} %add.42), channel_id=1, source_target_pairs={{0,2},{1,3},{2,0},{3,1},{4,6},{5,7},{6,4},{7,5},{8,10},{9,11},{10,... | collective-permute-start | bytes 393224 | tf_op jit(solution)/shard_map/ppermute | solution.py:29
  23.4 15.5 %collective-permute-start.3 = (f32[2,2,128,128]{3,2,1,0:T(8,128)S(1)}, f32[2,2,128,128]{3,2,1,0:T(8,128)S(1)}, u32[]{:S(2)}, u32[]{:S(2)}) collective-permute-start(f32[2,2,128,128]{3,2,1,0:T(8,128)S(1)} %get-tuple-element.19.refs_0_), channel_id=1, source_target_pairs={{0,2},{1,3},{2,0},{3,1},{4,6},{5,7},{6,4},{7,5},{8,10},{9,11},{10,... | collective-permute-start | bytes 786440 | tf_op jit(solution)/shard_map/ppermute | solution.py:29
  28.0 5.7 %collective-permute-start.8 = (f32[2,128,128]{2,1,0:T(8,128)S(1)}, f32[2,128,128]{2,1,0:T(8,128)S(1)}, u32[]{:S(2)}, u32[]{:S(2)}) collective-permute-start(f32[2,128,128]{2,1,0:T(8,128)S(1)} %add.43), channel_id=1, source_target_pairs={{0,4},{4,0},{8,12},{12,8},{16,20},{20,16},{24,28},{28,24},{1,5},{5... | collective-permute-start | bytes 393224 | tf_op jit(solution)/shard_map/ppermute | solution.py:29
  33.7 6.3 %collective-permute-start.9 = (f32[2,128,128]{2,1,0:T(8,128)S(1)}, f32[2,128,128]{2,1,0:T(8,128)S(1)}, u32[]{:S(2)}, u32[]{:S(2)}) collective-permute-start(f32[2,128,128]{2,1,0:T(8,128)S(1)} %add.44), channel_id=1, source_target_pairs={{0,8},{4,12},{8,0},{12,4},{16,24},{20,28},{24,16},{28,20},{1,9},{5... | collective-permute-start | bytes 393224 | tf_op jit(solution)/shard_map/ppermute | solution.py:29
  35.3 3.5 %collective-permute-start = (s32[5]{0:T(128)S(1)}, s32[5]{0:T(128)S(1)}, u32[]{:S(2)}, u32[]{:S(2)}) collective-permute-start(s32[5]{0:T(128)S(1)} %stack.47.place_ref), channel_id=1, source_target_pairs={{0,2},{1,3},{2,0},{3,1},{4,6},{5,7},{6,4},{7,5},{8,10},{9,11},{10,... | collective-permute-start | bytes 68 | tf_op jit(solution)/shard_map/ppermute | solution.py:29
  39.9 9.8 %collective-permute-start.4 = (f32[2,2,64,384]{3,2,1,0:T(8,128)S(1)}, f32[2,2,64,384]{3,2,1,0:T(8,128)S(1)}, u32[]{:S(2)}, u32[]{:S(2)}) collective-permute-start(f32[2,2,64,384]{3,2,1,0:T(8,128)S(1)} %get-tuple-element.21), channel_id=1, source_target_pairs={{0,1},{1,0},{2,3},{3,2},{4,5},{5,4},{6,7},{7,6},{8,9},{9,8},{10,11... | collective-permute-start | bytes 1179656 | tf_op jit(solution)/shard_map/ppermute | solution.py:29
  40.0 9.5 %collective-permute-start.10 = (f32[2,128,128]{2,1,0:T(8,128)S(1)}, f32[2,128,128]{2,1,0:T(8,128)S(1)}, u32[]{:S(2)}, u32[]{:S(2)}) collective-permute-start(f32[2,128,128]{2,1,0:T(8,128)S(1)} %add.45), channel_id=1, source_target_pairs={{0,16},{4,20},{8,24},{12,28},{16,0},{20,4},{24,8},{28,12},{1,17},{... | collective-permute-start | bytes 393224 | tf_op jit(solution)/shard_map/ppermute | solution.py:29
  49.6 4.2 %collective-permute-start.11 = (f32[2,128,128]{2,1,0:T(8,128)S(1)}, f32[2,128,128]{2,1,0:T(8,128)S(1)}, u32[]{:S(2)}, u32[]{:S(2)}) collective-permute-start(f32[2,128,128]{2,1,0:T(8,128)S(1)} %add_multiply_fusion), channel_id=1, source_target_pairs={{0,1},{1,0},{2,3},{3,2},{4,5},{5,4},{6,7},{7,6},{8,9},{9,8},{10,11... | collective-permute-start | bytes 393224 | tf_op jit(solution)/shard_map/ppermute | solution.py:29
  49.8 7.3 %collective-permute-start.5 = (f32[2,2,64,128]{3,2,1,0:T(8,128)S(1)}, f32[2,2,64,128]{3,2,1,0:T(8,128)S(1)}, u32[]{:S(2)}, u32[]{:S(2)}) collective-permute-start(f32[2,2,64,128]{3,2,1,0:T(8,128)S(1)} %slice.53), channel_id=1, source_target_pairs={{0,4},{4,8},{8,12},{12,16},{16,20},{20,24},{24,28},{1,5},{5,9},{9,... | collective-permute-start | bytes 393224 | tf_op jit(solution)/shard_map/ppermute | solution.py:25
  57.1 0.7 %copy-start.4 = (f32[1,2,2,64,256]{4,3,2,1,0:T(8,128)}, f32[1,2,2,64,256]{4,3,2,1,0:T(8,128)S(1)}, u32[]{:S(2)}) copy-start(f32[1,2,2,64,256]{4,3,2,1,0:T(8,128)S(1)} %fusion.1) | copy-start | bytes 786436

commit v2 on v1

v2 whole, which is shorter than its diff:
```python
import functools
import math

import jax
import jax.numpy as jnp
import numpy as np
from jax import lax
from jax.experimental import pallas as pl
from jax.experimental.pallas import tpu as pltpu
from jax.sharding import PartitionSpec as P

TGX = 8


LOSS_SCALE = 0.05

F32 = jnp.float32
BF16 = jnp.bfloat16
ROWS = 8


def passed_along(block, axis, distance):
    devices = range(lax.axis_size(axis))
    route = [(i - distance, i) for i in devices if i - distance in devices]
    return lax.ppermute(block, axis, route)


def exchanged(block, axis, bit):
    return lax.ppermute(block, axis, [(i, i ^ bit) for i in range(lax.axis_size(axis))])


def after(value, *others):
    return lax.optimization_barrier((value, *others))[0]


def fourier_tables(extent):
    indices = np.arange(extent)
    phases = (indices[:, None] * indices[None, :] % extent) * (2.0 * math.pi / extent)
    tables = np.stack([np.cos(phases), -np.sin(phases)]).astype(np.float32) / np.float32(math.sqrt(extent))
    high = tables.astype(BF16)
    low = (tables - high.astype(np.float32)).astype(BF16)
    return jnp.asarray(np.stack([high, low]))


def split(value):
    high = value.astype(BF16)
    return high, (value - high.astype(F32)).astype(BF16)


def product(left_op, right_op):
    dot = functools.partial(jnp.dot, preferred_element_type=F32)
    return dot(left_op[0], right_op[0]) + (dot(left_op[0], right_op[1]) + dot(left_op[1], right_op[0]))


def block_matrix(cos_part, sin_part):
    return jnp.concatenate(
        [jnp.concatenate([cos_part, sin_part], 1), jnp.concatenate([-sin_part, cos_part], 1)], 0
    )


def transform(fields, on_left, on_right):
    extent = fields[0][0].shape[0]
    stacked = jnp.concatenate(
        [jnp.concatenate([f[part] for f in fields], 1) for part in range(2)], 0
    )
    left = product(on_left, split(stacked))
    stacked = jnp.concatenate(
        [
            jnp.concatenate(
                [left[part * extent : (part + 1) * extent, m * extent : (m + 1) * extent] for part in range(2)], 1
            )
            for m in range(len(fields))
        ],
        0,
    )
    out = product(split(stacked), on_right)
    return [
        tuple(
            out[m * extent : (m + 1) * extent, part * extent : (part + 1) * extent] for part in range(2)
        )
        for m in range(len(fields))
    ]


def times(a, b):
    return (a[0] * b[0] - a[1] * b[1], a[0] * b[1] + a[1] * b[0])


def times_conj(a, b):
    return (a[0] * b[0] + a[1] * b[1], a[1] * b[0] - a[0] * b[1])


def rows_from(row, extent, tile_side):
    span = extent + ROWS
    first = jnp.minimum(row // ROWS * ROWS, tile_side - span)
    return pl.ds(pl.multiple_of(first, ROWS), span), row - first


def cut(wide, row, col, extent):
    rows, cols = wide.shape
    wide = pltpu.roll(wide, lax.rem(cols - col, cols), 1)[:, :extent]
    return pltpu.roll(wide, lax.rem(rows - row, rows), 0)[:extent]


def own_kernel(count, *refs):
    offset_refs = refs[:count]
    tile_ref, phase_ref, probe_in_ref, table_in_ref, own_ref, prop_ref, probe_ref, table_ref = refs[count:]
    extent = phase_ref.shape[-1]
    for p, offset_ref in enumerate(offset_refs):
        rows, shift = rows_from(offset_ref[0], extent, tile_ref.shape[-1])
        for layer in range(tile_ref.shape[0]):
            for part in range(2):
                own_ref[p, layer, part] = cut(tile_ref[layer, part, rows, :], shift, offset_ref[1], extent)
    prop_ref[0] = jnp.cos(phase_ref[...])
    prop_ref[1] = jnp.sin(phase_ref[...])
    probe_ref[...] = probe_in_ref[...]
    table_ref[...] = table_in_ref[...]


def whole_windows(offset_refs, core_ref, own_ref, first, pieces, strip_ref):
    mine_ref, other_ref = pieces[:2]
    layers, _, half, extent = mine_ref.shape
    tile_side = 2 * half
    core = core_ref[0]
    strip_ref[:, :, pl.ds(pl.multiple_of(core * half, half), half), :] = mine_ref[...]
    strip_ref[:, :, pl.ds(pl.multiple_of((1 - core) * half, half), half), :] = other_ref[...]

    def block(layer, part, p):
        row, col = offset_refs[p][0], offset_refs[p][1]
        rows, shift = rows_from(row, extent, tile_side)
        past_row = lax.broadcasted_iota(jnp.int32, (extent, extent), 0) >= tile_side - row
        past_col = lax.broadcasted_iota(jnp.int32, (extent, extent), 1) >= tile_side - col
        col_in = lax.rem(col, extent)
        row_in = lax.rem(row, extent)
        right = cut(strip_ref[layer, part, rows, :], shift, col_in, extent)
        value = jnp.where(past_col, right, own_ref[p, first + layer, part])
        if len(pieces) > 2:
            below = cut(pieces[2][layer, part], row_in, col, extent)
            corner = cut(pieces[3][layer, part], row_in, col_in, extent)
            value = jnp.where(past_row, jnp.where(past_col, corner, below), value)
        return value

    positions = range(len(offset_refs))
    return [[tuple(block(layer, part, p) for part in range(2)) for p in positions] for layer in range(layers)]


def wave_tools(probe_ref, prop_ref, table_ref):
    probe = [tuple(probe_ref[m, part] for part in range(2)) for m in range(probe_ref.shape[0])]
    prop = (prop_ref[0], prop_ref[1])
    forward = tuple(block_matrix(table_ref[k, 0], table_ref[k, 1]) for k in range(2))
    backward = tuple(block_matrix(table_ref[k, 0], -table_ref[k, 1]) for k in range(2))
    return probe, prop, forward, backward


def propagated(fields, prop, forward, backward):
    fields = transform(fields, backward, forward)
    fields = [times(f, prop) for f in fields]
    return transform(fields, forward, backward)


def enter_kernel(count, positions, *refs):
    offset_refs, core_ref = refs[:positions], refs[positions]
    own_ref, probe_ref, prop_ref, table_ref = refs[positions + 1 : positions + 5]
    pieces, (window_ref, wave_ref, strip_ref) = refs[positions + 5 : positions + 5 + count], refs[positions + 5 + count :]
    probe, prop, forward, backward = wave_tools(probe_ref, prop_ref, table_ref)
    (windows,) = whole_windows(offset_refs, core_ref, own_ref, 0, pieces, strip_ref)
    fields = propagated([times(p, w) for w in windows for p in probe], prop, forward, backward)
    for part in range(2):
        for p, window in enumerate(windows):
            window_ref[p, part] = window[part]
        for k, field in enumerate(fields):
            wave_ref[k, part] = field[part]


def wave_kernel(count, positions, *refs):
    offset_refs, core_ref = refs[:positions], refs[positions]
    own_ref, probe_ref, prop_ref, table_ref, window_ref, wave_ref = refs[positions + 1 : positions + 7]
    measured_refs = refs[positions + 7 : 2 * positions + 7]
    pieces = refs[2 * positions + 7 : 2 * positions + 7 + count]
    grad_ref, keep_ref, send_ref, strip_ref = refs[2 * positions + 7 + count :]
    layers = own_ref.shape[1]
    probe, prop, forward, backward = wave_tools(probe_ref, prop_ref, table_ref)
    modes = len(probe)
    windows = [[(window_ref[p, 0], window_ref[p, 1]) for p in range(positions)]]
    windows += whole_windows(offset_refs, core_ref, own_ref, 1, pieces, strip_ref)
    windows = [[w for w in layer for _ in range(modes)] for layer in windows]
    fields = [(wave_ref[k, 0], wave_ref[k, 1]) for k in range(positions * modes)]
    entering = [probe * positions]
    for layer in range(1, layers):
        if layer > 1:
            fields = propagated(fields, prop, forward, backward)
        entering.append(fields)
        fields = [times(f, w) for f, w in zip(fields, windows[layer])]
    fields = transform(fields, backward, forward)
    slopes = []
    for p in range(positions):
        intensity = sum(f[0] * f[0] + f[1] * f[1] for f in fields[p * modes : (p + 1) * modes])
        slopes += [(4.0 * LOSS_SCALE) * (intensity - measured_refs[p][...])] * modes
    fields = [(slope * f[0], slope * f[1]) for slope, f in zip(slopes, fields)]
    fields = transform(fields, forward, backward)
    for layer in reversed(range(layers)):
        parts = [times_conj(f, e) for f, e in zip(fields, entering[layer])]
        for p in range(positions):
            for part in range(2):
                grad_ref[p, layer, part] = sum(c[part] for c in parts[p * modes : (p + 1) * modes])
        fields = [times_conj(f, w) for f, w in zip(fields, windows[layer])]
        if layer > 0:
            fields = transform(fields, backward, forward)
            fields = [times_conj(f, prop) for f in fields]
            fields = transform(fields, forward, backward)
    core = core_ref[0]
    for m in range(modes):
        real, imag = (sum(fields[p * modes + m][part] for p in range(positions)) for part in range(2))
        keep_ref[m] = jnp.where(core == 0, real, imag)
        send_ref[m] = jnp.where(core == 0, imag, real)


VMEM = pl.BlockSpec(memory_space=pltpu.VMEM)
SMEM = pl.BlockSpec(memory_space=pltpu.SMEM)


def kernel_call(kernel, name, scalars, arrays, outs, scratch=(), flops=0):
    sizes = sum(math.prod(a.shape) * a.dtype.itemsize for a in arrays)
    return pl.pallas_call(
        kernel,
        out_shape=[jax.ShapeDtypeStruct(shape, dtype) for shape, dtype in outs],
        in_specs=[SMEM] * len(scalars) + [VMEM] * len(arrays),
        out_specs=[VMEM] * len(outs),
        scratch_shapes=[pltpu.VMEM(shape, F32) for shape in scratch],
        compiler_params=pltpu.CompilerParams(vmem_limit_bytes=24 << 20),
        cost_estimate=pl.CostEstimate(flops=flops, bytes_accessed=sizes, transcendentals=0),
        name=name,
    )(*scalars, *arrays)


def spread_kernel(shares, *refs):
    offset_refs, (share_ref, window_ref, keep_ref, send_ref, frame_ref) = refs[:-5], refs[-5:]
    extent = window_ref.shape[-1]
    frame_ref[...] = jnp.zeros_like(frame_ref)
    for p, offset_ref in enumerate(offset_refs):
        row, col = offset_ref[0], offset_ref[1]
        rows = pl.ds(pl.multiple_of(row // ROWS * ROWS, ROWS), extent + ROWS)
        cols = pl.ds(pl.multiple_of(col // extent * extent, extent), 2 * extent)
        for layer in range(window_ref.shape[1]):
            for part in range(2):
                block = jnp.concatenate([window_ref[p, layer, part], jnp.zeros((ROWS, extent), F32)], 0)
                block = pltpu.roll(block, lax.rem(row, ROWS), 0)
                wide = pltpu.roll(jnp.concatenate([block, jnp.zeros_like(block)], 1), lax.rem(col, extent), 1)
                at = (layer, part, rows, cols)
                frame_ref[at] = wide if p == 0 else wide + frame_ref[at]
    count = keep_ref.shape[2]
    for share, out_ref in ((share_ref[0], keep_ref), (share_ref[0] ^ 1, send_ref)):
        share = share if shares > 1 else 0
        out_ref[...] = frame_ref[:, :, pl.ds(pl.multiple_of(share * count, count), count), :]


def local(object_slices, probe, prop_phase, scan_offsets, measured):
    own_tile = object_slices[0]
    layers = own_tile.shape[0]
    tile_side = own_tile.shape[-1]
    extent = probe.shape[-1]
    tiles = lax.axis_size("tile")
    shares = lax.axis_size("batch")
    tall = tiles > TGX
    share = lax.axis_index("batch").reshape(1)
    core = share & 1
    half = tile_side // 2
    offset = scan_offsets[0, 0]
    table = fourier_tables(extent)

    def halo(first, count):
        strip = lax.dynamic_slice(own_tile, (first, 0, core[0] * half, 0), (count, 2, half, extent))
        strip = passed_along(strip, "tile", -1)
        if first == 0:
            strip = after(strip, own)
        pieces = [strip, exchanged(strip, "batch", 1)]
        if tall:
            rim = own_tile[first : first + count, :, :extent]
            pieces.append(passed_along(rim, "tile", -TGX))
            pieces.append(passed_along(rim[..., :extent], "tile", -TGX - 1))
        return pieces

    field = (extent, extent)
    paired = not tall and shares == 4
    offsets, targets = [offset], [measured[0, 0]]
    if paired:
        offsets.append(exchanged(offset, "batch", 2))
        targets.append(exchanged(measured[0, 0], "batch", 2))
    positions = len(offsets)
    own, prop, probe_in, table_in = kernel_call(
        functools.partial(own_kernel, positions), "own_windows", offsets, [own_tile, prop_phase, probe, table],
        [((positions, layers, 2) + field, F32), ((2,) + field, F32), (probe.shape, F32), (table.shape, BF16)],
    )
    if paired:
        own = after(own, targets[1])
    early = halo(0, 1)
    late = halo(1, layers - 1)
    shared = [own, probe_in, prop, table_in]
    window, wave = kernel_call(
        functools.partial(enter_kernel, len(early), positions), "entering_wave", offsets + [core], shared + early,
        [((positions, 2) + field, F32), ((positions * probe.shape[0], 2) + field, F32)],
        [(1, 2, tile_side, extent)],
    )
    window_grad, probe_keep, probe_send = kernel_call(
        functools.partial(wave_kernel, len(late), positions), "wave_gradients", offsets + [core],
        shared + [window, wave] + targets + late,
        [((positions, layers, 2) + field, F32), (probe.shape[:1] + field, F32), (probe.shape[:1] + field, F32)],
        [(layers - 1, 2, tile_side, extent)],
    )

    got = exchanged(probe_send, "batch", 1)
    cols = tile_side + extent
    rounds = [("batch", 1 << k) for k in range(1, (shares - 1).bit_length())]
    if paired:
        rounds = []
    rounds += [("tile", 1 << k) for k in range((tiles - 1).bit_length())]
    rows = tile_side + (extent if tall else 0)
    share_rows = tile_side // shares if paired else rows
    kept, given = kernel_call(
        functools.partial(spread_kernel, shares if paired else 1), "spread_windows", offsets + [share], [window_grad],
        [((layers, 2, share_rows, cols), F32)] * 2, [(layers, 2, rows + ROWS, cols)],
    )
    if paired:
        total = probe_keep + after(got, given)
        summed = kept + exchanged(given, "batch", 1)
        landed = passed_along(summed[:, :, :, tile_side:], "tile", 1)
        object_share = summed[:, :, :, :tile_side].at[:, :, :, :extent].add(landed)
        beside = [(summed,)]
    else:
        total = probe_keep + got
        core_grad = kept[:, :, :tile_side, :tile_side]
        parts = [(1, kept[:, :, :tile_side, tile_side:])]
        if tall:
            parts.append((TGX, kept[:, :, tile_side:, :tile_side]))
            parts.append((TGX + 1, kept[:, :, tile_side:, tile_side:]))
        for distance, part in parts:
            landed = passed_along(part, "tile", distance)
            core_grad = core_grad.at[:, :, : landed.shape[2], : landed.shape[3]].add(landed)
        object_share = lax.psum_scatter(core_grad, "batch", scatter_dimension=2, tiled=True)
        beside = []
    for k, (axis, bit) in enumerate(rounds):
        got = exchanged(total, axis, bit)
        total = total + (after(got, *beside[k]) if k < len(beside) else got)
    total = total / (tiles * shares)
    other = exchanged(total, "batch", 1)
    even = core[0] == 0
    probe_step = jnp.stack([jnp.where(even, total, other), jnp.where(even, other, total)], 1)
    return (object_share[None], probe_step)


def solution(mesh):
    in_specs = (
        P("tile", None, None, None, None),
        P(),
        P(),
        P("tile", "batch", None),
        P("tile", "batch", None, None),
    )
    out_specs = (P("tile", None, None, "batch", None), P())
    return jax.shard_map(local, mesh=mesh, in_specs=in_specs, out_specs=out_specs, check_vma=False)
```

time: 58.1 us -> 48.8 us (0.84)
  waiting for transfers between devices: 25.4 us -> 15.5 us
  between operations: 6.08 us -> 0.88 us
  starting transfers between devices: 16.1 us -> 20 us
  Pallas kernels: 5.56 us -> 8.92 us
  local copies, waits for them, and re-layouts: 4.35 us -> 3.05 us
    ppermute x2 -> x3, waiting for transfers between devices: 6.46 us -> 0.01 us  [passed_along(): return lax.ppermute(block, axis, route)]
    ppermute x10, waiting for transfers between devices: 18.9 us -> 15.5 us  [exchanged(): lax.ppermute(block, axis, [(i, i ^ bit) for i in range(lax.axis_size(axis...]
    pallas_call x2 -> x4, Pallas kernels: 5.56 us -> 8.92 us  [kernel_call(): pl.pallas_call(kernel, out_shape=[jax.ShapeDtypeStruct(shape, dtype) for...]
    ppermute x10, starting transfers between devices: 10.7 us -> 14.1 us  [exchanged(): lax.ppermute(block, axis, [(i, i ^ bit) for i in range(lax.axis_size(axis...]
    ppermute x2 -> x3, starting transfers between devices: 5.36 us -> 5.99 us  [passed_along(): return lax.ppermute(block, axis, route)]
    slice x1 -> x0, local copies, waits for them, and re-layouts: 0.58 us -> none  [local(): offset[1] // extent]
  transfers between devices with their start and end apart: 12 -> 13, of which waited for: 8 -> 6; matrix products, arithmetic and copies ran while one was open for 3% -> 0% of each run, Pallas kernels for 2% -> 8%
where the time goes in v2:
time: 48.8 us; the launch traced here: 48.6 us
  starting transfers between devices  20 us (41%)
  waiting for transfers between devices  15.5 us (32%)
  Pallas kernels  8.92 us (18%)
  local copies, waits for them, and re-layouts  3.05 us (6%)
  between operations  0.88 us (2%)
    ppermute x10, waiting for transfers between devices, exchanged(): lax.ppermute(block, axis, [(i, i ^ bit) for i in range(lax.axis_size(axis...  15.5 us
    ppermute x10, starting transfers between devices, exchanged(): lax.ppermute(block, axis, [(i, i ^ bit) for i in range(lax.axis_size(axis...  14.1 us
    pallas_call x4, Pallas kernels, kernel_call(): pl.pallas_call(kernel, out_shape=[jax.ShapeDtypeStruct(shape, dtype) for...  8.92 us
    ppermute x3, starting transfers between devices, passed_along(): return lax.ppermute(block, axis, route)  5.99 us
    unnamed x15, local copies, waits for them, and re-layouts  1.97 us
    dynamic_slice x1, local copies, waits for them, and re-layouts, halo(): lax.dynamic_slice(own_tile, (first, 0, core[0] * half, 0), (count, 2, hal...  1.05 us
  transfers between devices with their start and end apart: 13, of which 6 were waited for; matrix products, arithmetic and copies ran while one was open for 0% of the time, Pallas kernels for 8%

profile of v2, /device:TPU:0, one launch (start us, length us, event | category | flops | bytes accessed | tf_op | source)
XLA Modules:
  0.0 48.6 jit_solution(15949394030489270592)
XLA Ops:
  0.7 1.1 %dynamic-slice_bitcast_fusion = (f32[1,2,128,128]{3,2,1,0:T(8,128)S(1)}, f32[1,2,128,128]{3,2,1,0:T(8,128)S(1)}) fusion(f32[1,2,2,256,256]{4,3,2,1,0:T(8,128)} %param.8, s32[]{:T(128)S(6)} %select_n.16), kind=kLoop, calls=%fused_computation.8 | loop fusion | bytes 524292 | tf_op jit(solution)/shard_map/dynamic_slice | solution.py:272
  1.7 1.3 %collective-permute-start.2 = (f32[1,2,128,128]{3,2,1,0:T(8,128)S(1)}, f32[1,2,128,128]{3,2,1,0:T(8,128)S(1)}, u32[]{:S(2)}, u32[]{:S(2)}) collective-permute-start(f32[1,2,128,128]{3,2,1,0:T(8,128)S(1)} %get-tuple-element.47), channel_id=1, source_target_pairs={{4,0},{8,4},{12,8},{16,12},{20,16},{24,20},{28,24},{5,1},{9,5},{13... | collective-permute-start | bytes 393224 | tf_op jit(solution)/shard_map/ppermute | solution.py:25
  3.0 1.3 %collective-permute-start.4 = (f32[1,2,128,128]{3,2,1,0:T(8,128)S(1)}, f32[1,2,128,128]{3,2,1,0:T(8,128)S(1)}, u32[]{:S(2)}, u32[]{:S(2)}) collective-permute-start(f32[1,2,128,128]{3,2,1,0:T(8,128)S(1)} %get-tuple-element.46), channel_id=1, source_target_pairs={{4,0},{8,4},{12,8},{16,12},{20,16},{24,20},{28,24},{5,1},{9,5},{13... | collective-permute-start | bytes 393224 | tf_op jit(solution)/shard_map/ppermute | solution.py:25
  4.4 3.0 %collective-permute-start.1 = (f32[128,128]{1,0:T(8,128)S(1)}, f32[128,128]{1,0:T(8,128)S(1)}, u32[]{:S(2)}, u32[]{:S(2)}) collective-permute-start(f32[128,128]{1,0:T(8,128)S(1)} %bitcast.21), channel_id=1, source_target_pairs={{0,2},{1,3},{2,0},{3,1},{4,6},{5,7},{6,4},{7,5},{8,10},{9,11},{10,... | collective-permute-start | bytes 196616 | tf_op jit(solution)/shard_map/ppermute | solution.py:29
  7.4 0.6 %collective-permute-start = (s32[2]{0:T(128)S(1)}, s32[2]{0:T(128)S(1)}, u32[]{:S(2)}, u32[]{:S(2)}) collective-permute-start(s32[2]{0:T(128)S(1)} %bitcast.23), channel_id=1, source_target_pairs={{0,2},{1,3},{2,0},{3,1},{4,6},{5,7},{6,4},{7,5},{8,10},{9,11},{10,... | collective-permute-start | bytes 32 | tf_op jit(solution)/shard_map/ppermute | solution.py:29
  8.0 3.0 %collective-permute-done.refs_1_ = s32[2]{0:T(128)S(1)} collective-permute-done((s32[2]{0:T(128)S(1)}, s32[2]{0:T(128)S(1)}, u32[]{:S(2)}, u32[]{:S(2)}) %collective-permute-start) | collective-permute-done | bytes 40 | tf_op jit(solution)/shard_map/ppermute | solution.py:29
  11.0 1.2 %copy-done = f32[1,2,2,256,256]{4,3,2,1,0:T(8,128)S(1)} copy-done((f32[1,2,2,256,256]{4,3,2,1,0:T(8,128)S(1)}, f32[1,2,2,256,256]{4,3,2,1,0:T(8,128)}, u32[]{:S(2)}) %copy-start) | copy-done | bytes 1048600
  12.2 1.3 %own_windows.1 = (f32[2,2,2,128,128]{4,3,2,1,0:T(8,128)S(1)}, f32[2,128,128]{2,1,0:T(8,128)S(1)}, f32[2,2,128,128]{3,2,1,0:T(8,128)S(1)}, bf16[2,2,128,128]{3,2,1,0:T(8,128)(2,1)S(1)}) custom-call(s32[2]{0:T(128)S(1)} %bitcast.24, s32[2]{0:T(128)S(1)} %collective-permute-done.refs_1_, f32[2,2,256,256]{3,2,1,0:T(8,128)S(1)} %bitcast.20, ...), custom_call_target="tpu_custom_call" | custom-call | bytes 1507328 | tf_op jit(solution)/shard_map/own_windows/pallas_call | solution.py:224
  13.6 0.5 %collective-permute-start.5 = (f32[1,2,128,128]{3,2,1,0:T(8,128)S(1)}, f32[1,2,128,128]{3,2,1,0:T(8,128)S(1)}, u32[]{:S(2)}, u32[]{:S(2)}) collective-permute-start(f32[1,2,128,128]{3,2,1,0:T(8,128)S(1)} %collective-permute-done.4.refs_11_), channel_id=1, source_target_pairs={{0,1},{1,0},{2,3},{3,2},{4,5},{5,4},{6,7},{7,6},{8,9},{9,8},{10,11... | collective-permute-start | bytes 393224 | tf_op jit(solution)/shard_map/ppermute | solution.py:29
  14.1 0.8 %collective-permute-done.3.refs_8_ = f32[1,2,128,128]{3,2,1,0:T(8,128)S(1)} collective-permute-done((f32[1,2,128,128]{3,2,1,0:T(8,128)S(1)}, f32[1,2,128,128]{3,2,1,0:T(8,128)S(1)}, u32[]{:S(2)}, u32[]{:S(2)}) %collective-permute-start.3) | collective-permute-done | bytes 131104 | tf_op jit(solution)/shard_map/ppermute | solution.py:29
  14.9 2.4 %entering_wave.1 = (f32[2,2,128,128]{3,2,1,0:T(8,128)S(1)}, f32[4,2,128,128]{3,2,1,0:T(8,128)S(1)}) custom-call(s32[2]{0:T(128)S(1)} %bitcast.25, s32[2]{0:T(128)S(1)} %collective-permute-done.refs_1_, s32[1]{0:T(128)S(6)} %and.7.refs_2_, f32[2,2,2,128,128]{4,3,2,1,0:T(8,128)S(1)} %get-tuple-element.30.refs_3_, ...), custom_call_target="tpu_custom_call" | custom-call | bytes 1310720 | tf_op jit(solution)/shard_map/entering_wave/pallas_call | solution.py:224
  17.3 4.3 %wave_gradients.1 = (f32[2,2,2,128,128]{4,3,2,1,0:T(8,128)S(1)}, f32[2,128,128]{2,1,0:T(8,128)S(1)}, f32[2,128,128]{2,1,0:T(8,128)S(1)}) custom-call(s32[2]{0:T(128)S(1)} %bitcast.26, s32[2]{0:T(128)S(1)} %collective-permute-done.refs_1_, s32[1]{0:T(128)S(6)} %and.7.refs_2_, f32[2,2,2,128,128]{4,3,2,1,0:T(8,128)S(1)} %get-tuple-element.30.refs_3_, ...), custom_call_target="tpu_custom_call" | custom-call | bytes 2228224 | tf_op jit(solution)/shard_map/wave_gradients/pallas_call | solution.py:224
  21.6 0.9 %spread_windows.1 = (f32[2,2,64,384]{3,2,1,0:T(8,128)S(1)}, f32[2,2,64,384]{3,2,1,0:T(8,128)S(1)}) custom-call(s32[2]{0:T(128)S(1)} %bitcast.27, s32[2]{0:T(128)S(1)} %collective-permute-done.refs_1_, s32[1]{0:T(128)} %bitcast.1.refs_2_, f32[2,2,2,128,128]{4,3,2,1,0:T(8,128)S(1)} %get-tuple-element.37.refs_3_), custom_call_target="tpu_custom_call" | custom-call | bytes 524288 | tf_op jit(solution)/shard_map/spread_windows/pallas_call | solution.py:224
  22.6 0.2 collective-permute-start.6
  22.8 0.4 collective-permute-start.8
  23.1 1.4 %collective-permute-done.8 = f32[2,128,128]{2,1,0:T(8,128)S(1)} collective-permute-done((f32[2,128,128]{2,1,0:T(8,128)S(1)}, f32[2,128,128]{2,1,0:T(8,128)S(1)}, u32[]{:S(2)}, u32[]{:S(2)}) %collective-permute-start.8) | collective-permute-done | bytes 131104 | tf_op jit(solution)/shard_map/ppermute | solution.py:29
  24.6 3.3 %collective-permute-start.9 = (f32[2,128,128]{2,1,0:T(8,128)S(1)}, f32[2,128,128]{2,1,0:T(8,128)S(1)}, u32[]{:S(2)}, u32[]{:S(2)}) collective-permute-start(f32[2,128,128]{2,1,0:T(8,128)S(1)} %add.29), channel_id=1, source_target_pairs={{0,4},{4,0},{8,12},{12,8},{16,20},{20,16},{24,28},{28,24},{1,5},{5... | collective-permute-start | bytes 393224 | tf_op jit(solution)/shard_map/ppermute | solution.py:29
  27.9 3.8 %collective-permute-done.9 = f32[2,128,128]{2,1,0:T(8,128)S(1)} collective-permute-done((f32[2,128,128]{2,1,0:T(8,128)S(1)}, f32[2,128,128]{2,1,0:T(8,128)S(1)}, u32[]{:S(2)}, u32[]{:S(2)}) %collective-permute-start.9) | collective-permute-done | bytes 131104 | tf_op jit(solution)/shard_map/ppermute | solution.py:29
  31.7 3.3 %collective-permute-start.10 = (f32[2,128,128]{2,1,0:T(8,128)S(1)}, f32[2,128,128]{2,1,0:T(8,128)S(1)}, u32[]{:S(2)}, u32[]{:S(2)}) collective-permute-start(f32[2,128,128]{2,1,0:T(8,128)S(1)} %add.30), channel_id=1, source_target_pairs={{0,8},{4,12},{8,0},{12,4},{16,24},{20,28},{24,16},{28,20},{1,9},{5... | collective-permute-start | bytes 393224 | tf_op jit(solution)/shard_map/ppermute | solution.py:29
  35.0 3.4 %collective-permute-start.7 = (f32[2,2,64,128]{3,2,1,0:T(8,128)S(1)}, f32[2,2,64,128]{3,2,1,0:T(8,128)S(1)}, u32[]{:S(2)}, u32[]{:S(2)}) collective-permute-start(f32[2,2,64,128]{3,2,1,0:T(8,128)S(1)} %slice.41), channel_id=1, source_target_pairs={{0,4},{4,8},{8,12},{12,16},{16,20},{20,24},{24,28},{1,5},{5,9},{9,... | collective-permute-start | bytes 393224 | tf_op jit(solution)/shard_map/ppermute | solution.py:25
  38.4 2.7 %collective-permute-start.11 = (f32[2,128,128]{2,1,0:T(8,128)S(1)}, f32[2,128,128]{2,1,0:T(8,128)S(1)}, u32[]{:S(2)}, u32[]{:S(2)}) collective-permute-start(f32[2,128,128]{2,1,0:T(8,128)S(1)} %add.31), channel_id=1, source_target_pairs={{0,16},{4,20},{8,24},{12,28},{16,0},{20,4},{24,8},{28,12},{1,17},{... | collective-permute-start | bytes 393224 | tf_op jit(solution)/shard_map/ppermute | solution.py:29
  41.1 5.3 %collective-permute-done.11 = f32[2,128,128]{2,1,0:T(8,128)S(1)} collective-permute-done((f32[2,128,128]{2,1,0:T(8,128)S(1)}, f32[2,128,128]{2,1,0:T(8,128)S(1)}, u32[]{:S(2)}, u32[]{:S(2)}) %collective-permute-start.11) | collective-permute-done | bytes 131104 | tf_op jit(solution)/shard_map/ppermute | solution.py:29
  46.5 1.3 %collective-permute-done.12 = f32[2,128,128]{2,1,0:T(8,128)S(1)} collective-permute-done((f32[2,128,128]{2,1,0:T(8,128)S(1)}, f32[2,128,128]{2,1,0:T(8,128)S(1)}, u32[]{:S(2)}, u32[]{:S(2)}) %collective-permute-start.12) | collective-permute-done | bytes 131104 | tf_op jit(solution)/shard_map/ppermute | solution.py:29
  47.9 0.7 %copy.8 = f32[2,2,128,128]{3,2,1,0:T(8,128)} copy(f32[2,2,128,128]{3,2,0,1:T(8,128)S(1)} %pad_maximum_fusion) | data formatting | bytes 524288
  (32 shorter events, 0.4 us)
Async XLA Ops:
  0.6 3.7 %copy-start.4 = (f32[1,1,128,128]{3,2,1,0:T(8,128)S(1)}, f32[1,1,128,128]{3,2,1,0:T(8,128)}, u32[]{:S(2)}) copy-start(f32[1,1,128,128]{3,2,1,0:T(8,128)} %param.12) | copy-start | bytes 196612
  0.6 10.3 %copy-start.1 = (f32[2,2,128,128]{3,2,1,0:T(8,128)S(1)}, f32[2,2,128,128]{3,2,1,0:T(8,128)}, u32[]{:S(2)}) copy-start(f32[2,2,128,128]{3,2,1,0:T(8,128)} %refs_4_.1) | copy-start | bytes 786436
  0.7 10.3 %copy-start.2 = (bf16[2,2,128,128]{3,2,1,0:T(8,128)(2,1)S(1)}, bf16[2,2,128,128]{3,2,1,0:T(8,128)(2,1)}, u32[]{:S(2)}) copy-start(bf16[2,2,128,128]{3,2,1,0:T(8,128)(2,1)} %constant.51.clone.refs_5_) | copy-start | bytes 393220
  0.7 10.3 %copy-start.3 = (f32[128,128]{1,0:T(8,128)S(1)}, f32[128,128]{1,0:T(8,128)}, u32[]{:S(2)}) copy-start(f32[128,128]{1,0:T(8,128)} %refs_3_.1) | copy-start | bytes 196612
  1.7 11.8 %collective-permute-start.2 = (f32[1,2,128,128]{3,2,1,0:T(8,128)S(1)}, f32[1,2,128,128]{3,2,1,0:T(8,128)S(1)}, u32[]{:S(2)}, u32[]{:S(2)}) collective-permute-start(f32[1,2,128,128]{3,2,1,0:T(8,128)S(1)} %get-tuple-element.47), channel_id=1, source_target_pairs={{4,0},{8,4},{12,8},{16,12},{20,16},{24,20},{28,24},{5,1},{9,5},{13... | collective-permute-start | bytes 393224 | tf_op jit(solution)/shard_map/ppermute | solution.py:25
  3.0 10.6 %collective-permute-start.4 = (f32[1,2,128,128]{3,2,1,0:T(8,128)S(1)}, f32[1,2,128,128]{3,2,1,0:T(8,128)S(1)}, u32[]{:S(2)}, u32[]{:S(2)}) collective-permute-start(f32[1,2,128,128]{3,2,1,0:T(8,128)S(1)} %get-tuple-element.46), channel_id=1, source_target_pairs={{4,0},{8,4},{12,8},{16,12},{20,16},{24,20},{28,24},{5,1},{9,5},{13... | collective-permute-start | bytes 393224 | tf_op jit(solution)/shard_map/ppermute | solution.py:25
  4.3 3.0 %copy-start.5 = (s32[1,1,2]{2,1,0:T(1,128)S(1)}, s32[1,1,2]{2,1,0:T(1,128)}, u32[]{:S(2)}) copy-start(s32[1,1,2]{2,1,0:T(1,128)} %param.11) | copy-start | bytes 28
  4.4 9.1 %collective-permute-start.1 = (f32[128,128]{1,0:T(8,128)S(1)}, f32[128,128]{1,0:T(8,128)S(1)}, u32[]{:S(2)}, u32[]{:S(2)}) collective-permute-start(f32[128,128]{1,0:T(8,128)S(1)} %bitcast.21), channel_id=1, source_target_pairs={{0,2},{1,3},{2,0},{3,1},{4,6},{5,7},{6,4},{7,5},{8,10},{9,11},{10,... | collective-permute-start | bytes 196616 | tf_op jit(solution)/shard_map/ppermute | solution.py:29
  7.4 3.5 %collective-permute-start = (s32[2]{0:T(128)S(1)}, s32[2]{0:T(128)S(1)}, u32[]{:S(2)}, u32[]{:S(2)}) collective-permute-start(s32[2]{0:T(128)S(1)} %bitcast.23), channel_id=1, source_target_pairs={{0,2},{1,3},{2,0},{3,1},{4,6},{5,7},{6,4},{7,5},{8,10},{9,11},{10,... | collective-permute-start | bytes 32 | tf_op jit(solution)/shard_map/ppermute | solution.py:29
  10.9 1.2 %copy-start = (f32[1,2,2,256,256]{4,3,2,1,0:T(8,128)S(1)}, f32[1,2,2,256,256]{4,3,2,1,0:T(8,128)}, u32[]{:S(2)}) copy-start(f32[1,2,2,256,256]{4,3,2,1,0:T(8,128)} %param.8) | copy-start | bytes 3145732
  13.5 1.4 %collective-permute-start.3 = (f32[1,2,128,128]{3,2,1,0:T(8,128)S(1)}, f32[1,2,128,128]{3,2,1,0:T(8,128)S(1)}, u32[]{:S(2)}, u32[]{:S(2)}) collective-permute-start(f32[1,2,128,128]{3,2,1,0:T(8,128)S(1)} %collective-permute-done.2.refs_7_), channel_id=1, source_target_pairs={{0,1},{1,0},{2,3},{3,2},{4,5},{5,4},{6,7},{7,6},{8,9},{9,8},{10,11... | collective-permute-start | bytes 393224 | tf_op jit(solution)/shard_map/ppermute | solution.py:29
  13.6 3.7 %collective-permute-start.5 = (f32[1,2,128,128]{3,2,1,0:T(8,128)S(1)}, f32[1,2,128,128]{3,2,1,0:T(8,128)S(1)}, u32[]{:S(2)}, u32[]{:S(2)}) collective-permute-start(f32[1,2,128,128]{3,2,1,0:T(8,128)S(1)} %collective-permute-done.4.refs_11_), channel_id=1, source_target_pairs={{0,1},{1,0},{2,3},{3,2},{4,5},{5,4},{6,7},{7,6},{8,9},{9,8},{10,11... | collective-permute-start | bytes 393224 | tf_op jit(solution)/shard_map/ppermute | solution.py:29
  22.6 5.3 %collective-permute-start.6 = (f32[2,2,64,384]{3,2,1,0:T(8,128)S(1)}, f32[2,2,64,384]{3,2,1,0:T(8,128)S(1)}, u32[]{:S(2)}, u32[]{:S(2)}) collective-permute-start(f32[2,2,64,384]{3,2,1,0:T(8,128)S(1)} %get-tuple-element.39), channel_id=1, source_target_pairs={{0,1},{1,0},{2,3},{3,2},{4,5},{5,4},{6,7},{7,6},{8,9},{9,8},{10,11... | collective-permute-start | bytes 1179656 | tf_op jit(solution)/shard_map/ppermute | solution.py:29
  22.8 1.8 %collective-permute-start.8 = (f32[2,128,128]{2,1,0:T(8,128)S(1)}, f32[2,128,128]{2,1,0:T(8,128)S(1)}, u32[]{:S(2)}, u32[]{:S(2)}) collective-permute-start(f32[2,128,128]{2,1,0:T(8,128)S(1)} %get-tuple-element.41), channel_id=1, source_target_pairs={{0,1},{1,0},{2,3},{3,2},{4,5},{5,4},{6,7},{7,6},{8,9},{9,8},{10,11... | collective-permute-start | bytes 393224 | tf_op jit(solution)/shard_map/ppermute | solution.py:29
  24.6 7.1 %collective-permute-start.9 = (f32[2,128,128]{2,1,0:T(8,128)S(1)}, f32[2,128,128]{2,1,0:T(8,128)S(1)}, u32[]{:S(2)}, u32[]{:S(2)}) collective-permute-start(f32[2,128,128]{2,1,0:T(8,128)S(1)} %add.29), channel_id=1, source_target_pairs={{0,4},{4,0},{8,12},{12,8},{16,20},{20,16},{24,28},{28,24},{1,5},{5... | collective-permute-start | bytes 393224 | tf_op jit(solution)/shard_map/ppermute | solution.py:29
  31.7 6.7 %collective-permute-start.10 = (f32[2,128,128]{2,1,0:T(8,128)S(1)}, f32[2,128,128]{2,1,0:T(8,128)S(1)}, u32[]{:S(2)}, u32[]{:S(2)}) collective-permute-start(f32[2,128,128]{2,1,0:T(8,128)S(1)} %add.30), channel_id=1, source_target_pairs={{0,8},{4,12},{8,0},{12,4},{16,24},{20,28},{24,16},{28,20},{1,9},{5... | collective-permute-start | bytes 393224 | tf_op jit(solution)/shard_map/ppermute | solution.py:29
  35.0 11.5 %collective-permute-start.7 = (f32[2,2,64,128]{3,2,1,0:T(8,128)S(1)}, f32[2,2,64,128]{3,2,1,0:T(8,128)S(1)}, u32[]{:S(2)}, u32[]{:S(2)}) collective-permute-start(f32[2,2,64,128]{3,2,1,0:T(8,128)S(1)} %slice.41), channel_id=1, source_target_pairs={{0,4},{4,8},{8,12},{12,16},{16,20},{20,24},{24,28},{1,5},{5,9},{9,... | collective-permute-start | bytes 393224 | tf_op jit(solution)/shard_map/ppermute | solution.py:25
  38.4 7.9 %collective-permute-start.11 = (f32[2,128,128]{2,1,0:T(8,128)S(1)}, f32[2,128,128]{2,1,0:T(8,128)S(1)}, u32[]{:S(2)}, u32[]{:S(2)}) collective-permute-start(f32[2,128,128]{2,1,0:T(8,128)S(1)} %add.31), channel_id=1, source_target_pairs={{0,16},{4,20},{8,24},{12,28},{16,0},{20,4},{24,8},{28,12},{1,17},{... | collective-permute-start | bytes 393224 | tf_op jit(solution)/shard_map/ppermute | solution.py:29
  46.4 1.4 %collective-permute-start.12 = (f32[2,128,128]{2,1,0:T(8,128)S(1)}, f32[2,128,128]{2,1,0:T(8,128)S(1)}, u32[]{:S(2)}, u32[]{:S(2)}) collective-permute-start(f32[2,128,128]{2,1,0:T(8,128)S(1)} %add_multiply_fusion), channel_id=1, source_target_pairs={{0,1},{1,0},{2,3},{3,2},{4,5},{5,4},{6,7},{7,6},{8,9},{9,8},{10,11... | collective-permute-start | bytes 393224 | tf_op jit(solution)/shard_map/ppermute | solution.py:29
  46.5 1.3 %copy-start.6 = (f32[1,2,2,64,256]{4,3,2,1,0:T(8,128)}, f32[1,2,2,64,256]{4,3,2,1,0:T(8,128)S(1)}, u32[]{:S(2)}) copy-start(f32[1,2,2,64,256]{4,3,2,1,0:T(8,128)S(1)} %fusion.1) | copy-start | bytes 786436

commit v3 on v2

--- a/solution.py
+++ b/solution.py
@@ -102,22 +102,27 @@
     return pltpu.roll(wide, lax.rem(rows - row, rows), 0)[:extent]
 
 
-def own_kernel(count, *refs):
-    offset_refs = refs[:count]
-    tile_ref, phase_ref, probe_in_ref, table_in_ref, own_ref, prop_ref, probe_ref, table_ref = refs[count:]
-    extent = phase_ref.shape[-1]
-    for p, offset_ref in enumerate(offset_refs):
-        rows, shift = rows_from(offset_ref[0], extent, tile_ref.shape[-1])
-        for layer in range(tile_ref.shape[0]):
-            for part in range(2):
-                own_ref[p, layer, part] = cut(tile_ref[layer, part, rows, :], shift, offset_ref[1], extent)
+def own_windows(row, col, tile_ref, own_ref):
+    extent = own_ref.shape[-1]
+    rows, shift = rows_from(row, extent, tile_ref.shape[-1])
+    for layer in range(tile_ref.shape[0]):
+        for part in range(2):
+            own_ref[layer, part] = cut(tile_ref[layer, part, rows, :], shift, col, extent)
+
+
+def own_kernel(offset_ref, tile_ref, phase_ref, probe_in_ref, table_in_ref, own_ref, prop_ref, probe_ref, table_ref):
+    own_windows(offset_ref[0], offset_ref[1], tile_ref, own_ref)
     prop_ref[0] = jnp.cos(phase_ref[...])
     prop_ref[1] = jnp.sin(phase_ref[...])
     probe_ref[...] = probe_in_ref[...]
     table_ref[...] = table_in_ref[...]
 
 
-def whole_windows(offset_refs, core_ref, own_ref, first, pieces, strip_ref):
+def partner_kernel(offset_ref, tile_ref, own_ref):
+    own_windows(offset_ref[0], offset_ref[1], tile_ref, own_ref)
+
+
+def whole_windows(offset_refs, core_ref, own_refs, first, pieces, strip_ref):
     mine_ref, other_ref = pieces[:2]
     layers, _, half, extent = mine_ref.shape
     tile_side = 2 * half
@@ -133,7 +138,7 @@
         col_in = lax.rem(col, extent)
         row_in = lax.rem(row, extent)
         right = cut(strip_ref[layer, part, rows, :], shift, col_in, extent)
-        value = jnp.where(past_col, right, own_ref[p, first + layer, part])
+        value = jnp.where(past_col, right, own_refs[p][first + layer, part])
         if len(pieces) > 2:
             below = cut(pieces[2][layer, part], row_in, col, extent)
             corner = cut(pieces[3][layer, part], row_in, col_in, extent)
@@ -158,12 +163,12 @@
     return transform(fields, forward, backward)
 
 
-def enter_kernel(count, positions, *refs):
+def enter_kernel(positions, *refs):
     offset_refs, core_ref = refs[:positions], refs[positions]
-    own_ref, probe_ref, prop_ref, table_ref = refs[positions + 1 : positions + 5]
-    pieces, (window_ref, wave_ref, strip_ref) = refs[positions + 5 : positions + 5 + count], refs[positions + 5 + count :]
+    own_refs, (probe_ref, prop_ref, table_ref) = refs[positions + 1 : 2 * positions + 1], refs[2 * positions + 1 :][:3]
+    pieces, (window_ref, wave_ref, strip_ref) = refs[2 * positions + 4 : -3], refs[-3:]
     probe, prop, forward, backward = wave_tools(probe_ref, prop_ref, table_ref)
-    (windows,) = whole_windows(offset_refs, core_ref, own_ref, 0, pieces, strip_ref)
+    (windows,) = whole_windows(offset_refs, core_ref, own_refs, 0, pieces, strip_ref)
     fields = propagated([times(p, w) for w in windows for p in probe], prop, forward, backward)
     for part in range(2):
         for p, window in enumerate(windows):
@@ -172,17 +177,17 @@
             wave_ref[k, part] = field[part]
 
 
-def wave_kernel(count, positions, *refs):
+def wave_kernel(positions, *refs):
     offset_refs, core_ref = refs[:positions], refs[positions]
-    own_ref, probe_ref, prop_ref, table_ref, window_ref, wave_ref = refs[positions + 1 : positions + 7]
-    measured_refs = refs[positions + 7 : 2 * positions + 7]
-    pieces = refs[2 * positions + 7 : 2 * positions + 7 + count]
-    grad_ref, keep_ref, send_ref, strip_ref = refs[2 * positions + 7 + count :]
-    layers = own_ref.shape[1]
+    own_refs, refs = refs[positions + 1 : 2 * positions + 1], refs[2 * positions + 1 :]
+    probe_ref, prop_ref, table_ref, window_ref, wave_ref = refs[:5]
+    measured_refs, pieces = refs[5 : 5 + positions], refs[5 + positions : -4]
+    grad_ref, keep_ref, send_ref, strip_ref = refs[-4:]
+    layers = own_refs[0].shape[0]
     probe, prop, forward, backward = wave_tools(probe_ref, prop_ref, table_ref)
     modes = len(probe)
     windows = [[(window_ref[p, 0], window_ref[p, 1]) for p in range(positions)]]
-    windows += whole_windows(offset_refs, core_ref, own_ref, 1, pieces, strip_ref)
+    windows += whole_windows(offset_refs, core_ref, own_refs, 1, pieces, strip_ref)
     windows = [[w for w in layer for _ in range(modes)] for layer in windows]
     fields = [(wave_ref[k, 0], wave_ref[k, 1]) for k in range(positions * modes)]
     entering = [probe * positions]
@@ -225,7 +230,7 @@
         kernel,
         out_shape=[jax.ShapeDtypeStruct(shape, dtype) for shape, dtype in outs],
         in_specs=[SMEM] * len(scalars) + [VMEM] * len(arrays),
-        out_specs=[VMEM] * len(outs),
+        out_specs=[SMEM if dtype == jnp.int32 else VMEM for _, dtype in outs],
         scratch_shapes=[pltpu.VMEM(shape, F32) for shape in scratch],
         compiler_params=pltpu.CompilerParams(vmem_limit_bytes=24 << 20),
         cost_estimate=pl.CostEstimate(flops=flops, bytes_accessed=sizes, transcendentals=0),
@@ -272,7 +277,7 @@
         strip = lax.dynamic_slice(own_tile, (first, 0, core[0] * half, 0), (count, 2, half, extent))
         strip = passed_along(strip, "tile", -1)
         if first == 0:
-            strip = after(strip, own)
+            strip = after(strip, *owns)
         pieces = [strip, exchanged(strip, "batch", 1)]
         if tall:
             rim = own_tile[first : first + count, :, :extent]
@@ -283,26 +288,30 @@
     field = (extent, extent)
     paired = not tall and shares == 4
     offsets, targets = [offset], [measured[0, 0]]
+    own, prop, probe_in, table_in = kernel_call(
+        own_kernel, "own_windows", offsets, [own_tile, prop_phase, probe, table],
+        [((layers, 2) + field, F32), ((2,) + field, F32), (probe.shape, F32), (table.shape, BF16)],
+    )
+    owns = [own]
     if paired:
-        offsets.append(exchanged(offset, "batch", 2))
-        targets.append(exchanged(measured[0, 0], "batch", 2))
+        offsets.append(after(exchanged(offset, "batch", 2), own))
+        (partner_own,) = kernel_call(
+            partner_kernel, "partner_windows", [offsets[1]], [own_tile], [((layers, 2) + field, F32)]
+        )
+        owns.append(partner_own)
     positions = len(offsets)
-    own, prop, probe_in, table_in = kernel_call(
-        functools.partial(own_kernel, positions), "own_windows", offsets, [own_tile, prop_phase, probe, table],
-        [((positions, layers, 2) + field, F32), ((2,) + field, F32), (probe.shape, F32), (table.shape, BF16)],
-    )
-    if paired:
-        own = after(own, targets[1])
     early = halo(0, 1)
     late = halo(1, layers - 1)
-    shared = [own, probe_in, prop, table_in]
+    if paired:
+        targets.append(exchanged(after(measured[0, 0], early[0]), "batch", 2))
+    shared = owns + [probe_in, prop, table_in]
     window, wave = kernel_call(
-        functools.partial(enter_kernel, len(early), positions), "entering_wave", offsets + [core], shared + early,
+        functools.partial(enter_kernel, positions), "entering_wave", offsets + [core], shared + early,
         [((positions, 2) + field, F32), ((positions * probe.shape[0], 2) + field, F32)],
         [(1, 2, tile_side, extent)],
     )
     window_grad, probe_keep, probe_send = kernel_call(
-        functools.partial(wave_kernel, len(late), positions), "wave_gradients", offsets + [core],
+        functools.partial(wave_kernel, positions), "wave_gradients", offsets + [core],
         shared + [window, wave] + targets + late,
         [((positions, layers, 2) + field, F32), (probe.shape[:1] + field, F32), (probe.shape[:1] + field, F32)],
         [(layers - 1, 2, tile_side, extent)],
@@ -314,11 +323,11 @@
     if paired:
         rounds = []
     rounds += [("tile", 1 << k) for k in range((tiles - 1).bit_length())]
-    rows = tile_side + (extent if tall else 0)
-    share_rows = tile_side // shares if paired else rows
+    frame_rows = tile_side + (extent if tall else 0)
+    share_rows = tile_side // shares if paired else frame_rows
     kept, given = kernel_call(
         functools.partial(spread_kernel, shares if paired else 1), "spread_windows", offsets + [share], [window_grad],
-        [((layers, 2, share_rows, cols), F32)] * 2, [(layers, 2, rows + ROWS, cols)],
+        [((layers, 2, share_rows, cols), F32)] * 2, [(layers, 2, frame_rows + ROWS, cols)],
     )
     if paired:
         total = probe_keep + after(got, given)

time: 48.8 us -> 47 us (0.963)
  starting transfers between devices: 20 us -> 18.7 us
  waiting for transfers between devices: 15.5 us -> 14.3 us
  Pallas kernels: 8.92 us -> 9.55 us
    ppermute x10, waiting for transfers between devices: 15.5 us -> 12 us  [exchanged(): lax.ppermute(block, axis, [(i, i ^ bit) for i in range(lax.axis_size(axis...]
    ppermute x3, waiting for transfers between devices: 0.01 us -> 2.25 us  [passed_along(): return lax.ppermute(block, axis, route)]
    ppermute x10, starting transfers between devices: 14.1 us -> 12.8 us  [exchanged(): lax.ppermute(block, axis, [(i, i ^ bit) for i in range(lax.axis_size(axis...]
    pallas_call x4 -> x5, Pallas kernels: 8.92 us -> 9.55 us  [kernel_call(): pl.pallas_call(kernel, out_shape=[jax.ShapeDtypeStruct(shape, dtype) for...]
    unnamed x15 -> x17, local copies, waits for them, and re-layouts: 1.97 us -> 2.02 us
  transfers between devices with their start and end apart: 13 -> 13, of which waited for: 6 -> 7; matrix products, arithmetic and copies ran while one was open for 0% -> 0% of each run, Pallas kernels for 8% -> 9%
where the time goes in v3:
time: 47 us; the launch traced here: 46.7 us
  starting transfers between devices  18.7 us (40%)
  waiting for transfers between devices  14.3 us (30%)
  Pallas kernels  9.55 us (20%)
  local copies, waits for them, and re-layouts  3.09 us (7%)
  between operations  0.86 us (2%)
    ppermute x10, starting transfers between devices, exchanged(): lax.ppermute(block, axis, [(i, i ^ bit) for i in range(lax.axis_size(axis...  12.8 us
    ppermute x10, waiting for transfers between devices, exchanged(): lax.ppermute(block, axis, [(i, i ^ bit) for i in range(lax.axis_size(axis...  12 us
    pallas_call x5, Pallas kernels, kernel_call(): pl.pallas_call(kernel, out_shape=[jax.ShapeDtypeStruct(shape, dtype) for...  9.55 us
    ppermute x3, starting transfers between devices, passed_along(): return lax.ppermute(block, axis, route)  5.99 us
    ppermute x3, waiting for transfers between devices, passed_along(): return lax.ppermute(block, axis, route)  2.25 us
    unnamed x17, local copies, waits for them, and re-layouts  2.02 us
    dynamic_slice x1, local copies, waits for them, and re-layouts, halo(): lax.dynamic_slice(own_tile, (first, 0, core[0] * half, 0), (count, 2, hal...  1.05 us
  transfers between devices with their start and end apart: 13, of which 7 were waited for; matrix products, arithmetic and copies ran while one was open for 0% of the time, Pallas kernels for 9%

profile of v3, /device:TPU:0, one launch (start us, length us, event | category | flops | bytes accessed | tf_op | source)
XLA Modules:
  0.0 46.7 jit_solution(3334400942588436135)
XLA Ops:
  0.7 1.0 %dynamic-slice_bitcast_fusion = (f32[1,2,128,128]{3,2,1,0:T(8,128)S(1)}, f32[1,2,128,128]{3,2,1,0:T(8,128)S(1)}) fusion(f32[1,2,2,256,256]{4,3,2,1,0:T(8,128)} %param.8, s32[]{:T(128)S(6)} %select_n.16), kind=kLoop, calls=%fused_computation.8 | loop fusion | bytes 524292 | tf_op jit(solution)/shard_map/dynamic_slice | solution.py:277
  1.7 1.3 %collective-permute-start.1 = (f32[1,2,128,128]{3,2,1,0:T(8,128)S(1)}, f32[1,2,128,128]{3,2,1,0:T(8,128)S(1)}, u32[]{:S(2)}, u32[]{:S(2)}) collective-permute-start(f32[1,2,128,128]{3,2,1,0:T(8,128)S(1)} %get-tuple-element.49), channel_id=1, source_target_pairs={{4,0},{8,4},{12,8},{16,12},{20,16},{24,20},{28,24},{5,1},{9,5},{13... | collective-permute-start | bytes 393224 | tf_op jit(solution)/shard_map/ppermute | solution.py:25
  3.0 1.3 %collective-permute-start.4 = (f32[1,2,128,128]{3,2,1,0:T(8,128)S(1)}, f32[1,2,128,128]{3,2,1,0:T(8,128)S(1)}, u32[]{:S(2)}, u32[]{:S(2)}) collective-permute-start(f32[1,2,128,128]{3,2,1,0:T(8,128)S(1)} %get-tuple-element.48), channel_id=1, source_target_pairs={{4,0},{8,4},{12,8},{16,12},{20,16},{24,20},{28,24},{5,1},{9,5},{13... | collective-permute-start | bytes 393224 | tf_op jit(solution)/shard_map/ppermute | solution.py:25
  4.3 3.0 %collective-permute-start = (s32[2]{0:T(128)S(1)}, s32[2]{0:T(128)S(1)}, u32[]{:S(2)}, u32[]{:S(2)}) collective-permute-start(s32[2]{0:T(128)S(1)} %bitcast.24), channel_id=1, source_target_pairs={{0,2},{1,3},{2,0},{3,1},{4,6},{5,7},{6,4},{7,5},{8,10},{9,11},{10,... | collective-permute-start | bytes 32 | tf_op jit(solution)/shard_map/ppermute | solution.py:29
  7.4 1.2 %copy-done = f32[1,2,2,256,256]{4,3,2,1,0:T(8,128)S(1)} copy-done((f32[1,2,2,256,256]{4,3,2,1,0:T(8,128)S(1)}, f32[1,2,2,256,256]{4,3,2,1,0:T(8,128)}, u32[]{:S(2)}) %copy-start) | copy-done | bytes 1048600
  8.6 1.2 %own_windows.1 = (f32[2,2,128,128]{3,2,1,0:T(8,128)S(1)}, f32[2,128,128]{2,1,0:T(8,128)S(1)}, f32[2,2,128,128]{3,2,1,0:T(8,128)S(1)}, bf16[2,2,128,128]{3,2,1,0:T(8,128)(2,1)S(1)}) custom-call(s32[2]{0:T(128)S(1)} %bitcast.25, f32[2,2,256,256]{3,2,1,0:T(8,128)S(1)} %bitcast.20, f32[128,128]{1,0:T(8,128)S(1)} %copy-done.4, f32[2,2,128,128]{3,2,1,0:T(8,128)S(1)} %copy-done.2, ...), custom_call_target="tpu_custom_call" | custom-call | bytes 1507328 | tf_op jit(solution)/shard_map/own_windows/pallas_call | solution.py:229
  9.8 0.8 %partner_windows.1.refs_4_ = f32[2,2,128,128]{3,2,1,0:T(8,128)S(1)} custom-call(s32[2]{0:T(128)S(1)} %collective-permute-done.offset_ref.refs_1_, f32[2,2,256,256]{3,2,1,0:T(8,128)S(1)} %bitcast.21), custom_call_target="tpu_custom_call" | custom-call | bytes 1048576 | tf_op jit(solution)/shard_map/partner_windows/pallas_call | solution.py:229
  10.6 0.3 collective-permute-done.1.refs_8_
  10.9 2.0 %collective-permute-done.4.refs_12_ = f32[1,2,128,128]{3,2,1,0:T(8,128)S(1)} collective-permute-done((f32[1,2,128,128]{3,2,1,0:T(8,128)S(1)}, f32[1,2,128,128]{3,2,1,0:T(8,128)S(1)}, u32[]{:S(2)}, u32[]{:S(2)}) %collective-permute-start.4) | collective-permute-done | bytes 131104 | tf_op jit(solution)/shard_map/ppermute | solution.py:25
  12.9 1.8 %collective-permute-start.3 = (f32[128,128]{1,0:T(8,128)S(1)}, f32[128,128]{1,0:T(8,128)S(1)}, u32[]{:S(2)}, u32[]{:S(2)}) collective-permute-start(f32[128,128]{1,0:T(8,128)S(1)} %bitcast.22), channel_id=1, source_target_pairs={{0,2},{1,3},{2,0},{3,1},{4,6},{5,7},{6,4},{7,5},{8,10},{9,11},{10,... | collective-permute-start | bytes 196616 | tf_op jit(solution)/shard_map/ppermute | solution.py:29
  14.6 2.4 %entering_wave.1 = (f32[2,2,128,128]{3,2,1,0:T(8,128)S(1)}, f32[4,2,128,128]{3,2,1,0:T(8,128)S(1)}) custom-call(s32[2]{0:T(128)S(1)} %bitcast.26, s32[2]{0:T(128)S(1)} %collective-permute-done.offset_ref.refs_1_, s32[1]{0:T(128)S(6)} %and.7.refs_2_, f32[2,2,128,128]{3,2,1,0:T(8,128)S(1)} %get-tuple-element.30.refs_3_, ...), custom_call_target="tpu_custom_call" | custom-call | bytes 1310720 | tf_op jit(solution)/shard_map/entering_wave/pallas_call | solution.py:229
  17.1 0.3 collective-permute-done.3.refs_11_
  17.4 4.3 %wave_gradients.1 = (f32[2,2,2,128,128]{4,3,2,1,0:T(8,128)S(1)}, f32[2,128,128]{2,1,0:T(8,128)S(1)}, f32[2,128,128]{2,1,0:T(8,128)S(1)}) custom-call(s32[2]{0:T(128)S(1)} %bitcast.27, s32[2]{0:T(128)S(1)} %collective-permute-done.offset_ref.refs_1_, s32[1]{0:T(128)S(6)} %and.7.refs_2_, f32[2,2,128,128]{3,2,1,0:T(8,128)S(1)} %get-tuple-element.30.refs_3_, ...), custom_call_target="tpu_custom_call" | custom-call | bytes 2228224 | tf_op jit(solution)/shard_map/wave_gradients/pallas_call | solution.py:229
  21.7 0.9 %spread_windows.1 = (f32[2,2,64,384]{3,2,1,0:T(8,128)S(1)}, f32[2,2,64,384]{3,2,1,0:T(8,128)S(1)}) custom-call(s32[2]{0:T(128)S(1)} %bitcast.28, s32[2]{0:T(128)S(1)} %collective-permute-done.offset_ref.refs_1_, s32[1]{0:T(128)} %bitcast.2.refs_2_, f32[2,2,2,128,128]{4,3,2,1,0:T(8,128)S(1)} %get-tuple-element.39.refs_3_), custom_call_target="tpu_custom_call" | custom-call | bytes 524288 | tf_op jit(solution)/shard_map/spread_windows/pallas_call | solution.py:229
  22.7 0.5 %collective-permute-start.8 = (f32[2,128,128]{2,1,0:T(8,128)S(1)}, f32[2,128,128]{2,1,0:T(8,128)S(1)}, u32[]{:S(2)}, u32[]{:S(2)}) collective-permute-start(f32[2,128,128]{2,1,0:T(8,128)S(1)} %get-tuple-element.43), channel_id=1, source_target_pairs={{0,1},{1,0},{2,3},{3,2},{4,5},{5,4},{6,7},{7,6},{8,9},{9,8},{10,11... | collective-permute-start | bytes 393224 | tf_op jit(solution)/shard_map/ppermute | solution.py:29
  23.2 1.4 %collective-permute-done.8 = f32[2,128,128]{2,1,0:T(8,128)S(1)} collective-permute-done((f32[2,128,128]{2,1,0:T(8,128)S(1)}, f32[2,128,128]{2,1,0:T(8,128)S(1)}, u32[]{:S(2)}, u32[]{:S(2)}) %collective-permute-start.8) | collective-permute-done | bytes 131104 | tf_op jit(solution)/shard_map/ppermute | solution.py:29
  24.6 2.7 %collective-permute-start.9 = (f32[2,128,128]{2,1,0:T(8,128)S(1)}, f32[2,128,128]{2,1,0:T(8,128)S(1)}, u32[]{:S(2)}, u32[]{:S(2)}) collective-permute-start(f32[2,128,128]{2,1,0:T(8,128)S(1)} %add.29), channel_id=1, source_target_pairs={{0,4},{4,0},{8,12},{12,8},{16,20},{20,16},{24,28},{28,24},{1,5},{5... | collective-permute-start | bytes 393224 | tf_op jit(solution)/shard_map/ppermute | solution.py:29
  27.3 3.7 %collective-permute-done.9 = f32[2,128,128]{2,1,0:T(8,128)S(1)} collective-permute-done((f32[2,128,128]{2,1,0:T(8,128)S(1)}, f32[2,128,128]{2,1,0:T(8,128)S(1)}, u32[]{:S(2)}, u32[]{:S(2)}) %collective-permute-start.9) | collective-permute-done | bytes 131104 | tf_op jit(solution)/shard_map/ppermute | solution.py:29
  31.1 2.0 %collective-permute-start.10 = (f32[2,128,128]{2,1,0:T(8,128)S(1)}, f32[2,128,128]{2,1,0:T(8,128)S(1)}, u32[]{:S(2)}, u32[]{:S(2)}) collective-permute-start(f32[2,128,128]{2,1,0:T(8,128)S(1)} %add.30), channel_id=1, source_target_pairs={{0,8},{4,12},{8,0},{12,4},{16,24},{20,28},{24,16},{28,20},{1,9},{5... | collective-permute-start | bytes 393224 | tf_op jit(solution)/shard_map/ppermute | solution.py:29
  33.1 3.4 %collective-permute-start.7 = (f32[2,2,64,128]{3,2,1,0:T(8,128)S(1)}, f32[2,2,64,128]{3,2,1,0:T(8,128)S(1)}, u32[]{:S(2)}, u32[]{:S(2)}) collective-permute-start(f32[2,2,64,128]{3,2,1,0:T(8,128)S(1)} %slice.41), channel_id=1, source_target_pairs={{0,4},{4,8},{8,12},{12,16},{16,20},{20,24},{24,28},{1,5},{5,9},{9,... | collective-permute-start | bytes 393224 | tf_op jit(solution)/shard_map/ppermute | solution.py:25
  36.6 2.7 %collective-permute-start.11 = (f32[2,128,128]{2,1,0:T(8,128)S(1)}, f32[2,128,128]{2,1,0:T(8,128)S(1)}, u32[]{:S(2)}, u32[]{:S(2)}) collective-permute-start(f32[2,128,128]{2,1,0:T(8,128)S(1)} %add.31), channel_id=1, source_target_pairs={{0,16},{4,20},{8,24},{12,28},{16,0},{20,4},{24,8},{28,12},{1,17},{... | collective-permute-start | bytes 393224 | tf_op jit(solution)/shard_map/ppermute | solution.py:29
  39.2 5.2 %collective-permute-done.11 = f32[2,128,128]{2,1,0:T(8,128)S(1)} collective-permute-done((f32[2,128,128]{2,1,0:T(8,128)S(1)}, f32[2,128,128]{2,1,0:T(8,128)S(1)}, u32[]{:S(2)}, u32[]{:S(2)}) %collective-permute-start.11) | collective-permute-done | bytes 131104 | tf_op jit(solution)/shard_map/ppermute | solution.py:29
  44.6 1.3 %collective-permute-done.12 = f32[2,128,128]{2,1,0:T(8,128)S(1)} collective-permute-done((f32[2,128,128]{2,1,0:T(8,128)S(1)}, f32[2,128,128]{2,1,0:T(8,128)S(1)}, u32[]{:S(2)}, u32[]{:S(2)}) %collective-permute-start.12) | collective-permute-done | bytes 131104 | tf_op jit(solution)/shard_map/ppermute | solution.py:29
  46.0 0.7 %copy.8 = f32[2,2,128,128]{3,2,1,0:T(8,128)} copy(f32[2,2,128,128]{3,2,0,1:T(8,128)S(1)} %pad_maximum_fusion) | data formatting | bytes 524288
  (35 shorter events, 0.4 us)
Async XLA Ops:
  0.6 6.7 %copy-start.2 = (f32[2,2,128,128]{3,2,1,0:T(8,128)S(1)}, f32[2,2,128,128]{3,2,1,0:T(8,128)}, u32[]{:S(2)}) copy-start(f32[2,2,128,128]{3,2,1,0:T(8,128)} %probe_in_ref.1) | copy-start | bytes 786436
  0.6 6.7 %copy-start.3 = (bf16[2,2,128,128]{3,2,1,0:T(8,128)(2,1)S(1)}, bf16[2,2,128,128]{3,2,1,0:T(8,128)(2,1)}, u32[]{:S(2)}) copy-start(bf16[2,2,128,128]{3,2,1,0:T(8,128)(2,1)} %constant.51.clone.table_in_ref) | copy-start | bytes 393220
  0.7 6.7 %copy-start.4 = (f32[128,128]{1,0:T(8,128)S(1)}, f32[128,128]{1,0:T(8,128)}, u32[]{:S(2)}) copy-start(f32[128,128]{1,0:T(8,128)} %phase_ref.1) | copy-start | bytes 196612
  1.7 9.2 %collective-permute-start.1 = (f32[1,2,128,128]{3,2,1,0:T(8,128)S(1)}, f32[1,2,128,128]{3,2,1,0:T(8,128)S(1)}, u32[]{:S(2)}, u32[]{:S(2)}) collective-permute-start(f32[1,2,128,128]{3,2,1,0:T(8,128)S(1)} %get-tuple-element.49), channel_id=1, source_target_pairs={{4,0},{8,4},{12,8},{16,12},{20,16},{24,20},{28,24},{5,1},{9,5},{13... | collective-permute-start | bytes 393224 | tf_op jit(solution)/shard_map/ppermute | solution.py:25
  3.0 1.3 %copy-start.6 = (s32[1,1,2]{2,1,0:T(1,128)S(1)}, s32[1,1,2]{2,1,0:T(1,128)}, u32[]{:S(2)}) copy-start(s32[1,1,2]{2,1,0:T(1,128)} %param.11) | copy-start | bytes 28
  3.0 9.8 %collective-permute-start.4 = (f32[1,2,128,128]{3,2,1,0:T(8,128)S(1)}, f32[1,2,128,128]{3,2,1,0:T(8,128)S(1)}, u32[]{:S(2)}, u32[]{:S(2)}) collective-permute-start(f32[1,2,128,128]{3,2,1,0:T(8,128)S(1)} %get-tuple-element.48), channel_id=1, source_target_pairs={{4,0},{8,4},{12,8},{16,12},{20,16},{24,20},{28,24},{5,1},{9,5},{13... | collective-permute-start | bytes 393224 | tf_op jit(solution)/shard_map/ppermute | solution.py:25
  4.3 5.4 %collective-permute-start = (s32[2]{0:T(128)S(1)}, s32[2]{0:T(128)S(1)}, u32[]{:S(2)}, u32[]{:S(2)}) collective-permute-start(s32[2]{0:T(128)S(1)} %bitcast.24), channel_id=1, source_target_pairs={{0,2},{1,3},{2,0},{3,1},{4,6},{5,7},{6,4},{7,5},{8,10},{9,11},{10,... | collective-permute-start | bytes 32 | tf_op jit(solution)/shard_map/ppermute | solution.py:29
  7.4 1.2 %copy-start = (f32[1,2,2,256,256]{4,3,2,1,0:T(8,128)S(1)}, f32[1,2,2,256,256]{4,3,2,1,0:T(8,128)}, u32[]{:S(2)}) copy-start(f32[1,2,2,256,256]{4,3,2,1,0:T(8,128)} %param.8) | copy-start | bytes 3145732
  8.6 1.2 %copy-start.1 = (f32[1,2,2,256,256]{4,3,2,1,0:T(8,128)S(1)}, f32[1,2,2,256,256]{4,3,2,1,0:T(8,128)}, u32[]{:S(2)}) copy-start(f32[1,2,2,256,256]{4,3,2,1,0:T(8,128)} %param.8) | copy-start | bytes 3145732
  9.8 3.0 %copy-start.5 = (f32[1,1,128,128]{3,2,1,0:T(8,128)S(1)}, f32[1,1,128,128]{3,2,1,0:T(8,128)}, u32[]{:S(2)}) copy-start(f32[1,1,128,128]{3,2,1,0:T(8,128)} %param.12) | copy-start | bytes 196612
  10.9 3.8 %collective-permute-start.2 = (f32[1,2,128,128]{3,2,1,0:T(8,128)S(1)}, f32[1,2,128,128]{3,2,1,0:T(8,128)S(1)}, u32[]{:S(2)}, u32[]{:S(2)}) collective-permute-start(f32[1,2,128,128]{3,2,1,0:T(8,128)S(1)} %collective-permute-done.1.refs_8_), channel_id=1, source_target_pairs={{0,1},{1,0},{2,3},{3,2},{4,5},{5,4},{6,7},{7,6},{8,9},{9,8},{10,11... | collective-permute-start | bytes 393224 | tf_op jit(solution)/shard_map/ppermute | solution.py:29
  12.9 4.5 %collective-permute-start.5 = (f32[1,2,128,128]{3,2,1,0:T(8,128)S(1)}, f32[1,2,128,128]{3,2,1,0:T(8,128)S(1)}, u32[]{:S(2)}, u32[]{:S(2)}) collective-permute-start(f32[1,2,128,128]{3,2,1,0:T(8,128)S(1)} %collective-permute-done.4.refs_12_), channel_id=1, source_target_pairs={{0,1},{1,0},{2,3},{3,2},{4,5},{5,4},{6,7},{7,6},{8,9},{9,8},{10,11... | collective-permute-start | bytes 393224 | tf_op jit(solution)/shard_map/ppermute | solution.py:29
  12.9 4.5 %collective-permute-start.3 = (f32[128,128]{1,0:T(8,128)S(1)}, f32[128,128]{1,0:T(8,128)S(1)}, u32[]{:S(2)}, u32[]{:S(2)}) collective-permute-start(f32[128,128]{1,0:T(8,128)S(1)} %bitcast.22), channel_id=1, source_target_pairs={{0,2},{1,3},{2,0},{3,1},{4,6},{5,7},{6,4},{7,5},{8,10},{9,11},{10,... | collective-permute-start | bytes 196616 | tf_op jit(solution)/shard_map/ppermute | solution.py:29
  22.6 4.7 %collective-permute-start.6 = (f32[2,2,64,384]{3,2,1,0:T(8,128)S(1)}, f32[2,2,64,384]{3,2,1,0:T(8,128)S(1)}, u32[]{:S(2)}, u32[]{:S(2)}) collective-permute-start(f32[2,2,64,384]{3,2,1,0:T(8,128)S(1)} %get-tuple-element.41), channel_id=1, source_target_pairs={{0,1},{1,0},{2,3},{3,2},{4,5},{5,4},{6,7},{7,6},{8,9},{9,8},{10,11... | collective-permute-start | bytes 1179656 | tf_op jit(solution)/shard_map/ppermute | solution.py:29
  22.7 1.9 %collective-permute-start.8 = (f32[2,128,128]{2,1,0:T(8,128)S(1)}, f32[2,128,128]{2,1,0:T(8,128)S(1)}, u32[]{:S(2)}, u32[]{:S(2)}) collective-permute-start(f32[2,128,128]{2,1,0:T(8,128)S(1)} %get-tuple-element.43), channel_id=1, source_target_pairs={{0,1},{1,0},{2,3},{3,2},{4,5},{5,4},{6,7},{7,6},{8,9},{9,8},{10,11... | collective-permute-start | bytes 393224 | tf_op jit(solution)/shard_map/ppermute | solution.py:29
  24.6 6.5 %collective-permute-start.9 = (f32[2,128,128]{2,1,0:T(8,128)S(1)}, f32[2,128,128]{2,1,0:T(8,128)S(1)}, u32[]{:S(2)}, u32[]{:S(2)}) collective-permute-start(f32[2,128,128]{2,1,0:T(8,128)S(1)} %add.29), channel_id=1, source_target_pairs={{0,4},{4,0},{8,12},{12,8},{16,20},{20,16},{24,28},{28,24},{1,5},{5... | collective-permute-start | bytes 393224 | tf_op jit(solution)/shard_map/ppermute | solution.py:29
  31.1 5.4 %collective-permute-start.10 = (f32[2,128,128]{2,1,0:T(8,128)S(1)}, f32[2,128,128]{2,1,0:T(8,128)S(1)}, u32[]{:S(2)}, u32[]{:S(2)}) collective-permute-start(f32[2,128,128]{2,1,0:T(8,128)S(1)} %add.30), channel_id=1, source_target_pairs={{0,8},{4,12},{8,0},{12,4},{16,24},{20,28},{24,16},{28,20},{1,9},{5... | collective-permute-start | bytes 393224 | tf_op jit(solution)/shard_map/ppermute | solution.py:29
  33.1 11.5 %collective-permute-start.7 = (f32[2,2,64,128]{3,2,1,0:T(8,128)S(1)}, f32[2,2,64,128]{3,2,1,0:T(8,128)S(1)}, u32[]{:S(2)}, u32[]{:S(2)}) collective-permute-start(f32[2,2,64,128]{3,2,1,0:T(8,128)S(1)} %slice.41), channel_id=1, source_target_pairs={{0,4},{4,8},{8,12},{12,16},{16,20},{20,24},{24,28},{1,5},{5,9},{9,... | collective-permute-start | bytes 393224 | tf_op jit(solution)/shard_map/ppermute | solution.py:25
  36.6 7.9 %collective-permute-start.11 = (f32[2,128,128]{2,1,0:T(8,128)S(1)}, f32[2,128,128]{2,1,0:T(8,128)S(1)}, u32[]{:S(2)}, u32[]{:S(2)}) collective-permute-start(f32[2,128,128]{2,1,0:T(8,128)S(1)} %add.31), channel_id=1, source_target_pairs={{0,16},{4,20},{8,24},{12,28},{16,0},{20,4},{24,8},{28,12},{1,17},{... | collective-permute-start | bytes 393224 | tf_op jit(solution)/shard_map/ppermute | solution.py:29
  44.5 1.4 %collective-permute-start.12 = (f32[2,128,128]{2,1,0:T(8,128)S(1)}, f32[2,128,128]{2,1,0:T(8,128)S(1)}, u32[]{:S(2)}, u32[]{:S(2)}) collective-permute-start(f32[2,128,128]{2,1,0:T(8,128)S(1)} %add_multiply_fusion), channel_id=1, source_target_pairs={{0,1},{1,0},{2,3},{3,2},{4,5},{5,4},{6,7},{7,6},{8,9},{9,8},{10,11... | collective-permute-start | bytes 393224 | tf_op jit(solution)/shard_map/ppermute | solution.py:29
  44.6 1.3 %copy-start.7 = (f32[1,2,2,64,256]{4,3,2,1,0:T(8,128)}, f32[1,2,2,64,256]{4,3,2,1,0:T(8,128)S(1)}, u32[]{:S(2)}) copy-start(f32[1,2,2,64,256]{4,3,2,1,0:T(8,128)S(1)} %fusion.1) | copy-start | bytes 786436

commit v4 on v3

--- a/solution.py
+++ b/solution.py
@@ -122,7 +122,7 @@
     own_windows(offset_ref[0], offset_ref[1], tile_ref, own_ref)
 
 
-def whole_windows(offset_refs, core_ref, own_refs, first, pieces, strip_ref):
+def whole_windows(offset_refs, core_ref, own_refs, pieces, strip_ref):
     mine_ref, other_ref = pieces[:2]
     layers, _, half, extent = mine_ref.shape
     tile_side = 2 * half
@@ -138,7 +138,7 @@
         col_in = lax.rem(col, extent)
         row_in = lax.rem(row, extent)
         right = cut(strip_ref[layer, part, rows, :], shift, col_in, extent)
-        value = jnp.where(past_col, right, own_refs[p][first + layer, part])
+        value = jnp.where(past_col, right, own_refs[p][layer, part])
         if len(pieces) > 2:
             below = cut(pieces[2][layer, part], row_in, col, extent)
             corner = cut(pieces[3][layer, part], row_in, col_in, extent)
@@ -163,36 +163,21 @@
     return transform(fields, forward, backward)
 
 
-def enter_kernel(positions, *refs):
-    offset_refs, core_ref = refs[:positions], refs[positions]
-    own_refs, (probe_ref, prop_ref, table_ref) = refs[positions + 1 : 2 * positions + 1], refs[2 * positions + 1 :][:3]
-    pieces, (window_ref, wave_ref, strip_ref) = refs[2 * positions + 4 : -3], refs[-3:]
-    probe, prop, forward, backward = wave_tools(probe_ref, prop_ref, table_ref)
-    (windows,) = whole_windows(offset_refs, core_ref, own_refs, 0, pieces, strip_ref)
-    fields = propagated([times(p, w) for w in windows for p in probe], prop, forward, backward)
-    for part in range(2):
-        for p, window in enumerate(windows):
-            window_ref[p, part] = window[part]
-        for k, field in enumerate(fields):
-            wave_ref[k, part] = field[part]
-
-
 def wave_kernel(positions, *refs):
     offset_refs, core_ref = refs[:positions], refs[positions]
     own_refs, refs = refs[positions + 1 : 2 * positions + 1], refs[2 * positions + 1 :]
-    probe_ref, prop_ref, table_ref, window_ref, wave_ref = refs[:5]
-    measured_refs, pieces = refs[5 : 5 + positions], refs[5 + positions : -4]
+    probe_ref, prop_ref, table_ref = refs[:3]
+    measured_refs, pieces = refs[3 : 3 + positions], refs[3 + positions : -4]
     grad_ref, keep_ref, send_ref, strip_ref = refs[-4:]
     layers = own_refs[0].shape[0]
     probe, prop, forward, backward = wave_tools(probe_ref, prop_ref, table_ref)
     modes = len(probe)
-    windows = [[(window_ref[p, 0], window_ref[p, 1]) for p in range(positions)]]
-    windows += whole_windows(offset_refs, core_ref, own_refs, 1, pieces, strip_ref)
+    windows = whole_windows(offset_refs, core_ref, own_refs, pieces, strip_ref)
     windows = [[w for w in layer for _ in range(modes)] for layer in windows]
-    fields = [(wave_ref[k, 0], wave_ref[k, 1]) for k in range(positions * modes)]
-    entering = [probe * positions]
-    for layer in range(1, layers):
-        if layer > 1:
+    fields = probe * positions
+    entering = []
+    for layer in range(layers):
+        if layer > 0:
             fields = propagated(fields, prop, forward, backward)
         entering.append(fields)
         fields = [times(f, w) for f, w in zip(fields, windows[layer])]
@@ -273,18 +258,6 @@
     offset = scan_offsets[0, 0]
     table = fourier_tables(extent)
 
-    def halo(first, count):
-        strip = lax.dynamic_slice(own_tile, (first, 0, core[0] * half, 0), (count, 2, half, extent))
-        strip = passed_along(strip, "tile", -1)
-        if first == 0:
-            strip = after(strip, *owns)
-        pieces = [strip, exchanged(strip, "batch", 1)]
-        if tall:
-            rim = own_tile[first : first + count, :, :extent]
-            pieces.append(passed_along(rim, "tile", -TGX))
-            pieces.append(passed_along(rim[..., :extent], "tile", -TGX - 1))
-        return pieces
-
     field = (extent, extent)
     paired = not tall and shares == 4
     offsets, targets = [offset], [measured[0, 0]]
@@ -299,22 +272,20 @@
             partner_kernel, "partner_windows", [offsets[1]], [own_tile], [((layers, 2) + field, F32)]
         )
         owns.append(partner_own)
+        targets.append(exchanged(measured[0, 0], "batch", 2))
     positions = len(offsets)
-    early = halo(0, 1)
-    late = halo(1, layers - 1)
-    if paired:
-        targets.append(exchanged(after(measured[0, 0], early[0]), "batch", 2))
-    shared = owns + [probe_in, prop, table_in]
-    window, wave = kernel_call(
-        functools.partial(enter_kernel, positions), "entering_wave", offsets + [core], shared + early,
-        [((positions, 2) + field, F32), ((positions * probe.shape[0], 2) + field, F32)],
-        [(1, 2, tile_side, extent)],
-    )
+    strip = lax.dynamic_slice(own_tile, (0, 0, core[0] * half, 0), (layers, 2, half, extent))
+    strip = after(passed_along(strip, "tile", -1), *owns, *targets)
+    pieces = [strip, exchanged(strip, "batch", 1)]
+    if tall:
+        rim = own_tile[:, :, :extent]
+        pieces.append(passed_along(rim, "tile", -TGX))
+        pieces.append(passed_along(rim[..., :extent], "tile", -TGX - 1))
     window_grad, probe_keep, probe_send = kernel_call(
         functools.partial(wave_kernel, positions), "wave_gradients", offsets + [core],
-        shared + [window, wave] + targets + late,
+        owns + [probe_in, prop, table_in] + targets + pieces,
         [((positions, layers, 2) + field, F32), (probe.shape[:1] + field, F32), (probe.shape[:1] + field, F32)],
-        [(layers - 1, 2, tile_side, extent)],
+        [(layers, 2, tile_side, extent)],
     )
 
     got = exchanged(probe_send, "batch", 1)

time: 47 us -> 45.7 us (0.972)
  starting transfers between devices: 18.7 us -> 16 us
  waiting for transfers between devices: 14.3 us -> 16.5 us
  Pallas kernels: 9.55 us -> 8.97 us
    ppermute x10 -> x9, waiting for transfers between devices: 12 us -> 14 us  [exchanged(): lax.ppermute(block, axis, [(i, i ^ bit) for i in range(lax.axis_size(axis...]
    ppermute x10 -> x9, starting transfers between devices: 12.8 us -> 11 us  [exchanged(): lax.ppermute(block, axis, [(i, i ^ bit) for i in range(lax.axis_size(axis...]
    ppermute x3 -> x2, starting transfers between devices: 5.99 us -> 4.94 us  [passed_along(): return lax.ppermute(block, axis, route)]
    pallas_call x5 -> x4, Pallas kernels: 9.55 us -> 8.97 us  [kernel_call(): pl.pallas_call(kernel, out_shape=[jax.ShapeDtypeStruct(shape, dtype) for...]
    ppermute x3 -> x2, waiting for transfers between devices: 2.25 us -> 2.46 us  [passed_along(): return lax.ppermute(block, axis, route)]
  transfers between devices with their start and end apart: 13 -> 11, of which waited for: 7 -> 7; matrix products, arithmetic and copies ran while one was open for 0% -> 0% of each run, Pallas kernels for 9% -> 4%
where the time goes in v4:
time: 45.7 us; the launch traced here: 45.5 us
  waiting for transfers between devices  16.5 us (36%)
  starting transfers between devices  16 us (35%)
  Pallas kernels  8.97 us (20%)
  local copies, waits for them, and re-layouts  3.04 us (7%)
  between operations  0.84 us (2%)
    ppermute x9, waiting for transfers between devices, exchanged(): lax.ppermute(block, axis, [(i, i ^ bit) for i in range(lax.axis_size(axis...  14 us
    ppermute x9, starting transfers between devices, exchanged(): lax.ppermute(block, axis, [(i, i ^ bit) for i in range(lax.axis_size(axis...  11 us
    pallas_call x4, Pallas kernels, kernel_call(): pl.pallas_call(kernel, out_shape=[jax.ShapeDtypeStruct(shape, dtype) for...  8.97 us
    ppermute x2, starting transfers between devices, passed_along(): return lax.ppermute(block, axis, route)  4.94 us
    ppermute x2, waiting for transfers between devices, passed_along(): return lax.ppermute(block, axis, route)  2.46 us
    unnamed x17, local copies, waits for them, and re-layouts  1.98 us
    dynamic_slice x1, local copies, waits for them, and re-layouts, local(): lax.dynamic_slice(own_tile, (0, 0, core[0] * half, 0), (layers, 2, half,...  1.04 us
  transfers between devices with their start and end apart: 11, of which 7 were waited for; matrix products, arithmetic and copies ran while one was open for 0% of the time, Pallas kernels for 4%

profile of v4, /device:TPU:0, one launch (start us, length us, event | category | flops | bytes accessed | tf_op | source)
XLA Modules:
  0.0 45.5 jit_solution(5730967265493723584)
XLA Ops:
  0.7 1.0 %dynamic-slice_bitcast_fusion = f32[2,2,128,128]{3,2,1,0:T(8,128)S(1)} fusion(f32[1,2,2,256,256]{4,3,2,1,0:T(8,128)} %param.8, s32[]{:T(128)S(6)} %select_n.15), kind=kLoop, calls=%fused_computation.2 | loop fusion | bytes 524292 | tf_op jit(solution)/shard_map/dynamic_slice | solution.py:277
  1.7 1.3 %collective-permute-start.2 = (f32[2,2,128,128]{3,2,1,0:T(8,128)S(1)}, f32[2,2,128,128]{3,2,1,0:T(8,128)S(1)}, u32[]{:S(2)}, u32[]{:S(2)}) collective-permute-start(f32[2,2,128,128]{3,2,1,0:T(8,128)S(1)} %dynamic-slice_bitcast_fusion), channel_id=1, source_target_pairs={{4,0},{8,4},{12,8},{16,12},{20,16},{24,20},{28,24},{5,1},{9,5},{13... | collective-permute-start | bytes 786440 | tf_op jit(solution)/shard_map/ppermute | solution.py:25
  3.0 3.0 %collective-permute-start.1 = (f32[128,128]{1,0:T(8,128)S(1)}, f32[128,128]{1,0:T(8,128)S(1)}, u32[]{:S(2)}, u32[]{:S(2)}) collective-permute-start(f32[128,128]{1,0:T(8,128)S(1)} %bitcast.20), channel_id=1, source_target_pairs={{0,2},{1,3},{2,0},{3,1},{4,6},{5,7},{6,4},{7,5},{8,10},{9,11},{10,... | collective-permute-start | bytes 196616 | tf_op jit(solution)/shard_map/ppermute | solution.py:29
  6.1 0.6 %collective-permute-start = (s32[2]{0:T(128)S(1)}, s32[2]{0:T(128)S(1)}, u32[]{:S(2)}, u32[]{:S(2)}) collective-permute-start(s32[2]{0:T(128)S(1)} %bitcast.22), channel_id=1, source_target_pairs={{0,2},{1,3},{2,0},{3,1},{4,6},{5,7},{6,4},{7,5},{8,10},{9,11},{10,... | collective-permute-start | bytes 32 | tf_op jit(solution)/shard_map/ppermute | solution.py:29
  6.7 1.2 %copy-done = f32[1,2,2,256,256]{4,3,2,1,0:T(8,128)S(1)} copy-done((f32[1,2,2,256,256]{4,3,2,1,0:T(8,128)S(1)}, f32[1,2,2,256,256]{4,3,2,1,0:T(8,128)}, u32[]{:S(2)}) %copy-start) | copy-done | bytes 1048600
  7.9 1.2 %own_windows.1 = (f32[2,2,128,128]{3,2,1,0:T(8,128)S(1)}, f32[2,128,128]{2,1,0:T(8,128)S(1)}, f32[2,2,128,128]{3,2,1,0:T(8,128)S(1)}, bf16[2,2,128,128]{3,2,1,0:T(8,128)(2,1)S(1)}) custom-call(s32[2]{0:T(128)S(1)} %bitcast.23, f32[2,2,256,256]{3,2,1,0:T(8,128)S(1)} %bitcast.18, f32[128,128]{1,0:T(8,128)S(1)} %copy-done.4, f32[2,2,128,128]{3,2,1,0:T(8,128)S(1)} %copy-done.2, ...), custom_call_target="tpu_custom_call" | custom-call | bytes 1507328 | tf_op jit(solution)/shard_map/own_windows/pallas_call | solution.py:214
  9.1 0.6 %collective-permute-done.offset_ref.refs_1_ = s32[2]{0:T(128)S(1)} collective-permute-done((s32[2]{0:T(128)S(1)}, s32[2]{0:T(128)S(1)}, u32[]{:S(2)}, u32[]{:S(2)}) %collective-permute-start) | collective-permute-done | bytes 40 | tf_op jit(solution)/shard_map/ppermute | solution.py:29
  9.6 0.8 %partner_windows.1.refs_4_ = f32[2,2,128,128]{3,2,1,0:T(8,128)S(1)} custom-call(s32[2]{0:T(128)S(1)} %collective-permute-done.offset_ref.refs_1_, f32[2,2,256,256]{3,2,1,0:T(8,128)S(1)} %bitcast.19), custom_call_target="tpu_custom_call" | custom-call | bytes 1048576 | tf_op jit(solution)/shard_map/partner_windows/pallas_call | solution.py:214
  10.4 2.5 %collective-permute-done.2.refs_10_ = f32[2,2,128,128]{3,2,1,0:T(8,128)S(1)} collective-permute-done((f32[2,2,128,128]{3,2,1,0:T(8,128)S(1)}, f32[2,2,128,128]{3,2,1,0:T(8,128)S(1)}, u32[]{:S(2)}, u32[]{:S(2)}) %collective-permute-start.2) | collective-permute-done | bytes 262176 | tf_op jit(solution)/shard_map/ppermute | solution.py:25
  12.9 1.5 %collective-permute-done.3.refs_11_ = f32[2,2,128,128]{3,2,1,0:T(8,128)S(1)} collective-permute-done((f32[2,2,128,128]{3,2,1,0:T(8,128)S(1)}, f32[2,2,128,128]{3,2,1,0:T(8,128)S(1)}, u32[]{:S(2)}, u32[]{:S(2)}) %collective-permute-start.3) | collective-permute-done | bytes 262176 | tf_op jit(solution)/shard_map/ppermute | solution.py:29
  14.4 6.1 %wave_gradients.1 = (f32[2,2,2,128,128]{4,3,2,1,0:T(8,128)S(1)}, f32[2,128,128]{2,1,0:T(8,128)S(1)}, f32[2,128,128]{2,1,0:T(8,128)S(1)}) custom-call(s32[2]{0:T(128)S(1)} %bitcast.24, s32[2]{0:T(128)S(1)} %collective-permute-done.offset_ref.refs_1_, s32[1]{0:T(128)S(6)} %and.7.refs_2_, f32[2,2,128,128]{3,2,1,0:T(8,128)S(1)} %get-tuple-element.27.refs_3_, ...), custom_call_target="tpu_custom_call" | custom-call | bytes 1703936 | tf_op jit(solution)/shard_map/wave_gradients/pallas_call | solution.py:214
  20.5 0.9 %spread_windows.1 = (f32[2,2,64,384]{3,2,1,0:T(8,128)S(1)}, f32[2,2,64,384]{3,2,1,0:T(8,128)S(1)}) custom-call(s32[2]{0:T(128)S(1)} %bitcast.25, s32[2]{0:T(128)S(1)} %collective-permute-done.offset_ref.refs_1_, s32[1]{0:T(128)} %bitcast.2.refs_2_, f32[2,2,2,128,128]{4,3,2,1,0:T(8,128)S(1)} %get-tuple-element.33.refs_3_), custom_call_target="tpu_custom_call" | custom-call | bytes 524288 | tf_op jit(solution)/shard_map/spread_windows/pallas_call | solution.py:214
  21.5 0.2 collective-permute-start.4
  21.6 0.4 collective-permute-start.6
  22.0 1.4 %collective-permute-done.6 = f32[2,128,128]{2,1,0:T(8,128)S(1)} collective-permute-done((f32[2,128,128]{2,1,0:T(8,128)S(1)}, f32[2,128,128]{2,1,0:T(8,128)S(1)}, u32[]{:S(2)}, u32[]{:S(2)}) %collective-permute-start.6) | collective-permute-done | bytes 131104 | tf_op jit(solution)/shard_map/ppermute | solution.py:29
  23.4 2.7 %collective-permute-start.7 = (f32[2,128,128]{2,1,0:T(8,128)S(1)}, f32[2,128,128]{2,1,0:T(8,128)S(1)}, u32[]{:S(2)}, u32[]{:S(2)}) collective-permute-start(f32[2,128,128]{2,1,0:T(8,128)S(1)} %add.28), channel_id=1, source_target_pairs={{0,4},{4,0},{8,12},{12,8},{16,20},{20,16},{24,28},{28,24},{1,5},{5... | collective-permute-start | bytes 393224 | tf_op jit(solution)/shard_map/ppermute | solution.py:29
  26.2 3.8 %collective-permute-done.7 = f32[2,128,128]{2,1,0:T(8,128)S(1)} collective-permute-done((f32[2,128,128]{2,1,0:T(8,128)S(1)}, f32[2,128,128]{2,1,0:T(8,128)S(1)}, u32[]{:S(2)}, u32[]{:S(2)}) %collective-permute-start.7) | collective-permute-done | bytes 131104 | tf_op jit(solution)/shard_map/ppermute | solution.py:29
  30.0 1.6 %collective-permute-start.8 = (f32[2,128,128]{2,1,0:T(8,128)S(1)}, f32[2,128,128]{2,1,0:T(8,128)S(1)}, u32[]{:S(2)}, u32[]{:S(2)}) collective-permute-start(f32[2,128,128]{2,1,0:T(8,128)S(1)} %add.29), channel_id=1, source_target_pairs={{0,8},{4,12},{8,0},{12,4},{16,24},{20,28},{24,16},{28,20},{1,9},{5... | collective-permute-start | bytes 393224 | tf_op jit(solution)/shard_map/ppermute | solution.py:29
  31.6 3.7 %collective-permute-start.5 = (f32[2,2,64,128]{3,2,1,0:T(8,128)S(1)}, f32[2,2,64,128]{3,2,1,0:T(8,128)S(1)}, u32[]{:S(2)}, u32[]{:S(2)}) collective-permute-start(f32[2,2,64,128]{3,2,1,0:T(8,128)S(1)} %slice.41), channel_id=1, source_target_pairs={{0,4},{4,8},{8,12},{12,16},{16,20},{20,24},{24,28},{1,5},{5,9},{9,... | collective-permute-start | bytes 393224 | tf_op jit(solution)/shard_map/ppermute | solution.py:25
  35.3 2.4 %collective-permute-start.9 = (f32[2,128,128]{2,1,0:T(8,128)S(1)}, f32[2,128,128]{2,1,0:T(8,128)S(1)}, u32[]{:S(2)}, u32[]{:S(2)}) collective-permute-start(f32[2,128,128]{2,1,0:T(8,128)S(1)} %add.30), channel_id=1, source_target_pairs={{0,16},{4,20},{8,24},{12,28},{16,0},{20,4},{24,8},{28,12},{1,17},{... | collective-permute-start | bytes 393224 | tf_op jit(solution)/shard_map/ppermute | solution.py:29
  37.8 5.5 %collective-permute-done.9 = f32[2,128,128]{2,1,0:T(8,128)S(1)} collective-permute-done((f32[2,128,128]{2,1,0:T(8,128)S(1)}, f32[2,128,128]{2,1,0:T(8,128)S(1)}, u32[]{:S(2)}, u32[]{:S(2)}) %collective-permute-start.9) | collective-permute-done | bytes 131104 | tf_op jit(solution)/shard_map/ppermute | solution.py:29
  43.3 0.1 collective-permute-start.10
  43.4 1.3 %collective-permute-done.10 = f32[2,128,128]{2,1,0:T(8,128)S(1)} collective-permute-done((f32[2,128,128]{2,1,0:T(8,128)S(1)}, f32[2,128,128]{2,1,0:T(8,128)S(1)}, u32[]{:S(2)}, u32[]{:S(2)}) %collective-permute-start.10) | collective-permute-done | bytes 131104 | tf_op jit(solution)/shard_map/ppermute | solution.py:29
  44.7 0.7 %copy.8 = f32[2,2,128,128]{3,2,1,0:T(8,128)} copy(f32[2,2,128,128]{3,2,0,1:T(8,128)S(1)} %pad_maximum_fusion) | data formatting | bytes 524288
  (30 shorter events, 0.2 us)
Async XLA Ops:
  0.6 2.4 %copy-start.5 = (f32[1,1,128,128]{3,2,1,0:T(8,128)S(1)}, f32[1,1,128,128]{3,2,1,0:T(8,128)}, u32[]{:S(2)}) copy-start(f32[1,1,128,128]{3,2,1,0:T(8,128)} %param.12) | copy-start | bytes 196612
  0.6 6.0 %copy-start.2 = (f32[2,2,128,128]{3,2,1,0:T(8,128)S(1)}, f32[2,2,128,128]{3,2,1,0:T(8,128)}, u32[]{:S(2)}) copy-start(f32[2,2,128,128]{3,2,1,0:T(8,128)} %probe_in_ref.1) | copy-start | bytes 786436
  0.7 6.0 %copy-start.3 = (bf16[2,2,128,128]{3,2,1,0:T(8,128)(2,1)S(1)}, bf16[2,2,128,128]{3,2,1,0:T(8,128)(2,1)}, u32[]{:S(2)}) copy-start(bf16[2,2,128,128]{3,2,1,0:T(8,128)(2,1)} %constant.48.clone.table_in_ref) | copy-start | bytes 393220
  0.7 6.0 %copy-start.4 = (f32[128,128]{1,0:T(8,128)S(1)}, f32[128,128]{1,0:T(8,128)}, u32[]{:S(2)}) copy-start(f32[128,128]{1,0:T(8,128)} %phase_ref.1) | copy-start | bytes 196612
  1.7 11.1 %collective-permute-start.2 = (f32[2,2,128,128]{3,2,1,0:T(8,128)S(1)}, f32[2,2,128,128]{3,2,1,0:T(8,128)S(1)}, u32[]{:S(2)}, u32[]{:S(2)}) collective-permute-start(f32[2,2,128,128]{3,2,1,0:T(8,128)S(1)} %dynamic-slice_bitcast_fusion), channel_id=1, source_target_pairs={{4,0},{8,4},{12,8},{16,12},{20,16},{24,20},{28,24},{5,1},{9,5},{13... | collective-permute-start | bytes 786440 | tf_op jit(solution)/shard_map/ppermute | solution.py:25
  3.0 3.0 %copy-start.6 = (s32[1,1,2]{2,1,0:T(1,128)S(1)}, s32[1,1,2]{2,1,0:T(1,128)}, u32[]{:S(2)}) copy-start(s32[1,1,2]{2,1,0:T(1,128)} %param.11) | copy-start | bytes 28
  3.0 7.4 %collective-permute-start.1 = (f32[128,128]{1,0:T(8,128)S(1)}, f32[128,128]{1,0:T(8,128)S(1)}, u32[]{:S(2)}, u32[]{:S(2)}) collective-permute-start(f32[128,128]{1,0:T(8,128)S(1)} %bitcast.20), channel_id=1, source_target_pairs={{0,2},{1,3},{2,0},{3,1},{4,6},{5,7},{6,4},{7,5},{8,10},{9,11},{10,... | collective-permute-start | bytes 196616 | tf_op jit(solution)/shard_map/ppermute | solution.py:29
  6.1 3.5 %collective-permute-start = (s32[2]{0:T(128)S(1)}, s32[2]{0:T(128)S(1)}, u32[]{:S(2)}, u32[]{:S(2)}) collective-permute-start(s32[2]{0:T(128)S(1)} %bitcast.22), channel_id=1, source_target_pairs={{0,2},{1,3},{2,0},{3,1},{4,6},{5,7},{6,4},{7,5},{8,10},{9,11},{10,... | collective-permute-start | bytes 32 | tf_op jit(solution)/shard_map/ppermute | solution.py:29
  6.7 1.2 %copy-start = (f32[1,2,2,256,256]{4,3,2,1,0:T(8,128)S(1)}, f32[1,2,2,256,256]{4,3,2,1,0:T(8,128)}, u32[]{:S(2)}) copy-start(f32[1,2,2,256,256]{4,3,2,1,0:T(8,128)} %param.8) | copy-start | bytes 3145732
  7.9 1.7 %copy-start.1 = (f32[1,2,2,256,256]{4,3,2,1,0:T(8,128)S(1)}, f32[1,2,2,256,256]{4,3,2,1,0:T(8,128)}, u32[]{:S(2)}) copy-start(f32[1,2,2,256,256]{4,3,2,1,0:T(8,128)} %param.8) | copy-start | bytes 3145732
  12.9 1.5 %collective-permute-start.3 = (f32[2,2,128,128]{3,2,1,0:T(8,128)S(1)}, f32[2,2,128,128]{3,2,1,0:T(8,128)S(1)}, u32[]{:S(2)}, u32[]{:S(2)}) collective-permute-start(f32[2,2,128,128]{3,2,1,0:T(8,128)S(1)} %collective-permute-done.2.refs_10_), channel_id=1, source_target_pairs={{0,1},{1,0},{2,3},{3,2},{4,5},{5,4},{6,7},{7,6},{8,9},{9,8},{10,11... | collective-permute-start | bytes 786440 | tf_op jit(solution)/shard_map/ppermute | solution.py:29
  21.5 4.7 %collective-permute-start.4 = (f32[2,2,64,384]{3,2,1,0:T(8,128)S(1)}, f32[2,2,64,384]{3,2,1,0:T(8,128)S(1)}, u32[]{:S(2)}, u32[]{:S(2)}) collective-permute-start(f32[2,2,64,384]{3,2,1,0:T(8,128)S(1)} %get-tuple-element.35), channel_id=1, source_target_pairs={{0,1},{1,0},{2,3},{3,2},{4,5},{5,4},{6,7},{7,6},{8,9},{9,8},{10,11... | collective-permute-start | bytes 1179656 | tf_op jit(solution)/shard_map/ppermute | solution.py:29
  21.6 1.8 %collective-permute-start.6 = (f32[2,128,128]{2,1,0:T(8,128)S(1)}, f32[2,128,128]{2,1,0:T(8,128)S(1)}, u32[]{:S(2)}, u32[]{:S(2)}) collective-permute-start(f32[2,128,128]{2,1,0:T(8,128)S(1)} %get-tuple-element.37), channel_id=1, source_target_pairs={{0,1},{1,0},{2,3},{3,2},{4,5},{5,4},{6,7},{7,6},{8,9},{9,8},{10,11... | collective-permute-start | bytes 393224 | tf_op jit(solution)/shard_map/ppermute | solution.py:29
  23.4 6.5 %collective-permute-start.7 = (f32[2,128,128]{2,1,0:T(8,128)S(1)}, f32[2,128,128]{2,1,0:T(8,128)S(1)}, u32[]{:S(2)}, u32[]{:S(2)}) collective-permute-start(f32[2,128,128]{2,1,0:T(8,128)S(1)} %add.28), channel_id=1, source_target_pairs={{0,4},{4,0},{8,12},{12,8},{16,20},{20,16},{24,28},{28,24},{1,5},{5... | collective-permute-start | bytes 393224 | tf_op jit(solution)/shard_map/ppermute | solution.py:29
  30.0 5.3 %collective-permute-start.8 = (f32[2,128,128]{2,1,0:T(8,128)S(1)}, f32[2,128,128]{2,1,0:T(8,128)S(1)}, u32[]{:S(2)}, u32[]{:S(2)}) collective-permute-start(f32[2,128,128]{2,1,0:T(8,128)S(1)} %add.29), channel_id=1, source_target_pairs={{0,8},{4,12},{8,0},{12,4},{16,24},{20,28},{24,16},{28,20},{1,9},{5... | collective-permute-start | bytes 393224 | tf_op jit(solution)/shard_map/ppermute | solution.py:29
  31.6 11.7 %collective-permute-start.5 = (f32[2,2,64,128]{3,2,1,0:T(8,128)S(1)}, f32[2,2,64,128]{3,2,1,0:T(8,128)S(1)}, u32[]{:S(2)}, u32[]{:S(2)}) collective-permute-start(f32[2,2,64,128]{3,2,1,0:T(8,128)S(1)} %slice.41), channel_id=1, source_target_pairs={{0,4},{4,8},{8,12},{12,16},{16,20},{20,24},{24,28},{1,5},{5,9},{9,... | collective-permute-start | bytes 393224 | tf_op jit(solution)/shard_map/ppermute | solution.py:25
  35.3 7.9 %collective-permute-start.9 = (f32[2,128,128]{2,1,0:T(8,128)S(1)}, f32[2,128,128]{2,1,0:T(8,128)S(1)}, u32[]{:S(2)}, u32[]{:S(2)}) collective-permute-start(f32[2,128,128]{2,1,0:T(8,128)S(1)} %add.30), channel_id=1, source_target_pairs={{0,16},{4,20},{8,24},{12,28},{16,0},{20,4},{24,8},{28,12},{1,17},{... | collective-permute-start | bytes 393224 | tf_op jit(solution)/shard_map/ppermute | solution.py:29
  43.3 1.4 %collective-permute-start.10 = (f32[2,128,128]{2,1,0:T(8,128)S(1)}, f32[2,128,128]{2,1,0:T(8,128)S(1)}, u32[]{:S(2)}, u32[]{:S(2)}) collective-permute-start(f32[2,128,128]{2,1,0:T(8,128)S(1)} %add_multiply_fusion), channel_id=1, source_target_pairs={{0,1},{1,0},{2,3},{3,2},{4,5},{5,4},{6,7},{7,6},{8,9},{9,8},{10,11... | collective-permute-start | bytes 393224 | tf_op jit(solution)/shard_map/ppermute | solution.py:29
  43.4 1.3 %copy-start.7 = (f32[1,2,2,64,256]{4,3,2,1,0:T(8,128)}, f32[1,2,2,64,256]{4,3,2,1,0:T(8,128)S(1)}, u32[]{:S(2)}) copy-start(f32[1,2,2,64,256]{4,3,2,1,0:T(8,128)S(1)} %fusion.1) | copy-start | bytes 786436

commit v5 on v4

--- a/solution.py
+++ b/solution.py
@@ -167,8 +167,9 @@
     offset_refs, core_ref = refs[:positions], refs[positions]
     own_refs, refs = refs[positions + 1 : 2 * positions + 1], refs[2 * positions + 1 :]
     probe_ref, prop_ref, table_ref = refs[:3]
-    measured_refs, pieces = refs[3 : 3 + positions], refs[3 + positions : -4]
-    grad_ref, keep_ref, send_ref, strip_ref = refs[-4:]
+    measured_refs, pieces = refs[3 : 3 + positions], refs[3 + positions : -6]
+    kept_ref, given_ref, keep_ref, send_ref, strip_ref, frame_ref = refs[-6:]
+    frame_ref[...] = jnp.zeros_like(frame_ref)
     layers = own_refs[0].shape[0]
     probe, prop, forward, backward = wave_tools(probe_ref, prop_ref, table_ref)
     modes = len(probe)
@@ -192,17 +193,33 @@
         parts = [times_conj(f, e) for f, e in zip(fields, entering[layer])]
         for p in range(positions):
             for part in range(2):
-                grad_ref[p, layer, part] = sum(c[part] for c in parts[p * modes : (p + 1) * modes])
+                block = sum(c[part] for c in parts[p * modes : (p + 1) * modes])
+                lay(frame_ref, layer, part, offset_refs[p], block, p == 0)
         fields = [times_conj(f, w) for f, w in zip(fields, windows[layer])]
         if layer > 0:
             fields = transform(fields, backward, forward)
             fields = [times_conj(f, prop) for f in fields]
             fields = transform(fields, forward, backward)
     core = core_ref[0]
+    count = kept_ref.shape[2]
+    for share, out_ref in ((core_ref[1], kept_ref), (core_ref[1] ^ 1, given_ref)):
+        share = share if positions > 1 else 0
+        out_ref[...] = frame_ref[:, :, pl.ds(pl.multiple_of(share * count, count), count), :]
     for m in range(modes):
         real, imag = (sum(fields[p * modes + m][part] for p in range(positions)) for part in range(2))
         keep_ref[m] = jnp.where(core == 0, real, imag)
         send_ref[m] = jnp.where(core == 0, imag, real)
+
+
+def lay(frame_ref, layer, part, offset_ref, block, first):
+    extent = block.shape[-1]
+    row, col = offset_ref[0], offset_ref[1]
+    rows = pl.ds(pl.multiple_of(row // ROWS * ROWS, ROWS), extent + ROWS)
+    cols = pl.ds(pl.multiple_of(col // extent * extent, extent), 2 * extent)
+    block = jnp.concatenate([block, jnp.zeros((ROWS, extent), F32)], 0)
+    block = pltpu.roll(block, lax.rem(row, ROWS), 0)
+    wide = pltpu.roll(jnp.concatenate([block, jnp.zeros_like(block)], 1), lax.rem(col, extent), 1)
+    frame_ref[layer, part, rows, cols] = wide if first else wide + frame_ref[layer, part, rows, cols]
 
 
 VMEM = pl.BlockSpec(memory_space=pltpu.VMEM)
@@ -221,27 +238,6 @@
         cost_estimate=pl.CostEstimate(flops=flops, bytes_accessed=sizes, transcendentals=0),
         name=name,
     )(*scalars, *arrays)
-
-
-def spread_kernel(shares, *refs):
-    offset_refs, (share_ref, window_ref, keep_ref, send_ref, frame_ref) = refs[:-5], refs[-5:]
-    extent = window_ref.shape[-1]
-    frame_ref[...] = jnp.zeros_like(frame_ref)
-    for p, offset_ref in enumerate(offset_refs):
-        row, col = offset_ref[0], offset_ref[1]
-        rows = pl.ds(pl.multiple_of(row // ROWS * ROWS, ROWS), extent + ROWS)
-        cols = pl.ds(pl.multiple_of(col // extent * extent, extent), 2 * extent)
-        for layer in range(window_ref.shape[1]):
-            for part in range(2):
-                block = jnp.concatenate([window_ref[p, layer, part], jnp.zeros((ROWS, extent), F32)], 0)
-                block = pltpu.roll(block, lax.rem(row, ROWS), 0)
-                wide = pltpu.roll(jnp.concatenate([block, jnp.zeros_like(block)], 1), lax.rem(col, extent), 1)
-                at = (layer, part, rows, cols)
-                frame_ref[at] = wide if p == 0 else wide + frame_ref[at]
-    count = keep_ref.shape[2]
-    for share, out_ref in ((share_ref[0], keep_ref), (share_ref[0] ^ 1, send_ref)):
-        share = share if shares > 1 else 0
-        out_ref[...] = frame_ref[:, :, pl.ds(pl.multiple_of(share * count, count), count), :]
 
 
 def local(object_slices, probe, prop_phase, scan_offsets, measured):
@@ -281,27 +277,21 @@
         rim = own_tile[:, :, :extent]
         pieces.append(passed_along(rim, "tile", -TGX))
         pieces.append(passed_along(rim[..., :extent], "tile", -TGX - 1))
-    window_grad, probe_keep, probe_send = kernel_call(
-        functools.partial(wave_kernel, positions), "wave_gradients", offsets + [core],
-        owns + [probe_in, prop, table_in] + targets + pieces,
-        [((positions, layers, 2) + field, F32), (probe.shape[:1] + field, F32), (probe.shape[:1] + field, F32)],
-        [(layers, 2, tile_side, extent)],
-    )
-
-    got = exchanged(probe_send, "batch", 1)
     cols = tile_side + extent
-    rounds = [("batch", 1 << k) for k in range(1, (shares - 1).bit_length())]
-    if paired:
-        rounds = []
-    rounds += [("tile", 1 << k) for k in range((tiles - 1).bit_length())]
     frame_rows = tile_side + (extent if tall else 0)
     share_rows = tile_side // shares if paired else frame_rows
-    kept, given = kernel_call(
-        functools.partial(spread_kernel, shares if paired else 1), "spread_windows", offsets + [share], [window_grad],
-        [((layers, 2, share_rows, cols), F32)] * 2, [(layers, 2, frame_rows + ROWS, cols)],
-    )
+    kept, given, probe_keep, probe_send = kernel_call(
+        functools.partial(wave_kernel, positions), "wave_gradients", offsets + [jnp.concatenate([core, share])],
+        owns + [probe_in, prop, table_in] + targets + pieces,
+        [((layers, 2, share_rows, cols), F32)] * 2 + [(probe.shape[:1] + field, F32)] * 2,
+        [(layers, 2, tile_side, extent), (layers, 2, frame_rows + ROWS, cols)],
+    )
+
+    got = exchanged(probe_send, "batch", 1)
+    rounds = [] if paired else [("batch", 1 << k) for k in range(1, (shares - 1).bit_length())]
+    rounds += [("tile", 1 << k) for k in range((tiles - 1).bit_length())]
     if paired:
-        total = probe_keep + after(got, given)
+        total = probe_keep + got
         summed = kept + exchanged(given, "batch", 1)
         landed = passed_along(summed[:, :, :, tile_side:], "tile", 1)
         object_share = summed[:, :, :, :tile_side].at[:, :, :, :extent].add(landed)
@@ -318,9 +308,15 @@
             core_grad = core_grad.at[:, :, : landed.shape[2], : landed.shape[3]].add(landed)
         object_share = lax.psum_scatter(core_grad, "batch", scatter_dimension=2, tiled=True)
         beside = []
-    for k, (axis, bit) in enumerate(rounds):
-        got = exchanged(total, axis, bit)
-        total = total + (after(got, *beside[k]) if k < len(beside) else got)
+    if paired:
+        nodes = range(tiles * shares)
+        for k in range(len(rounds)):
+            even, odd = shares * rounds[k][1], shares * rounds[(0, 2, 1)[k]][1]
+            got = lax.ppermute(total, ("tile", "batch"), [(i, i ^ (odd if i % 2 else even)) for i in nodes])
+            total = total + (after(got, *beside[k]) if k < len(beside) else got)
+    else:
+        for axis, bit in rounds:
+            total = total + exchanged(total, axis, bit)
     total = total / (tiles * shares)
     other = exchanged(total, "batch", 1)
     even = core[0] == 0

time: 45.7 us -> 43.4 us (0.950)
  waiting for transfers between devices: 16.5 us -> 15.2 us
  Pallas kernels: 8.97 us -> 8.32 us
  starting transfers between devices: 16 us -> 15.5 us
    ppermute x9 -> x6, waiting for transfers between devices: 14 us -> 4.71 us  [exchanged(): lax.ppermute(block, axis, [(i, i ^ bit) for i in range(lax.axis_size(axis...]
    ppermute x0 -> x3, waiting for transfers between devices: none -> 8.06 us  [local(): lax.ppermute(total, ('tile', 'batch'), [(i, i ^ (odd if i % 2 else even))...]
    ppermute x9 -> x6, starting transfers between devices: 11 us -> 4.26 us  [exchanged(): lax.ppermute(block, axis, [(i, i ^ bit) for i in range(lax.axis_size(axis...]
    ppermute x0 -> x3, starting transfers between devices: none -> 6.32 us  [local(): lax.ppermute(total, ('tile', 'batch'), [(i, i ^ (odd if i % 2 else even))...]
    pallas_call x4 -> x3, Pallas kernels: 8.97 us -> 8.32 us  [kernel_call(): pl.pallas_call(kernel, out_shape=[jax.ShapeDtypeStruct(shape, dtype) for...]
  transfers between devices with their start and end apart: 11 -> 11, of which waited for: 7 -> 8; matrix products, arithmetic and copies ran while one was open for 0% -> 1% of each run, Pallas kernels for 4% -> 4%
where the time goes in v5:
time: 43.4 us; the launch traced here: 43.2 us
  starting transfers between devices  15.5 us (36%)
  waiting for transfers between devices  15.2 us (35%)
  Pallas kernels  8.32 us (19%)
  local copies, waits for them, and re-layouts  3.04 us (7%)
  between operations  0.83 us (2%)
    pallas_call x3, Pallas kernels, kernel_call(): pl.pallas_call(kernel, out_shape=[jax.ShapeDtypeStruct(shape, dtype) for...  8.32 us
    ppermute x3, waiting for transfers between devices, local(): lax.ppermute(total, ('tile', 'batch'), [(i, i ^ (odd if i % 2 else even))...  8.06 us
    ppermute x3, starting transfers between devices, local(): lax.ppermute(total, ('tile', 'batch'), [(i, i ^ (odd if i % 2 else even))...  6.32 us
    ppermute x2, starting transfers between devices, passed_along(): return lax.ppermute(block, axis, route)  4.94 us
    ppermute x6, waiting for transfers between devices, exchanged(): lax.ppermute(block, axis, [(i, i ^ bit) for i in range(lax.axis_size(axis...  4.71 us
    ppermute x6, starting transfers between devices, exchanged(): lax.ppermute(block, axis, [(i, i ^ bit) for i in range(lax.axis_size(axis...  4.26 us
    ppermute x2, waiting for transfers between devices, passed_along(): return lax.ppermute(block, axis, route)  2.46 us
    unnamed x17, local copies, waits for them, and re-layouts  1.98 us
  transfers between devices with their start and end apart: 11, of which 8 were waited for; matrix products, arithmetic and copies ran while one was open for 1% of the time, Pallas kernels for 4%

profile of v5, /device:TPU:0, one launch (start us, length us, event | category | flops | bytes accessed | tf_op | source)
XLA Modules:
  0.0 43.2 jit_solution(16006856205729971122)
XLA Ops:
  0.7 1.0 %dynamic-slice_bitcast_fusion = f32[2,2,128,128]{3,2,1,0:T(8,128)S(1)} fusion(f32[1,2,2,256,256]{4,3,2,1,0:T(8,128)} %param.8, s32[]{:T(128)S(6)} %select_n.15), kind=kLoop, calls=%fused_computation.2 | loop fusion | bytes 524292 | tf_op jit(solution)/shard_map/dynamic_slice | solution.py:273
  1.7 1.3 %collective-permute-start.2 = (f32[2,2,128,128]{3,2,1,0:T(8,128)S(1)}, f32[2,2,128,128]{3,2,1,0:T(8,128)S(1)}, u32[]{:S(2)}, u32[]{:S(2)}) collective-permute-start(f32[2,2,128,128]{3,2,1,0:T(8,128)S(1)} %dynamic-slice_bitcast_fusion), channel_id=1, source_target_pairs={{4,0},{8,4},{12,8},{16,12},{20,16},{24,20},{28,24},{5,1},{9,5},{13... | collective-permute-start | bytes 786440 | tf_op jit(solution)/shard_map/ppermute | solution.py:25
  3.0 3.0 %collective-permute-start.1 = (f32[128,128]{1,0:T(8,128)S(1)}, f32[128,128]{1,0:T(8,128)S(1)}, u32[]{:S(2)}, u32[]{:S(2)}) collective-permute-start(f32[128,128]{1,0:T(8,128)S(1)} %bitcast.20), channel_id=1, source_target_pairs={{0,2},{1,3},{2,0},{3,1},{4,6},{5,7},{6,4},{7,5},{8,10},{9,11},{10,... | collective-permute-start | bytes 196616 | tf_op jit(solution)/shard_map/ppermute | solution.py:29
  6.1 0.6 %collective-permute-start = (s32[2]{0:T(128)S(1)}, s32[2]{0:T(128)S(1)}, u32[]{:S(2)}, u32[]{:S(2)}) collective-permute-start(s32[2]{0:T(128)S(1)} %bitcast.22), channel_id=1, source_target_pairs={{0,2},{1,3},{2,0},{3,1},{4,6},{5,7},{6,4},{7,5},{8,10},{9,11},{10,... | collective-permute-start | bytes 32 | tf_op jit(solution)/shard_map/ppermute | solution.py:29
  6.7 1.2 %copy-done = f32[1,2,2,256,256]{4,3,2,1,0:T(8,128)S(1)} copy-done((f32[1,2,2,256,256]{4,3,2,1,0:T(8,128)S(1)}, f32[1,2,2,256,256]{4,3,2,1,0:T(8,128)}, u32[]{:S(2)}) %copy-start) | copy-done | bytes 1048600
  7.9 1.2 %own_windows.1 = (f32[2,2,128,128]{3,2,1,0:T(8,128)S(1)}, f32[2,128,128]{2,1,0:T(8,128)S(1)}, f32[2,2,128,128]{3,2,1,0:T(8,128)S(1)}, bf16[2,2,128,128]{3,2,1,0:T(8,128)(2,1)S(1)}) custom-call(s32[2]{0:T(128)S(1)} %bitcast.23, f32[2,2,256,256]{3,2,1,0:T(8,128)S(1)} %bitcast.18, f32[128,128]{1,0:T(8,128)S(1)} %copy-done.4, f32[2,2,128,128]{3,2,1,0:T(8,128)S(1)} %copy-done.2, ...), custom_call_target="tpu_custom_call" | custom-call | bytes 1507328 | tf_op jit(solution)/shard_map/own_windows/pallas_call | solution.py:231
  9.1 0.6 %collective-permute-done.offset_ref.refs_1_ = s32[2]{0:T(128)S(1)} collective-permute-done((s32[2]{0:T(128)S(1)}, s32[2]{0:T(128)S(1)}, u32[]{:S(2)}, u32[]{:S(2)}) %collective-permute-start) | collective-permute-done | bytes 40 | tf_op jit(solution)/shard_map/ppermute | solution.py:29
  9.6 0.8 %partner_windows.1.refs_4_ = f32[2,2,128,128]{3,2,1,0:T(8,128)S(1)} custom-call(s32[2]{0:T(128)S(1)} %collective-permute-done.offset_ref.refs_1_, f32[2,2,256,256]{3,2,1,0:T(8,128)S(1)} %bitcast.19), custom_call_target="tpu_custom_call" | custom-call | bytes 1048576 | tf_op jit(solution)/shard_map/partner_windows/pallas_call | solution.py:231
  10.4 2.5 %collective-permute-done.2.refs_10_ = f32[2,2,128,128]{3,2,1,0:T(8,128)S(1)} collective-permute-done((f32[2,2,128,128]{3,2,1,0:T(8,128)S(1)}, f32[2,2,128,128]{3,2,1,0:T(8,128)S(1)}, u32[]{:S(2)}, u32[]{:S(2)}) %collective-permute-start.2) | collective-permute-done | bytes 262176 | tf_op jit(solution)/shard_map/ppermute | solution.py:25
  12.9 0.1 pad_add_fusion.refs_2_
  12.9 1.5 %collective-permute-done.3.refs_11_ = f32[2,2,128,128]{3,2,1,0:T(8,128)S(1)} collective-permute-done((f32[2,2,128,128]{3,2,1,0:T(8,128)S(1)}, f32[2,2,128,128]{3,2,1,0:T(8,128)S(1)}, u32[]{:S(2)}, u32[]{:S(2)}) %collective-permute-start.3) | collective-permute-done | bytes 262176 | tf_op jit(solution)/shard_map/ppermute | solution.py:29
  14.4 6.4 %wave_gradients.1 = (f32[2,2,64,384]{3,2,1,0:T(8,128)S(1)}, f32[2,2,64,384]{3,2,1,0:T(8,128)S(1)}, f32[2,128,128]{2,1,0:T(8,128)S(1)}, f32[2,128,128]{2,1,0:T(8,128)S(1)}) custom-call(s32[2]{0:T(128)S(1)} %bitcast.24, s32[2]{0:T(128)S(1)} %collective-permute-done.offset_ref.refs_1_, s32[2]{0:T(128)S(1)} %pad_add_fusion.refs_2_, ...), custom_call_target="tpu_custom_call" | custom-call | bytes 1703936 | tf_op jit(solution)/shard_map/wave_gradients/pallas_call | solution.py:231
  20.8 0.2 collective-permute-start.4
  21.0 0.4 collective-permute-start.6
  21.4 1.4 %collective-permute-done.6 = f32[2,128,128]{2,1,0:T(8,128)S(1)} collective-permute-done((f32[2,128,128]{2,1,0:T(8,128)S(1)}, f32[2,128,128]{2,1,0:T(8,128)S(1)}, u32[]{:S(2)}, u32[]{:S(2)}) %collective-permute-start.6) | collective-permute-done | bytes 131104 | tf_op jit(solution)/shard_map/ppermute | solution.py:29
  22.8 2.7 %collective-permute-start.7 = (f32[2,128,128]{2,1,0:T(8,128)S(1)}, f32[2,128,128]{2,1,0:T(8,128)S(1)}, u32[]{:S(2)}, u32[]{:S(2)}) collective-permute-start(f32[2,128,128]{2,1,0:T(8,128)S(1)} %add.28), channel_id=1, source_target_pairs={{0,4},{1,5},{2,6},{3,7},{4,0},{5,1},{6,2},{7,3},{8,12},{9,13},{10,... | collective-permute-start | bytes 393224 | tf_op jit(solution)/shard_map/ppermute | solution.py:315
  25.6 3.7 %collective-permute-done.7 = f32[2,128,128]{2,1,0:T(8,128)S(1)} collective-permute-done((f32[2,128,128]{2,1,0:T(8,128)S(1)}, f32[2,128,128]{2,1,0:T(8,128)S(1)}, u32[]{:S(2)}, u32[]{:S(2)}) %collective-permute-start.7) | collective-permute-done | bytes 131104 | tf_op jit(solution)/shard_map/ppermute | solution.py:315
  29.3 1.6 %collective-permute-start.8 = (f32[2,128,128]{2,1,0:T(8,128)S(1)}, f32[2,128,128]{2,1,0:T(8,128)S(1)}, u32[]{:S(2)}, u32[]{:S(2)}) collective-permute-start(f32[2,128,128]{2,1,0:T(8,128)S(1)} %add.29), channel_id=1, source_target_pairs={{0,8},{1,17},{2,10},{3,19},{4,12},{5,21},{6,14},{7,23},{8,0},{9,25... | collective-permute-start | bytes 393224 | tf_op jit(solution)/shard_map/ppermute | solution.py:315
  31.0 3.7 %collective-permute-start.5 = (f32[2,2,64,128]{3,2,1,0:T(8,128)S(1)}, f32[2,2,64,128]{3,2,1,0:T(8,128)S(1)}, u32[]{:S(2)}, u32[]{:S(2)}) collective-permute-start(f32[2,2,64,128]{3,2,1,0:T(8,128)S(1)} %slice.41), channel_id=1, source_target_pairs={{0,4},{4,8},{8,12},{12,16},{16,20},{20,24},{24,28},{1,5},{5,9},{9,... | collective-permute-start | bytes 393224 | tf_op jit(solution)/shard_map/ppermute | solution.py:25
  34.6 0.4 collective-permute-done.8
  35.0 2.0 %collective-permute-start.9 = (f32[2,128,128]{2,1,0:T(8,128)S(1)}, f32[2,128,128]{2,1,0:T(8,128)S(1)}, u32[]{:S(2)}, u32[]{:S(2)}) collective-permute-start(f32[2,128,128]{2,1,0:T(8,128)S(1)} %add.30), channel_id=1, source_target_pairs={{0,16},{1,9},{2,18},{3,11},{4,20},{5,13},{6,22},{7,15},{8,24},{9,1... | collective-permute-start | bytes 393224 | tf_op jit(solution)/shard_map/ppermute | solution.py:315
  37.0 3.9 %collective-permute-done.9 = f32[2,128,128]{2,1,0:T(8,128)S(1)} collective-permute-done((f32[2,128,128]{2,1,0:T(8,128)S(1)}, f32[2,128,128]{2,1,0:T(8,128)S(1)}, u32[]{:S(2)}, u32[]{:S(2)}) %collective-permute-start.9) | collective-permute-done | bytes 131104 | tf_op jit(solution)/shard_map/ppermute | solution.py:315
  41.1 1.3 %collective-permute-done.10 = f32[2,128,128]{2,1,0:T(8,128)S(1)} collective-permute-done((f32[2,128,128]{2,1,0:T(8,128)S(1)}, f32[2,128,128]{2,1,0:T(8,128)S(1)}, u32[]{:S(2)}, u32[]{:S(2)}) %collective-permute-start.10) | collective-permute-done | bytes 131104 | tf_op jit(solution)/shard_map/ppermute | solution.py:29
  42.5 0.7 %copy.8 = f32[2,2,128,128]{3,2,1,0:T(8,128)} copy(f32[2,2,128,128]{3,2,0,1:T(8,128)S(1)} %pad_maximum_fusion) | data formatting | bytes 524288
  (30 shorter events, 0.3 us)
Async XLA Ops:
  0.6 2.4 %copy-start.5 = (f32[1,1,128,128]{3,2,1,0:T(8,128)S(1)}, f32[1,1,128,128]{3,2,1,0:T(8,128)}, u32[]{:S(2)}) copy-start(f32[1,1,128,128]{3,2,1,0:T(8,128)} %param.12) | copy-start | bytes 196612
  0.6 6.0 %copy-start.2 = (f32[2,2,128,128]{3,2,1,0:T(8,128)S(1)}, f32[2,2,128,128]{3,2,1,0:T(8,128)}, u32[]{:S(2)}) copy-start(f32[2,2,128,128]{3,2,1,0:T(8,128)} %probe_in_ref.1) | copy-start | bytes 786436
  0.7 6.0 %copy-start.3 = (bf16[2,2,128,128]{3,2,1,0:T(8,128)(2,1)S(1)}, bf16[2,2,128,128]{3,2,1,0:T(8,128)(2,1)}, u32[]{:S(2)}) copy-start(bf16[2,2,128,128]{3,2,1,0:T(8,128)(2,1)} %constant.48.clone.table_in_ref) | copy-start | bytes 393220
  0.7 6.0 %copy-start.4 = (f32[128,128]{1,0:T(8,128)S(1)}, f32[128,128]{1,0:T(8,128)}, u32[]{:S(2)}) copy-start(f32[128,128]{1,0:T(8,128)} %phase_ref.1) | copy-start | bytes 196612
  1.7 11.1 %collective-permute-start.2 = (f32[2,2,128,128]{3,2,1,0:T(8,128)S(1)}, f32[2,2,128,128]{3,2,1,0:T(8,128)S(1)}, u32[]{:S(2)}, u32[]{:S(2)}) collective-permute-start(f32[2,2,128,128]{3,2,1,0:T(8,128)S(1)} %dynamic-slice_bitcast_fusion), channel_id=1, source_target_pairs={{4,0},{8,4},{12,8},{16,12},{20,16},{24,20},{28,24},{5,1},{9,5},{13... | collective-permute-start | bytes 786440 | tf_op jit(solution)/shard_map/ppermute | solution.py:25
  3.0 3.0 %copy-start.6 = (s32[1,1,2]{2,1,0:T(1,128)S(1)}, s32[1,1,2]{2,1,0:T(1,128)}, u32[]{:S(2)}) copy-start(s32[1,1,2]{2,1,0:T(1,128)} %param.11) | copy-start | bytes 28
  3.0 7.4 %collective-permute-start.1 = (f32[128,128]{1,0:T(8,128)S(1)}, f32[128,128]{1,0:T(8,128)S(1)}, u32[]{:S(2)}, u32[]{:S(2)}) collective-permute-start(f32[128,128]{1,0:T(8,128)S(1)} %bitcast.20), channel_id=1, source_target_pairs={{0,2},{1,3},{2,0},{3,1},{4,6},{5,7},{6,4},{7,5},{8,10},{9,11},{10,... | collective-permute-start | bytes 196616 | tf_op jit(solution)/shard_map/ppermute | solution.py:29
  6.1 3.5 %collective-permute-start = (s32[2]{0:T(128)S(1)}, s32[2]{0:T(128)S(1)}, u32[]{:S(2)}, u32[]{:S(2)}) collective-permute-start(s32[2]{0:T(128)S(1)} %bitcast.22), channel_id=1, source_target_pairs={{0,2},{1,3},{2,0},{3,1},{4,6},{5,7},{6,4},{7,5},{8,10},{9,11},{10,... | collective-permute-start | bytes 32 | tf_op jit(solution)/shard_map/ppermute | solution.py:29
  6.7 1.2 %copy-start = (f32[1,2,2,256,256]{4,3,2,1,0:T(8,128)S(1)}, f32[1,2,2,256,256]{4,3,2,1,0:T(8,128)}, u32[]{:S(2)}) copy-start(f32[1,2,2,256,256]{4,3,2,1,0:T(8,128)} %param.8) | copy-start | bytes 3145732
  7.9 1.7 %copy-start.1 = (f32[1,2,2,256,256]{4,3,2,1,0:T(8,128)S(1)}, f32[1,2,2,256,256]{4,3,2,1,0:T(8,128)}, u32[]{:S(2)}) copy-start(f32[1,2,2,256,256]{4,3,2,1,0:T(8,128)} %param.8) | copy-start | bytes 3145732
  12.9 1.5 %collective-permute-start.3 = (f32[2,2,128,128]{3,2,1,0:T(8,128)S(1)}, f32[2,2,128,128]{3,2,1,0:T(8,128)S(1)}, u32[]{:S(2)}, u32[]{:S(2)}) collective-permute-start(f32[2,2,128,128]{3,2,1,0:T(8,128)S(1)} %collective-permute-done.2.refs_10_), channel_id=1, source_target_pairs={{0,1},{1,0},{2,3},{3,2},{4,5},{5,4},{6,7},{7,6},{8,9},{9,8},{10,11... | collective-permute-start | bytes 786440 | tf_op jit(solution)/shard_map/ppermute | solution.py:29
  20.8 4.7 %collective-permute-start.4 = (f32[2,2,64,384]{3,2,1,0:T(8,128)S(1)}, f32[2,2,64,384]{3,2,1,0:T(8,128)S(1)}, u32[]{:S(2)}, u32[]{:S(2)}) collective-permute-start(f32[2,2,64,384]{3,2,1,0:T(8,128)S(1)} %get-tuple-element.32), channel_id=1, source_target_pairs={{0,1},{1,0},{2,3},{3,2},{4,5},{5,4},{6,7},{7,6},{8,9},{9,8},{10,11... | collective-permute-start | bytes 1179656 | tf_op jit(solution)/shard_map/ppermute | solution.py:29
  21.0 1.8 %collective-permute-start.6 = (f32[2,128,128]{2,1,0:T(8,128)S(1)}, f32[2,128,128]{2,1,0:T(8,128)S(1)}, u32[]{:S(2)}, u32[]{:S(2)}) collective-permute-start(f32[2,128,128]{2,1,0:T(8,128)S(1)} %get-tuple-element.34), channel_id=1, source_target_pairs={{0,1},{1,0},{2,3},{3,2},{4,5},{5,4},{6,7},{7,6},{8,9},{9,8},{10,11... | collective-permute-start | bytes 393224 | tf_op jit(solution)/shard_map/ppermute | solution.py:29
  22.8 6.5 %collective-permute-start.7 = (f32[2,128,128]{2,1,0:T(8,128)S(1)}, f32[2,128,128]{2,1,0:T(8,128)S(1)}, u32[]{:S(2)}, u32[]{:S(2)}) collective-permute-start(f32[2,128,128]{2,1,0:T(8,128)S(1)} %add.28), channel_id=1, source_target_pairs={{0,4},{1,5},{2,6},{3,7},{4,0},{5,1},{6,2},{7,3},{8,12},{9,13},{10,... | collective-permute-start | bytes 393224 | tf_op jit(solution)/shard_map/ppermute | solution.py:315
  29.3 5.7 %collective-permute-start.8 = (f32[2,128,128]{2,1,0:T(8,128)S(1)}, f32[2,128,128]{2,1,0:T(8,128)S(1)}, u32[]{:S(2)}, u32[]{:S(2)}) collective-permute-start(f32[2,128,128]{2,1,0:T(8,128)S(1)} %add.29), channel_id=1, source_target_pairs={{0,8},{1,17},{2,10},{3,19},{4,12},{5,21},{6,14},{7,23},{8,0},{9,25... | collective-permute-start | bytes 393224 | tf_op jit(solution)/shard_map/ppermute | solution.py:315
  31.0 10.1 %collective-permute-start.5 = (f32[2,2,64,128]{3,2,1,0:T(8,128)S(1)}, f32[2,2,64,128]{3,2,1,0:T(8,128)S(1)}, u32[]{:S(2)}, u32[]{:S(2)}) collective-permute-start(f32[2,2,64,128]{3,2,1,0:T(8,128)S(1)} %slice.41), channel_id=1, source_target_pairs={{0,4},{4,8},{8,12},{12,16},{16,20},{20,24},{24,28},{1,5},{5,9},{9,... | collective-permute-start | bytes 393224 | tf_op jit(solution)/shard_map/ppermute | solution.py:25
  35.0 5.9 %collective-permute-start.9 = (f32[2,128,128]{2,1,0:T(8,128)S(1)}, f32[2,128,128]{2,1,0:T(8,128)S(1)}, u32[]{:S(2)}, u32[]{:S(2)}) collective-permute-start(f32[2,128,128]{2,1,0:T(8,128)S(1)} %add.30), channel_id=1, source_target_pairs={{0,16},{1,9},{2,18},{3,11},{4,20},{5,13},{6,22},{7,15},{8,24},{9,1... | collective-permute-start | bytes 393224 | tf_op jit(solution)/shard_map/ppermute | solution.py:315
  41.0 1.4 %collective-permute-start.10 = (f32[2,128,128]{2,1,0:T(8,128)S(1)}, f32[2,128,128]{2,1,0:T(8,128)S(1)}, u32[]{:S(2)}, u32[]{:S(2)}) collective-permute-start(f32[2,128,128]{2,1,0:T(8,128)S(1)} %add_multiply_fusion), channel_id=1, source_target_pairs={{0,1},{1,0},{2,3},{3,2},{4,5},{5,4},{6,7},{7,6},{8,9},{9,8},{10,11... | collective-permute-start | bytes 393224 | tf_op jit(solution)/shard_map/ppermute | solution.py:29
  41.1 1.3 %copy-start.7 = (f32[1,2,2,64,256]{4,3,2,1,0:T(8,128)}, f32[1,2,2,64,256]{4,3,2,1,0:T(8,128)S(1)}, u32[]{:S(2)}) copy-start(f32[1,2,2,64,256]{4,3,2,1,0:T(8,128)S(1)} %fusion.1) | copy-start | bytes 786436

commit v6 on v5

--- a/solution.py
+++ b/solution.py
@@ -59,6 +59,13 @@
 
 
 def transform(fields, on_left, on_right):
+    outs = []
+    for k in range(0, len(fields), 2):
+        outs += transform_pair(fields[k : k + 2], on_left, on_right)
+    return outs
+
+
+def transform_pair(fields, on_left, on_right):
     extent = fields[0][0].shape[0]
     stacked = jnp.concatenate(
         [jnp.concatenate([f[part] for f in fields], 1) for part in range(2)], 0
@@ -292,7 +299,7 @@
     rounds += [("tile", 1 << k) for k in range((tiles - 1).bit_length())]
     if paired:
         total = probe_keep + got
-        summed = kept + exchanged(given, "batch", 1)
+        summed = kept + exchanged(after(given, total), "batch", 1)
         landed = passed_along(summed[:, :, :, tile_side:], "tile", 1)
         object_share = summed[:, :, :, :tile_side].at[:, :, :, :extent].add(landed)
         beside = [(summed,)]

time: 43.4 us -> 42.2 us (0.972)
  Pallas kernels: 8.32 us -> 7.06 us
    pallas_call x3, Pallas kernels: 8.32 us -> 7.06 us  [kernel_call(): pl.pallas_call(kernel, out_shape=[jax.ShapeDtypeStruct(shape, dtype) for...]
    ppermute x3, waiting for transfers between devices: 8.06 us -> 8.53 us  [local(): lax.ppermute(total, ('tile', 'batch'), [(i, i ^ (odd if i % 2 else even))...]
  transfers between devices with their start and end apart: 11 -> 11, of which waited for: 8 -> 8; matrix products, arithmetic and copies ran while one was open for 1% -> 0% of each run, Pallas kernels for 4% -> 5%
where the time goes in v6:
time: 42.2 us; the launch traced here: 41.9 us
  waiting for transfers between devices  15.5 us (37%)
  starting transfers between devices  15.3 us (36%)
  Pallas kernels  7.06 us (17%)
  local copies, waits for them, and re-layouts  3.04 us (7%)
  between operations  0.83 us (2%)
    ppermute x3, waiting for transfers between devices, local(): lax.ppermute(total, ('tile', 'batch'), [(i, i ^ (odd if i % 2 else even))...  8.53 us
    pallas_call x3, Pallas kernels, kernel_call(): pl.pallas_call(kernel, out_shape=[jax.ShapeDtypeStruct(shape, dtype) for...  7.06 us
    ppermute x3, starting transfers between devices, local(): lax.ppermute(total, ('tile', 'batch'), [(i, i ^ (odd if i % 2 else even))...  6.21 us
    ppermute x2, starting transfers between devices, passed_along(): return lax.ppermute(block, axis, route)  4.95 us
    ppermute x6, waiting for transfers between devices, exchanged(): lax.ppermute(block, axis, [(i, i ^ bit) for i in range(lax.axis_size(axis...  4.52 us
    ppermute x6, starting transfers between devices, exchanged(): lax.ppermute(block, axis, [(i, i ^ bit) for i in range(lax.axis_size(axis...  4.1 us
    ppermute x2, waiting for transfers between devices, passed_along(): return lax.ppermute(block, axis, route)  2.46 us
    unnamed x17, local copies, waits for them, and re-layouts  1.98 us
  transfers between devices with their start and end apart: 11, of which 8 were waited for; matrix products, arithmetic and copies ran while one was open for 0% of the time, Pallas kernels for 5%

profile of v6, /device:TPU:0, one launch (start us, length us, event | category | flops | bytes accessed | tf_op | source)
XLA Modules:
  0.0 41.9 jit_solution(8907750588378325852)
XLA Ops:
  0.7 1.0 %dynamic-slice_bitcast_fusion = f32[2,2,128,128]{3,2,1,0:T(8,128)S(1)} fusion(f32[1,2,2,256,256]{4,3,2,1,0:T(8,128)} %param.8, s32[]{:T(128)S(6)} %select_n.15), kind=kLoop, calls=%fused_computation.2 | loop fusion | bytes 524292 | tf_op jit(solution)/shard_map/dynamic_slice | solution.py:280
  1.7 1.3 %collective-permute-start.2 = (f32[2,2,128,128]{3,2,1,0:T(8,128)S(1)}, f32[2,2,128,128]{3,2,1,0:T(8,128)S(1)}, u32[]{:S(2)}, u32[]{:S(2)}) collective-permute-start(f32[2,2,128,128]{3,2,1,0:T(8,128)S(1)} %dynamic-slice_bitcast_fusion), channel_id=1, source_target_pairs={{4,0},{8,4},{12,8},{16,12},{20,16},{24,20},{28,24},{5,1},{9,5},{13... | collective-permute-start | bytes 786440 | tf_op jit(solution)/shard_map/ppermute | solution.py:25
  3.0 3.0 %collective-permute-start.1 = (f32[128,128]{1,0:T(8,128)S(1)}, f32[128,128]{1,0:T(8,128)S(1)}, u32[]{:S(2)}, u32[]{:S(2)}) collective-permute-start(f32[128,128]{1,0:T(8,128)S(1)} %bitcast.20), channel_id=1, source_target_pairs={{0,2},{1,3},{2,0},{3,1},{4,6},{5,7},{6,4},{7,5},{8,10},{9,11},{10,... | collective-permute-start | bytes 196616 | tf_op jit(solution)/shard_map/ppermute | solution.py:29
  6.1 0.6 %collective-permute-start = (s32[2]{0:T(128)S(1)}, s32[2]{0:T(128)S(1)}, u32[]{:S(2)}, u32[]{:S(2)}) collective-permute-start(s32[2]{0:T(128)S(1)} %bitcast.22), channel_id=1, source_target_pairs={{0,2},{1,3},{2,0},{3,1},{4,6},{5,7},{6,4},{7,5},{8,10},{9,11},{10,... | collective-permute-start | bytes 32 | tf_op jit(solution)/shard_map/ppermute | solution.py:29
  6.7 1.2 %copy-done = f32[1,2,2,256,256]{4,3,2,1,0:T(8,128)S(1)} copy-done((f32[1,2,2,256,256]{4,3,2,1,0:T(8,128)S(1)}, f32[1,2,2,256,256]{4,3,2,1,0:T(8,128)}, u32[]{:S(2)}) %copy-start) | copy-done | bytes 1048600
  7.9 1.2 %own_windows.1 = (f32[2,2,128,128]{3,2,1,0:T(8,128)S(1)}, f32[2,128,128]{2,1,0:T(8,128)S(1)}, f32[2,2,128,128]{3,2,1,0:T(8,128)S(1)}, bf16[2,2,128,128]{3,2,1,0:T(8,128)(2,1)S(1)}) custom-call(s32[2]{0:T(128)S(1)} %bitcast.23, f32[2,2,256,256]{3,2,1,0:T(8,128)S(1)} %bitcast.18, f32[128,128]{1,0:T(8,128)S(1)} %copy-done.4, f32[2,2,128,128]{3,2,1,0:T(8,128)S(1)} %copy-done.2, ...), custom_call_target="tpu_custom_call" | custom-call | bytes 1507328 | tf_op jit(solution)/shard_map/own_windows/pallas_call | solution.py:238
  9.1 0.6 %collective-permute-done.offset_ref.refs_1_ = s32[2]{0:T(128)S(1)} collective-permute-done((s32[2]{0:T(128)S(1)}, s32[2]{0:T(128)S(1)}, u32[]{:S(2)}, u32[]{:S(2)}) %collective-permute-start) | collective-permute-done | bytes 40 | tf_op jit(solution)/shard_map/ppermute | solution.py:29
  9.6 0.8 %partner_windows.1.refs_4_ = f32[2,2,128,128]{3,2,1,0:T(8,128)S(1)} custom-call(s32[2]{0:T(128)S(1)} %collective-permute-done.offset_ref.refs_1_, f32[2,2,256,256]{3,2,1,0:T(8,128)S(1)} %bitcast.19), custom_call_target="tpu_custom_call" | custom-call | bytes 1048576 | tf_op jit(solution)/shard_map/partner_windows/pallas_call | solution.py:238
  10.4 2.5 %collective-permute-done.2.refs_10_ = f32[2,2,128,128]{3,2,1,0:T(8,128)S(1)} collective-permute-done((f32[2,2,128,128]{3,2,1,0:T(8,128)S(1)}, f32[2,2,128,128]{3,2,1,0:T(8,128)S(1)}, u32[]{:S(2)}, u32[]{:S(2)}) %collective-permute-start.2) | collective-permute-done | bytes 262176 | tf_op jit(solution)/shard_map/ppermute | solution.py:25
  12.9 0.1 pad_add_fusion.refs_2_
  12.9 1.5 %collective-permute-done.3.refs_11_ = f32[2,2,128,128]{3,2,1,0:T(8,128)S(1)} collective-permute-done((f32[2,2,128,128]{3,2,1,0:T(8,128)S(1)}, f32[2,2,128,128]{3,2,1,0:T(8,128)S(1)}, u32[]{:S(2)}, u32[]{:S(2)}) %collective-permute-start.3) | collective-permute-done | bytes 262176 | tf_op jit(solution)/shard_map/ppermute | solution.py:29
  14.4 5.1 %wave_gradients.1 = (f32[2,2,64,384]{3,2,1,0:T(8,128)S(1)}, f32[2,2,64,384]{3,2,1,0:T(8,128)S(1)}, f32[2,128,128]{2,1,0:T(8,128)S(1)}, f32[2,128,128]{2,1,0:T(8,128)S(1)}) custom-call(s32[2]{0:T(128)S(1)} %bitcast.24, s32[2]{0:T(128)S(1)} %collective-permute-done.offset_ref.refs_1_, s32[2]{0:T(128)S(1)} %pad_add_fusion.refs_2_, ...), custom_call_target="tpu_custom_call" | custom-call | bytes 1703936 | tf_op jit(solution)/shard_map/wave_gradients/pallas_call | solution.py:238
  19.5 0.2 collective-permute-start.4
  19.7 1.2 %collective-permute-done.4 = f32[2,128,128]{2,1,0:T(8,128)S(1)} collective-permute-done((f32[2,128,128]{2,1,0:T(8,128)S(1)}, f32[2,128,128]{2,1,0:T(8,128)S(1)}, u32[]{:S(2)}, u32[]{:S(2)}) %collective-permute-start.4) | collective-permute-done | bytes 131104 | tf_op jit(solution)/shard_map/ppermute | solution.py:29
  21.0 0.2 collective-permute-start.5
  21.2 2.6 %collective-permute-start.7 = (f32[2,128,128]{2,1,0:T(8,128)S(1)}, f32[2,128,128]{2,1,0:T(8,128)S(1)}, u32[]{:S(2)}, u32[]{:S(2)}) collective-permute-start(f32[2,128,128]{2,1,0:T(8,128)S(1)} %add.26), channel_id=1, source_target_pairs={{0,4},{1,5},{2,6},{3,7},{4,0},{5,1},{6,2},{7,3},{8,12},{9,13},{10,... | collective-permute-start | bytes 393224 | tf_op jit(solution)/shard_map/ppermute | solution.py:322
  23.9 3.9 %collective-permute-done.7 = f32[2,128,128]{2,1,0:T(8,128)S(1)} collective-permute-done((f32[2,128,128]{2,1,0:T(8,128)S(1)}, f32[2,128,128]{2,1,0:T(8,128)S(1)}, u32[]{:S(2)}, u32[]{:S(2)}) %collective-permute-start.7) | collective-permute-done | bytes 131104 | tf_op jit(solution)/shard_map/ppermute | solution.py:322
  27.8 1.6 %collective-permute-start.8 = (f32[2,128,128]{2,1,0:T(8,128)S(1)}, f32[2,128,128]{2,1,0:T(8,128)S(1)}, u32[]{:S(2)}, u32[]{:S(2)}) collective-permute-start(f32[2,128,128]{2,1,0:T(8,128)S(1)} %add.29), channel_id=1, source_target_pairs={{0,8},{1,17},{2,10},{3,19},{4,12},{5,21},{6,14},{7,23},{8,0},{9,25... | collective-permute-start | bytes 393224 | tf_op jit(solution)/shard_map/ppermute | solution.py:322
  29.5 3.7 %collective-permute-start.6 = (f32[2,2,64,128]{3,2,1,0:T(8,128)S(1)}, f32[2,2,64,128]{3,2,1,0:T(8,128)S(1)}, u32[]{:S(2)}, u32[]{:S(2)}) collective-permute-start(f32[2,2,64,128]{3,2,1,0:T(8,128)S(1)} %slice.41), channel_id=1, source_target_pairs={{0,4},{4,8},{8,12},{12,16},{16,20},{20,24},{24,28},{1,5},{5,9},{9,... | collective-permute-start | bytes 393224 | tf_op jit(solution)/shard_map/ppermute | solution.py:25
  33.2 0.6 %collective-permute-done.8 = f32[2,128,128]{2,1,0:T(8,128)S(1)} collective-permute-done((f32[2,128,128]{2,1,0:T(8,128)S(1)}, f32[2,128,128]{2,1,0:T(8,128)S(1)}, u32[]{:S(2)}, u32[]{:S(2)}) %collective-permute-start.8) | collective-permute-done | bytes 131104 | tf_op jit(solution)/shard_map/ppermute | solution.py:322
  33.8 1.9 %collective-permute-start.9 = (f32[2,128,128]{2,1,0:T(8,128)S(1)}, f32[2,128,128]{2,1,0:T(8,128)S(1)}, u32[]{:S(2)}, u32[]{:S(2)}) collective-permute-start(f32[2,128,128]{2,1,0:T(8,128)S(1)} %add.30), channel_id=1, source_target_pairs={{0,16},{1,9},{2,18},{3,11},{4,20},{5,13},{6,22},{7,15},{8,24},{9,1... | collective-permute-start | bytes 393224 | tf_op jit(solution)/shard_map/ppermute | solution.py:322
  35.7 4.0 %collective-permute-done.9 = f32[2,128,128]{2,1,0:T(8,128)S(1)} collective-permute-done((f32[2,128,128]{2,1,0:T(8,128)S(1)}, f32[2,128,128]{2,1,0:T(8,128)S(1)}, u32[]{:S(2)}, u32[]{:S(2)}) %collective-permute-start.9) | collective-permute-done | bytes 131104 | tf_op jit(solution)/shard_map/ppermute | solution.py:322
  39.9 1.3 %collective-permute-done.10 = f32[2,128,128]{2,1,0:T(8,128)S(1)} collective-permute-done((f32[2,128,128]{2,1,0:T(8,128)S(1)}, f32[2,128,128]{2,1,0:T(8,128)S(1)}, u32[]{:S(2)}, u32[]{:S(2)}) %collective-permute-start.10) | collective-permute-done | bytes 131104 | tf_op jit(solution)/shard_map/ppermute | solution.py:29
  41.2 0.7 %copy.8 = f32[2,2,128,128]{3,2,1,0:T(8,128)} copy(f32[2,2,128,128]{3,2,0,1:T(8,128)S(1)} %pad_maximum_fusion) | data formatting | bytes 524288
  (30 shorter events, 0.3 us)
Async XLA Ops:
  0.6 2.4 %copy-start.5 = (f32[1,1,128,128]{3,2,1,0:T(8,128)S(1)}, f32[1,1,128,128]{3,2,1,0:T(8,128)}, u32[]{:S(2)}) copy-start(f32[1,1,128,128]{3,2,1,0:T(8,128)} %param.12) | copy-start | bytes 196612
  0.6 6.0 %copy-start.2 = (f32[2,2,128,128]{3,2,1,0:T(8,128)S(1)}, f32[2,2,128,128]{3,2,1,0:T(8,128)}, u32[]{:S(2)}) copy-start(f32[2,2,128,128]{3,2,1,0:T(8,128)} %probe_in_ref.1) | copy-start | bytes 786436
  0.7 6.0 %copy-start.3 = (bf16[2,2,128,128]{3,2,1,0:T(8,128)(2,1)S(1)}, bf16[2,2,128,128]{3,2,1,0:T(8,128)(2,1)}, u32[]{:S(2)}) copy-start(bf16[2,2,128,128]{3,2,1,0:T(8,128)(2,1)} %constant.48.clone.table_in_ref) | copy-start | bytes 393220
  0.7 6.0 %copy-start.4 = (f32[128,128]{1,0:T(8,128)S(1)}, f32[128,128]{1,0:T(8,128)}, u32[]{:S(2)}) copy-start(f32[128,128]{1,0:T(8,128)} %phase_ref.1) | copy-start | bytes 196612
  1.7 11.1 %collective-permute-start.2 = (f32[2,2,128,128]{3,2,1,0:T(8,128)S(1)}, f32[2,2,128,128]{3,2,1,0:T(8,128)S(1)}, u32[]{:S(2)}, u32[]{:S(2)}) collective-permute-start(f32[2,2,128,128]{3,2,1,0:T(8,128)S(1)} %dynamic-slice_bitcast_fusion), channel_id=1, source_target_pairs={{4,0},{8,4},{12,8},{16,12},{20,16},{24,20},{28,24},{5,1},{9,5},{13... | collective-permute-start | bytes 786440 | tf_op jit(solution)/shard_map/ppermute | solution.py:25
  3.0 3.0 %copy-start.6 = (s32[1,1,2]{2,1,0:T(1,128)S(1)}, s32[1,1,2]{2,1,0:T(1,128)}, u32[]{:S(2)}) copy-start(s32[1,1,2]{2,1,0:T(1,128)} %param.11) | copy-start | bytes 28
  3.0 7.4 %collective-permute-start.1 = (f32[128,128]{1,0:T(8,128)S(1)}, f32[128,128]{1,0:T(8,128)S(1)}, u32[]{:S(2)}, u32[]{:S(2)}) collective-permute-start(f32[128,128]{1,0:T(8,128)S(1)} %bitcast.20), channel_id=1, source_target_pairs={{0,2},{1,3},{2,0},{3,1},{4,6},{5,7},{6,4},{7,5},{8,10},{9,11},{10,... | collective-permute-start | bytes 196616 | tf_op jit(solution)/shard_map/ppermute | solution.py:29
  6.1 3.5 %collective-permute-start = (s32[2]{0:T(128)S(1)}, s32[2]{0:T(128)S(1)}, u32[]{:S(2)}, u32[]{:S(2)}) collective-permute-start(s32[2]{0:T(128)S(1)} %bitcast.22), channel_id=1, source_target_pairs={{0,2},{1,3},{2,0},{3,1},{4,6},{5,7},{6,4},{7,5},{8,10},{9,11},{10,... | collective-permute-start | bytes 32 | tf_op jit(solution)/shard_map/ppermute | solution.py:29
  6.7 1.2 %copy-start = (f32[1,2,2,256,256]{4,3,2,1,0:T(8,128)S(1)}, f32[1,2,2,256,256]{4,3,2,1,0:T(8,128)}, u32[]{:S(2)}) copy-start(f32[1,2,2,256,256]{4,3,2,1,0:T(8,128)} %param.8) | copy-start | bytes 3145732
  7.9 1.7 %copy-start.1 = (f32[1,2,2,256,256]{4,3,2,1,0:T(8,128)S(1)}, f32[1,2,2,256,256]{4,3,2,1,0:T(8,128)}, u32[]{:S(2)}) copy-start(f32[1,2,2,256,256]{4,3,2,1,0:T(8,128)} %param.8) | copy-start | bytes 3145732
  12.9 1.5 %collective-permute-start.3 = (f32[2,2,128,128]{3,2,1,0:T(8,128)S(1)}, f32[2,2,128,128]{3,2,1,0:T(8,128)S(1)}, u32[]{:S(2)}, u32[]{:S(2)}) collective-permute-start(f32[2,2,128,128]{3,2,1,0:T(8,128)S(1)} %collective-permute-done.2.refs_10_), channel_id=1, source_target_pairs={{0,1},{1,0},{2,3},{3,2},{4,5},{5,4},{6,7},{7,6},{8,9},{9,8},{10,11... | collective-permute-start | bytes 786440 | tf_op jit(solution)/shard_map/ppermute | solution.py:29
  19.5 1.4 %collective-permute-start.4 = (f32[2,128,128]{2,1,0:T(8,128)S(1)}, f32[2,128,128]{2,1,0:T(8,128)S(1)}, u32[]{:S(2)}, u32[]{:S(2)}) collective-permute-start(f32[2,128,128]{2,1,0:T(8,128)S(1)} %get-tuple-element.35), channel_id=1, source_target_pairs={{0,1},{1,0},{2,3},{3,2},{4,5},{5,4},{6,7},{7,6},{8,9},{9,8},{10,11... | collective-permute-start | bytes 393224 | tf_op jit(solution)/shard_map/ppermute | solution.py:29
  21.0 2.9 %collective-permute-start.5 = (f32[2,2,64,384]{3,2,1,0:T(8,128)S(1)}, f32[2,2,64,384]{3,2,1,0:T(8,128)S(1)}, u32[]{:S(2)}, u32[]{:S(2)}) collective-permute-start(f32[2,2,64,384]{3,2,1,0:T(8,128)S(1)} %get-tuple-element.36), channel_id=1, source_target_pairs={{0,1},{1,0},{2,3},{3,2},{4,5},{5,4},{6,7},{7,6},{8,9},{9,8},{10,11... | collective-permute-start | bytes 1179656 | tf_op jit(solution)/shard_map/ppermute | solution.py:29
  21.2 6.6 %collective-permute-start.7 = (f32[2,128,128]{2,1,0:T(8,128)S(1)}, f32[2,128,128]{2,1,0:T(8,128)S(1)}, u32[]{:S(2)}, u32[]{:S(2)}) collective-permute-start(f32[2,128,128]{2,1,0:T(8,128)S(1)} %add.26), channel_id=1, source_target_pairs={{0,4},{1,5},{2,6},{3,7},{4,0},{5,1},{6,2},{7,3},{8,12},{9,13},{10,... | collective-permute-start | bytes 393224 | tf_op jit(solution)/shard_map/ppermute | solution.py:322
  27.8 5.9 %collective-permute-start.8 = (f32[2,128,128]{2,1,0:T(8,128)S(1)}, f32[2,128,128]{2,1,0:T(8,128)S(1)}, u32[]{:S(2)}, u32[]{:S(2)}) collective-permute-start(f32[2,128,128]{2,1,0:T(8,128)S(1)} %add.29), channel_id=1, source_target_pairs={{0,8},{1,17},{2,10},{3,19},{4,12},{5,21},{6,14},{7,23},{8,0},{9,25... | collective-permute-start | bytes 393224 | tf_op jit(solution)/shard_map/ppermute | solution.py:322
  29.5 10.3 %collective-permute-start.6 = (f32[2,2,64,128]{3,2,1,0:T(8,128)S(1)}, f32[2,2,64,128]{3,2,1,0:T(8,128)S(1)}, u32[]{:S(2)}, u32[]{:S(2)}) collective-permute-start(f32[2,2,64,128]{3,2,1,0:T(8,128)S(1)} %slice.41), channel_id=1, source_target_pairs={{0,4},{4,8},{8,12},{12,16},{16,20},{20,24},{24,28},{1,5},{5,9},{9,... | collective-permute-start | bytes 393224 | tf_op jit(solution)/shard_map/ppermute | solution.py:25
  33.8 5.9 %collective-permute-start.9 = (f32[2,128,128]{2,1,0:T(8,128)S(1)}, f32[2,128,128]{2,1,0:T(8,128)S(1)}, u32[]{:S(2)}, u32[]{:S(2)}) collective-permute-start(f32[2,128,128]{2,1,0:T(8,128)S(1)} %add.30), channel_id=1, source_target_pairs={{0,16},{1,9},{2,18},{3,11},{4,20},{5,13},{6,22},{7,15},{8,24},{9,1... | collective-permute-start | bytes 393224 | tf_op jit(solution)/shard_map/ppermute | solution.py:322
  39.7 1.4 %collective-permute-start.10 = (f32[2,128,128]{2,1,0:T(8,128)S(1)}, f32[2,128,128]{2,1,0:T(8,128)S(1)}, u32[]{:S(2)}, u32[]{:S(2)}) collective-permute-start(f32[2,128,128]{2,1,0:T(8,128)S(1)} %add_multiply_fusion), channel_id=1, source_target_pairs={{0,1},{1,0},{2,3},{3,2},{4,5},{5,4},{6,7},{7,6},{8,9},{9,8},{10,11... | collective-permute-start | bytes 393224 | tf_op jit(solution)/shard_map/ppermute | solution.py:29
  39.9 1.3 %copy-start.7 = (f32[1,2,2,64,256]{4,3,2,1,0:T(8,128)}, f32[1,2,2,64,256]{4,3,2,1,0:T(8,128)S(1)}, u32[]{:S(2)}) copy-start(f32[1,2,2,64,256]{4,3,2,1,0:T(8,128)S(1)} %fusion.1) | copy-start | bytes 786436

commit v7 on v5

--- a/solution.py
+++ b/solution.py
@@ -60,26 +60,19 @@
 
 def transform(fields, on_left, on_right):
     extent = fields[0][0].shape[0]
-    stacked = jnp.concatenate(
-        [jnp.concatenate([f[part] for f in fields], 1) for part in range(2)], 0
-    )
-    left = product(on_left, split(stacked))
-    stacked = jnp.concatenate(
-        [
-            jnp.concatenate(
-                [left[part * extent : (part + 1) * extent, m * extent : (m + 1) * extent] for part in range(2)], 1
-            )
-            for m in range(len(fields))
-        ],
-        0,
-    )
-    out = product(split(stacked), on_right)
-    return [
-        tuple(
-            out[m * extent : (m + 1) * extent, part * extent : (part + 1) * extent] for part in range(2)
-        )
-        for m in range(len(fields))
-    ]
+    lefts = []
+    for k in range(0, len(fields), 2):
+        stacked = [jnp.concatenate([f[part] for f in fields[k : k + 2]], 1) for part in range(2)]
+        pair = split(jnp.concatenate(stacked, 0))
+        upper, lower = (tuple(t[at : at + extent] for t in on_left) for at in (0, extent))
+        lefts.append((product(upper, pair), product(lower, pair)))
+    outs = []
+    for left in lefts:
+        for at in range(0, left[0].shape[1], extent):
+            row = jnp.concatenate([half[:, at : at + extent] for half in left], 1)
+            out = product(split(row), on_right)
+            outs.append((out[:, :extent], out[:, extent:]))
+    return outs
 
 
 def times(a, b):
@@ -292,7 +285,7 @@
     rounds += [("tile", 1 << k) for k in range((tiles - 1).bit_length())]
     if paired:
         total = probe_keep + got
-        summed = kept + exchanged(given, "batch", 1)
+        summed = kept + exchanged(after(given, total), "batch", 1)
         landed = passed_along(summed[:, :, :, tile_side:], "tile", 1)
         object_share = summed[:, :, :, :tile_side].at[:, :, :, :extent].add(landed)
         beside = [(summed,)]
@@ -310,9 +303,10 @@
         beside = []
     if paired:
         nodes = range(tiles * shares)
+        orders = [rounds, rounds[:1] + rounds[:0:-1]]
         for k in range(len(rounds)):
-            even, odd = shares * rounds[k][1], shares * rounds[(0, 2, 1)[k]][1]
-            got = lax.ppermute(total, ("tile", "batch"), [(i, i ^ (odd if i % 2 else even)) for i in nodes])
+            bits = [shares * order[k][1] for order in orders]
+            got = lax.ppermute(total, ("tile", "batch"), [(i, i ^ bits[i % 2]) for i in nodes])
             total = total + (after(got, *beside[k]) if k < len(beside) else got)
     else:
         for axis, bit in rounds:

time: 43.4 us -> 41.3 us (0.952)
  Pallas kernels: 8.32 us -> 6.16 us
    pallas_call x3, Pallas kernels: 8.32 us -> 6.16 us  [kernel_call(): pl.pallas_call(kernel, out_shape=[jax.ShapeDtypeStruct(shape, dtype) for...]
    ppermute x3, waiting for transfers between devices: 8.06 us -> 8.55 us  [local(): lax.ppermute(total, ('tile', 'batch'), [(i, i ^ bits[i % 2]) for i in nod...]
  transfers between devices with their start and end apart: 11 -> 11, of which waited for: 8 -> 8; matrix products, arithmetic and copies ran while one was open for 1% -> 0% of each run, Pallas kernels for 4% -> 5%
where the time goes in v7:
time: 41.3 us; the launch traced here: 41.1 us
  waiting for transfers between devices  15.5 us (38%)
  starting transfers between devices  15.3 us (37%)
  Pallas kernels  6.16 us (15%)
  local copies, waits for them, and re-layouts  3.04 us (7%)
  between operations  0.83 us (2%)
    ppermute x3, waiting for transfers between devices, local(): lax.ppermute(total, ('tile', 'batch'), [(i, i ^ bits[i % 2]) for i in nod...  8.55 us
    ppermute x3, starting transfers between devices, local(): lax.ppermute(total, ('tile', 'batch'), [(i, i ^ bits[i % 2]) for i in nod...  6.21 us
    pallas_call x3, Pallas kernels, kernel_call(): pl.pallas_call(kernel, out_shape=[jax.ShapeDtypeStruct(shape, dtype) for...  6.16 us
    ppermute x2, starting transfers between devices, passed_along(): return lax.ppermute(block, axis, route)  4.95 us
    ppermute x6, waiting for transfers between devices, exchanged(): lax.ppermute(block, axis, [(i, i ^ bit) for i in range(lax.axis_size(axis...  4.51 us
    ppermute x6, starting transfers between devices, exchanged(): lax.ppermute(block, axis, [(i, i ^ bit) for i in range(lax.axis_size(axis...  4.11 us
    ppermute x2, waiting for transfers between devices, passed_along(): return lax.ppermute(block, axis, route)  2.46 us
    unnamed x17, local copies, waits for them, and re-layouts  1.98 us
  transfers between devices with their start and end apart: 11, of which 8 were waited for; matrix products, arithmetic and copies ran while one was open for 0% of the time, Pallas kernels for 5%

profile of v7, /device:TPU:0, one launch (start us, length us, event | category | flops | bytes accessed | tf_op | source)
XLA Modules:
  0.0 41.1 jit_solution(1634886725788191432)
XLA Ops:
  0.7 1.0 %dynamic-slice_bitcast_fusion = f32[2,2,128,128]{3,2,1,0:T(8,128)S(1)} fusion(f32[1,2,2,256,256]{4,3,2,1,0:T(8,128)} %param.8, s32[]{:T(128)S(6)} %select_n.15), kind=kLoop, calls=%fused_computation.2 | loop fusion | bytes 524292 | tf_op jit(solution)/shard_map/dynamic_slice | solution.py:266
  1.7 1.3 %collective-permute-start.2 = (f32[2,2,128,128]{3,2,1,0:T(8,128)S(1)}, f32[2,2,128,128]{3,2,1,0:T(8,128)S(1)}, u32[]{:S(2)}, u32[]{:S(2)}) collective-permute-start(f32[2,2,128,128]{3,2,1,0:T(8,128)S(1)} %dynamic-slice_bitcast_fusion), channel_id=1, source_target_pairs={{4,0},{8,4},{12,8},{16,12},{20,16},{24,20},{28,24},{5,1},{9,5},{13... | collective-permute-start | bytes 786440 | tf_op jit(solution)/shard_map/ppermute | solution.py:25
  3.0 3.0 %collective-permute-start.1 = (f32[128,128]{1,0:T(8,128)S(1)}, f32[128,128]{1,0:T(8,128)S(1)}, u32[]{:S(2)}, u32[]{:S(2)}) collective-permute-start(f32[128,128]{1,0:T(8,128)S(1)} %bitcast.20), channel_id=1, source_target_pairs={{0,2},{1,3},{2,0},{3,1},{4,6},{5,7},{6,4},{7,5},{8,10},{9,11},{10,... | collective-permute-start | bytes 196616 | tf_op jit(solution)/shard_map/ppermute | solution.py:29
  6.1 0.6 %collective-permute-start = (s32[2]{0:T(128)S(1)}, s32[2]{0:T(128)S(1)}, u32[]{:S(2)}, u32[]{:S(2)}) collective-permute-start(s32[2]{0:T(128)S(1)} %bitcast.22), channel_id=1, source_target_pairs={{0,2},{1,3},{2,0},{3,1},{4,6},{5,7},{6,4},{7,5},{8,10},{9,11},{10,... | collective-permute-start | bytes 32 | tf_op jit(solution)/shard_map/ppermute | solution.py:29
  6.7 1.2 %copy-done = f32[1,2,2,256,256]{4,3,2,1,0:T(8,128)S(1)} copy-done((f32[1,2,2,256,256]{4,3,2,1,0:T(8,128)S(1)}, f32[1,2,2,256,256]{4,3,2,1,0:T(8,128)}, u32[]{:S(2)}) %copy-start) | copy-done | bytes 1048600
  7.9 1.2 %own_windows.1 = (f32[2,2,128,128]{3,2,1,0:T(8,128)S(1)}, f32[2,128,128]{2,1,0:T(8,128)S(1)}, f32[2,2,128,128]{3,2,1,0:T(8,128)S(1)}, bf16[2,2,128,128]{3,2,1,0:T(8,128)(2,1)S(1)}) custom-call(s32[2]{0:T(128)S(1)} %bitcast.23, f32[2,2,256,256]{3,2,1,0:T(8,128)S(1)} %bitcast.18, f32[128,128]{1,0:T(8,128)S(1)} %copy-done.4, f32[2,2,128,128]{3,2,1,0:T(8,128)S(1)} %copy-done.2, ...), custom_call_target="tpu_custom_call" | custom-call | bytes 1507328 | tf_op jit(solution)/shard_map/own_windows/pallas_call | solution.py:224
  9.1 0.6 %collective-permute-done.offset_ref.refs_1_ = s32[2]{0:T(128)S(1)} collective-permute-done((s32[2]{0:T(128)S(1)}, s32[2]{0:T(128)S(1)}, u32[]{:S(2)}, u32[]{:S(2)}) %collective-permute-start) | collective-permute-done | bytes 40 | tf_op jit(solution)/shard_map/ppermute | solution.py:29
  9.6 0.8 %partner_windows.1.refs_4_ = f32[2,2,128,128]{3,2,1,0:T(8,128)S(1)} custom-call(s32[2]{0:T(128)S(1)} %collective-permute-done.offset_ref.refs_1_, f32[2,2,256,256]{3,2,1,0:T(8,128)S(1)} %bitcast.19), custom_call_target="tpu_custom_call" | custom-call | bytes 1048576 | tf_op jit(solution)/shard_map/partner_windows/pallas_call | solution.py:224
  10.4 2.5 %collective-permute-done.2.refs_10_ = f32[2,2,128,128]{3,2,1,0:T(8,128)S(1)} collective-permute-done((f32[2,2,128,128]{3,2,1,0:T(8,128)S(1)}, f32[2,2,128,128]{3,2,1,0:T(8,128)S(1)}, u32[]{:S(2)}, u32[]{:S(2)}) %collective-permute-start.2) | collective-permute-done | bytes 262176 | tf_op jit(solution)/shard_map/ppermute | solution.py:25
  12.9 0.1 pad_add_fusion.refs_2_
  12.9 1.5 %collective-permute-done.3.refs_11_ = f32[2,2,128,128]{3,2,1,0:T(8,128)S(1)} collective-permute-done((f32[2,2,128,128]{3,2,1,0:T(8,128)S(1)}, f32[2,2,128,128]{3,2,1,0:T(8,128)S(1)}, u32[]{:S(2)}, u32[]{:S(2)}) %collective-permute-start.3) | collective-permute-done | bytes 262176 | tf_op jit(solution)/shard_map/ppermute | solution.py:29
  14.4 4.2 %wave_gradients.1 = (f32[2,2,64,384]{3,2,1,0:T(8,128)S(1)}, f32[2,2,64,384]{3,2,1,0:T(8,128)S(1)}, f32[2,128,128]{2,1,0:T(8,128)S(1)}, f32[2,128,128]{2,1,0:T(8,128)S(1)}) custom-call(s32[2]{0:T(128)S(1)} %bitcast.24, s32[2]{0:T(128)S(1)} %collective-permute-done.offset_ref.refs_1_, s32[2]{0:T(128)S(1)} %pad_add_fusion.refs_2_, ...), custom_call_target="tpu_custom_call" | custom-call | bytes 1703936 | tf_op jit(solution)/shard_map/wave_gradients/pallas_call | solution.py:224
  18.6 0.2 collective-permute-start.4
  18.8 1.2 %collective-permute-done.4 = f32[2,128,128]{2,1,0:T(8,128)S(1)} collective-permute-done((f32[2,128,128]{2,1,0:T(8,128)S(1)}, f32[2,128,128]{2,1,0:T(8,128)S(1)}, u32[]{:S(2)}, u32[]{:S(2)}) %collective-permute-start.4) | collective-permute-done | bytes 131104 | tf_op jit(solution)/shard_map/ppermute | solution.py:29
  20.1 0.2 collective-permute-start.5
  20.3 2.6 %collective-permute-start.7 = (f32[2,128,128]{2,1,0:T(8,128)S(1)}, f32[2,128,128]{2,1,0:T(8,128)S(1)}, u32[]{:S(2)}, u32[]{:S(2)}) collective-permute-start(f32[2,128,128]{2,1,0:T(8,128)S(1)} %add.26), channel_id=1, source_target_pairs={{0,4},{1,5},{2,6},{3,7},{4,0},{5,1},{6,2},{7,3},{8,12},{9,13},{10,... | collective-permute-start | bytes 393224 | tf_op jit(solution)/shard_map/ppermute | solution.py:309
  23.0 3.9 %collective-permute-done.7 = f32[2,128,128]{2,1,0:T(8,128)S(1)} collective-permute-done((f32[2,128,128]{2,1,0:T(8,128)S(1)}, f32[2,128,128]{2,1,0:T(8,128)S(1)}, u32[]{:S(2)}, u32[]{:S(2)}) %collective-permute-start.7) | collective-permute-done | bytes 131104 | tf_op jit(solution)/shard_map/ppermute | solution.py:309
  26.9 1.7 %collective-permute-start.8 = (f32[2,128,128]{2,1,0:T(8,128)S(1)}, f32[2,128,128]{2,1,0:T(8,128)S(1)}, u32[]{:S(2)}, u32[]{:S(2)}) collective-permute-start(f32[2,128,128]{2,1,0:T(8,128)S(1)} %add.29), channel_id=1, source_target_pairs={{0,8},{1,17},{2,10},{3,19},{4,12},{5,21},{6,14},{7,23},{8,0},{9,25... | collective-permute-start | bytes 393224 | tf_op jit(solution)/shard_map/ppermute | solution.py:309
  28.6 3.7 %collective-permute-start.6 = (f32[2,2,64,128]{3,2,1,0:T(8,128)S(1)}, f32[2,2,64,128]{3,2,1,0:T(8,128)S(1)}, u32[]{:S(2)}, u32[]{:S(2)}) collective-permute-start(f32[2,2,64,128]{3,2,1,0:T(8,128)S(1)} %slice.41), channel_id=1, source_target_pairs={{0,4},{4,8},{8,12},{12,16},{16,20},{20,24},{24,28},{1,5},{5,9},{9,... | collective-permute-start | bytes 393224 | tf_op jit(solution)/shard_map/ppermute | solution.py:25
  32.3 0.6 %collective-permute-done.8 = f32[2,128,128]{2,1,0:T(8,128)S(1)} collective-permute-done((f32[2,128,128]{2,1,0:T(8,128)S(1)}, f32[2,128,128]{2,1,0:T(8,128)S(1)}, u32[]{:S(2)}, u32[]{:S(2)}) %collective-permute-start.8) | collective-permute-done | bytes 131104 | tf_op jit(solution)/shard_map/ppermute | solution.py:309
  32.9 1.9 %collective-permute-start.9 = (f32[2,128,128]{2,1,0:T(8,128)S(1)}, f32[2,128,128]{2,1,0:T(8,128)S(1)}, u32[]{:S(2)}, u32[]{:S(2)}) collective-permute-start(f32[2,128,128]{2,1,0:T(8,128)S(1)} %add.30), channel_id=1, source_target_pairs={{0,16},{1,9},{2,18},{3,11},{4,20},{5,13},{6,22},{7,15},{8,24},{9,1... | collective-permute-start | bytes 393224 | tf_op jit(solution)/shard_map/ppermute | solution.py:309
  34.8 4.0 %collective-permute-done.9 = f32[2,128,128]{2,1,0:T(8,128)S(1)} collective-permute-done((f32[2,128,128]{2,1,0:T(8,128)S(1)}, f32[2,128,128]{2,1,0:T(8,128)S(1)}, u32[]{:S(2)}, u32[]{:S(2)}) %collective-permute-start.9) | collective-permute-done | bytes 131104 | tf_op jit(solution)/shard_map/ppermute | solution.py:309
  39.0 1.3 %collective-permute-done.10 = f32[2,128,128]{2,1,0:T(8,128)S(1)} collective-permute-done((f32[2,128,128]{2,1,0:T(8,128)S(1)}, f32[2,128,128]{2,1,0:T(8,128)S(1)}, u32[]{:S(2)}, u32[]{:S(2)}) %collective-permute-start.10) | collective-permute-done | bytes 131104 | tf_op jit(solution)/shard_map/ppermute | solution.py:29
  40.3 0.7 %copy.8 = f32[2,2,128,128]{3,2,1,0:T(8,128)} copy(f32[2,2,128,128]{3,2,0,1:T(8,128)S(1)} %pad_maximum_fusion) | data formatting | bytes 524288
  (30 shorter events, 0.3 us)
Async XLA Ops:
  0.6 2.4 %copy-start.5 = (f32[1,1,128,128]{3,2,1,0:T(8,128)S(1)}, f32[1,1,128,128]{3,2,1,0:T(8,128)}, u32[]{:S(2)}) copy-start(f32[1,1,128,128]{3,2,1,0:T(8,128)} %param.12) | copy-start | bytes 196612
  0.6 6.0 %copy-start.2 = (f32[2,2,128,128]{3,2,1,0:T(8,128)S(1)}, f32[2,2,128,128]{3,2,1,0:T(8,128)}, u32[]{:S(2)}) copy-start(f32[2,2,128,128]{3,2,1,0:T(8,128)} %probe_in_ref.1) | copy-start | bytes 786436
  0.7 6.0 %copy-start.3 = (bf16[2,2,128,128]{3,2,1,0:T(8,128)(2,1)S(1)}, bf16[2,2,128,128]{3,2,1,0:T(8,128)(2,1)}, u32[]{:S(2)}) copy-start(bf16[2,2,128,128]{3,2,1,0:T(8,128)(2,1)} %constant.48.clone.table_in_ref) | copy-start | bytes 393220
  0.7 6.0 %copy-start.4 = (f32[128,128]{1,0:T(8,128)S(1)}, f32[128,128]{1,0:T(8,128)}, u32[]{:S(2)}) copy-start(f32[128,128]{1,0:T(8,128)} %phase_ref.1) | copy-start | bytes 196612
  1.7 11.1 %collective-permute-start.2 = (f32[2,2,128,128]{3,2,1,0:T(8,128)S(1)}, f32[2,2,128,128]{3,2,1,0:T(8,128)S(1)}, u32[]{:S(2)}, u32[]{:S(2)}) collective-permute-start(f32[2,2,128,128]{3,2,1,0:T(8,128)S(1)} %dynamic-slice_bitcast_fusion), channel_id=1, source_target_pairs={{4,0},{8,4},{12,8},{16,12},{20,16},{24,20},{28,24},{5,1},{9,5},{13... | collective-permute-start | bytes 786440 | tf_op jit(solution)/shard_map/ppermute | solution.py:25
  3.0 3.0 %copy-start.6 = (s32[1,1,2]{2,1,0:T(1,128)S(1)}, s32[1,1,2]{2,1,0:T(1,128)}, u32[]{:S(2)}) copy-start(s32[1,1,2]{2,1,0:T(1,128)} %param.11) | copy-start | bytes 28
  3.0 7.4 %collective-permute-start.1 = (f32[128,128]{1,0:T(8,128)S(1)}, f32[128,128]{1,0:T(8,128)S(1)}, u32[]{:S(2)}, u32[]{:S(2)}) collective-permute-start(f32[128,128]{1,0:T(8,128)S(1)} %bitcast.20), channel_id=1, source_target_pairs={{0,2},{1,3},{2,0},{3,1},{4,6},{5,7},{6,4},{7,5},{8,10},{9,11},{10,... | collective-permute-start | bytes 196616 | tf_op jit(solution)/shard_map/ppermute | solution.py:29
  6.1 3.5 %collective-permute-start = (s32[2]{0:T(128)S(1)}, s32[2]{0:T(128)S(1)}, u32[]{:S(2)}, u32[]{:S(2)}) collective-permute-start(s32[2]{0:T(128)S(1)} %bitcast.22), channel_id=1, source_target_pairs={{0,2},{1,3},{2,0},{3,1},{4,6},{5,7},{6,4},{7,5},{8,10},{9,11},{10,... | collective-permute-start | bytes 32 | tf_op jit(solution)/shard_map/ppermute | solution.py:29
  6.7 1.2 %copy-start = (f32[1,2,2,256,256]{4,3,2,1,0:T(8,128)S(1)}, f32[1,2,2,256,256]{4,3,2,1,0:T(8,128)}, u32[]{:S(2)}) copy-start(f32[1,2,2,256,256]{4,3,2,1,0:T(8,128)} %param.8) | copy-start | bytes 3145732
  7.9 1.7 %copy-start.1 = (f32[1,2,2,256,256]{4,3,2,1,0:T(8,128)S(1)}, f32[1,2,2,256,256]{4,3,2,1,0:T(8,128)}, u32[]{:S(2)}) copy-start(f32[1,2,2,256,256]{4,3,2,1,0:T(8,128)} %param.8) | copy-start | bytes 3145732
  12.9 1.5 %collective-permute-start.3 = (f32[2,2,128,128]{3,2,1,0:T(8,128)S(1)}, f32[2,2,128,128]{3,2,1,0:T(8,128)S(1)}, u32[]{:S(2)}, u32[]{:S(2)}) collective-permute-start(f32[2,2,128,128]{3,2,1,0:T(8,128)S(1)} %collective-permute-done.2.refs_10_), channel_id=1, source_target_pairs={{0,1},{1,0},{2,3},{3,2},{4,5},{5,4},{6,7},{7,6},{8,9},{9,8},{10,11... | collective-permute-start | bytes 786440 | tf_op jit(solution)/shard_map/ppermute | solution.py:29
  18.6 1.4 %collective-permute-start.4 = (f32[2,128,128]{2,1,0:T(8,128)S(1)}, f32[2,128,128]{2,1,0:T(8,128)S(1)}, u32[]{:S(2)}, u32[]{:S(2)}) collective-permute-start(f32[2,128,128]{2,1,0:T(8,128)S(1)} %get-tuple-element.35), channel_id=1, source_target_pairs={{0,1},{1,0},{2,3},{3,2},{4,5},{5,4},{6,7},{7,6},{8,9},{9,8},{10,11... | collective-permute-start | bytes 393224 | tf_op jit(solution)/shard_map/ppermute | solution.py:29
  20.1 2.9 %collective-permute-start.5 = (f32[2,2,64,384]{3,2,1,0:T(8,128)S(1)}, f32[2,2,64,384]{3,2,1,0:T(8,128)S(1)}, u32[]{:S(2)}, u32[]{:S(2)}) collective-permute-start(f32[2,2,64,384]{3,2,1,0:T(8,128)S(1)} %get-tuple-element.36), channel_id=1, source_target_pairs={{0,1},{1,0},{2,3},{3,2},{4,5},{5,4},{6,7},{7,6},{8,9},{9,8},{10,11... | collective-permute-start | bytes 1179656 | tf_op jit(solution)/shard_map/ppermute | solution.py:29
  20.3 6.7 %collective-permute-start.7 = (f32[2,128,128]{2,1,0:T(8,128)S(1)}, f32[2,128,128]{2,1,0:T(8,128)S(1)}, u32[]{:S(2)}, u32[]{:S(2)}) collective-permute-start(f32[2,128,128]{2,1,0:T(8,128)S(1)} %add.26), channel_id=1, source_target_pairs={{0,4},{1,5},{2,6},{3,7},{4,0},{5,1},{6,2},{7,3},{8,12},{9,13},{10,... | collective-permute-start | bytes 393224 | tf_op jit(solution)/shard_map/ppermute | solution.py:309
  26.9 5.9 %collective-permute-start.8 = (f32[2,128,128]{2,1,0:T(8,128)S(1)}, f32[2,128,128]{2,1,0:T(8,128)S(1)}, u32[]{:S(2)}, u32[]{:S(2)}) collective-permute-start(f32[2,128,128]{2,1,0:T(8,128)S(1)} %add.29), channel_id=1, source_target_pairs={{0,8},{1,17},{2,10},{3,19},{4,12},{5,21},{6,14},{7,23},{8,0},{9,25... | collective-permute-start | bytes 393224 | tf_op jit(solution)/shard_map/ppermute | solution.py:309
  28.6 10.3 %collective-permute-start.6 = (f32[2,2,64,128]{3,2,1,0:T(8,128)S(1)}, f32[2,2,64,128]{3,2,1,0:T(8,128)S(1)}, u32[]{:S(2)}, u32[]{:S(2)}) collective-permute-start(f32[2,2,64,128]{3,2,1,0:T(8,128)S(1)} %slice.41), channel_id=1, source_target_pairs={{0,4},{4,8},{8,12},{12,16},{16,20},{20,24},{24,28},{1,5},{5,9},{9,... | collective-permute-start | bytes 393224 | tf_op jit(solution)/shard_map/ppermute | solution.py:25
  32.9 5.9 %collective-permute-start.9 = (f32[2,128,128]{2,1,0:T(8,128)S(1)}, f32[2,128,128]{2,1,0:T(8,128)S(1)}, u32[]{:S(2)}, u32[]{:S(2)}) collective-permute-start(f32[2,128,128]{2,1,0:T(8,128)S(1)} %add.30), channel_id=1, source_target_pairs={{0,16},{1,9},{2,18},{3,11},{4,20},{5,13},{6,22},{7,15},{8,24},{9,1... | collective-permute-start | bytes 393224 | tf_op jit(solution)/shard_map/ppermute | solution.py:309
  38.9 1.4 %collective-permute-start.10 = (f32[2,128,128]{2,1,0:T(8,128)S(1)}, f32[2,128,128]{2,1,0:T(8,128)S(1)}, u32[]{:S(2)}, u32[]{:S(2)}) collective-permute-start(f32[2,128,128]{2,1,0:T(8,128)S(1)} %add_multiply_fusion), channel_id=1, source_target_pairs={{0,1},{1,0},{2,3},{3,2},{4,5},{5,4},{6,7},{7,6},{8,9},{9,8},{10,11... | collective-permute-start | bytes 393224 | tf_op jit(solution)/shard_map/ppermute | solution.py:29
  39.0 1.3 %copy-start.7 = (f32[1,2,2,64,256]{4,3,2,1,0:T(8,128)}, f32[1,2,2,64,256]{4,3,2,1,0:T(8,128)S(1)}, u32[]{:S(2)}) copy-start(f32[1,2,2,64,256]{4,3,2,1,0:T(8,128)S(1)} %fusion.1) | copy-start | bytes 786436

commit v8 on v7

--- a/solution.py
+++ b/solution.py
@@ -303,7 +303,7 @@
         beside = []
     if paired:
         nodes = range(tiles * shares)
-        orders = [rounds, rounds[:1] + rounds[:0:-1]]
+        orders = [rounds[-1:] + rounds[:-1], rounds]
         for k in range(len(rounds)):
             bits = [shares * order[k][1] for order in orders]
             got = lax.ppermute(total, ("tile", "batch"), [(i, i ^ bits[i % 2]) for i in nodes])

time: 41.3 us -> 40.8 us (0.988)
  starting transfers between devices: 15.3 us -> 14.6 us
    ppermute x2, starting transfers between devices: 4.95 us -> 3.23 us  [passed_along(): return lax.ppermute(block, axis, route)]
    ppermute x3, starting transfers between devices: 6.21 us -> 7.29 us  [local(): lax.ppermute(total, ('tile', 'batch'), [(i, i ^ bits[i % 2]) for i in nod...]
where the time goes in v8:
time: 40.8 us; the launch traced here: 40.6 us
  waiting for transfers between devices  15.7 us (38%)
  starting transfers between devices  14.6 us (36%)
  Pallas kernels  6.16 us (15%)
  local copies, waits for them, and re-layouts  3.04 us (7%)
  between operations  0.83 us (2%)
    ppermute x3, waiting for transfers between devices, local(): lax.ppermute(total, ('tile', 'batch'), [(i, i ^ bits[i % 2]) for i in nod...  8.73 us
    ppermute x3, starting transfers between devices, local(): lax.ppermute(total, ('tile', 'batch'), [(i, i ^ bits[i % 2]) for i in nod...  7.29 us
    pallas_call x3, Pallas kernels, kernel_call(): pl.pallas_call(kernel, out_shape=[jax.ShapeDtypeStruct(shape, dtype) for...  6.16 us
    ppermute x6, waiting for transfers between devices, exchanged(): lax.ppermute(block, axis, [(i, i ^ bit) for i in range(lax.axis_size(axis...  4.53 us
    ppermute x6, starting transfers between devices, exchanged(): lax.ppermute(block, axis, [(i, i ^ bit) for i in range(lax.axis_size(axis...  4.09 us
    ppermute x2, starting transfers between devices, passed_along(): return lax.ppermute(block, axis, route)  3.23 us
    ppermute x2, waiting for transfers between devices, passed_along(): return lax.ppermute(block, axis, route)  2.46 us
    unnamed x17, local copies, waits for them, and re-layouts  1.98 us
  transfers between devices with their start and end apart: 11, of which 8 were waited for; matrix products, arithmetic and copies ran while one was open for 0% of the time, Pallas kernels for 5%

profile of v8, /device:TPU:0, one launch (start us, length us, event | category | flops | bytes accessed | tf_op | source)
XLA Modules:
  0.0 40.6 jit_solution(15566773415161715095)
XLA Ops:
  0.7 1.0 %dynamic-slice_bitcast_fusion = f32[2,2,128,128]{3,2,1,0:T(8,128)S(1)} fusion(f32[1,2,2,256,256]{4,3,2,1,0:T(8,128)} %param.8, s32[]{:T(128)S(6)} %select_n.15), kind=kLoop, calls=%fused_computation.2 | loop fusion | bytes 524292 | tf_op jit(solution)/shard_map/dynamic_slice | solution.py:266
  1.7 1.3 %collective-permute-start.2 = (f32[2,2,128,128]{3,2,1,0:T(8,128)S(1)}, f32[2,2,128,128]{3,2,1,0:T(8,128)S(1)}, u32[]{:S(2)}, u32[]{:S(2)}) collective-permute-start(f32[2,2,128,128]{3,2,1,0:T(8,128)S(1)} %dynamic-slice_bitcast_fusion), channel_id=1, source_target_pairs={{4,0},{8,4},{12,8},{16,12},{20,16},{24,20},{28,24},{5,1},{9,5},{13... | collective-permute-start | bytes 786440 | tf_op jit(solution)/shard_map/ppermute | solution.py:25
  3.0 3.0 %collective-permute-start.1 = (f32[128,128]{1,0:T(8,128)S(1)}, f32[128,128]{1,0:T(8,128)S(1)}, u32[]{:S(2)}, u32[]{:S(2)}) collective-permute-start(f32[128,128]{1,0:T(8,128)S(1)} %bitcast.20), channel_id=1, source_target_pairs={{0,2},{1,3},{2,0},{3,1},{4,6},{5,7},{6,4},{7,5},{8,10},{9,11},{10,... | collective-permute-start | bytes 196616 | tf_op jit(solution)/shard_map/ppermute | solution.py:29
  6.1 0.6 %collective-permute-start = (s32[2]{0:T(128)S(1)}, s32[2]{0:T(128)S(1)}, u32[]{:S(2)}, u32[]{:S(2)}) collective-permute-start(s32[2]{0:T(128)S(1)} %bitcast.22), channel_id=1, source_target_pairs={{0,2},{1,3},{2,0},{3,1},{4,6},{5,7},{6,4},{7,5},{8,10},{9,11},{10,... | collective-permute-start | bytes 32 | tf_op jit(solution)/shard_map/ppermute | solution.py:29
  6.7 1.2 %copy-done = f32[1,2,2,256,256]{4,3,2,1,0:T(8,128)S(1)} copy-done((f32[1,2,2,256,256]{4,3,2,1,0:T(8,128)S(1)}, f32[1,2,2,256,256]{4,3,2,1,0:T(8,128)}, u32[]{:S(2)}) %copy-start) | copy-done | bytes 1048600
  7.9 1.2 %own_windows.1 = (f32[2,2,128,128]{3,2,1,0:T(8,128)S(1)}, f32[2,128,128]{2,1,0:T(8,128)S(1)}, f32[2,2,128,128]{3,2,1,0:T(8,128)S(1)}, bf16[2,2,128,128]{3,2,1,0:T(8,128)(2,1)S(1)}) custom-call(s32[2]{0:T(128)S(1)} %bitcast.23, f32[2,2,256,256]{3,2,1,0:T(8,128)S(1)} %bitcast.18, f32[128,128]{1,0:T(8,128)S(1)} %copy-done.4, f32[2,2,128,128]{3,2,1,0:T(8,128)S(1)} %copy-done.2, ...), custom_call_target="tpu_custom_call" | custom-call | bytes 1507328 | tf_op jit(solution)/shard_map/own_windows/pallas_call | solution.py:224
  9.1 0.6 %collective-permute-done.offset_ref.refs_1_ = s32[2]{0:T(128)S(1)} collective-permute-done((s32[2]{0:T(128)S(1)}, s32[2]{0:T(128)S(1)}, u32[]{:S(2)}, u32[]{:S(2)}) %collective-permute-start) | collective-permute-done | bytes 40 | tf_op jit(solution)/shard_map/ppermute | solution.py:29
  9.6 0.8 %partner_windows.1.refs_4_ = f32[2,2,128,128]{3,2,1,0:T(8,128)S(1)} custom-call(s32[2]{0:T(128)S(1)} %collective-permute-done.offset_ref.refs_1_, f32[2,2,256,256]{3,2,1,0:T(8,128)S(1)} %bitcast.19), custom_call_target="tpu_custom_call" | custom-call | bytes 1048576 | tf_op jit(solution)/shard_map/partner_windows/pallas_call | solution.py:224
  10.4 2.5 %collective-permute-done.2.refs_10_ = f32[2,2,128,128]{3,2,1,0:T(8,128)S(1)} collective-permute-done((f32[2,2,128,128]{3,2,1,0:T(8,128)S(1)}, f32[2,2,128,128]{3,2,1,0:T(8,128)S(1)}, u32[]{:S(2)}, u32[]{:S(2)}) %collective-permute-start.2) | collective-permute-done | bytes 262176 | tf_op jit(solution)/shard_map/ppermute | solution.py:25
  12.9 0.1 pad_add_fusion.refs_2_
  12.9 1.5 %collective-permute-done.3.refs_11_ = f32[2,2,128,128]{3,2,1,0:T(8,128)S(1)} collective-permute-done((f32[2,2,128,128]{3,2,1,0:T(8,128)S(1)}, f32[2,2,128,128]{3,2,1,0:T(8,128)S(1)}, u32[]{:S(2)}, u32[]{:S(2)}) %collective-permute-start.3) | collective-permute-done | bytes 262176 | tf_op jit(solution)/shard_map/ppermute | solution.py:29
  14.4 4.2 %wave_gradients.1 = (f32[2,2,64,384]{3,2,1,0:T(8,128)S(1)}, f32[2,2,64,384]{3,2,1,0:T(8,128)S(1)}, f32[2,128,128]{2,1,0:T(8,128)S(1)}, f32[2,128,128]{2,1,0:T(8,128)S(1)}) custom-call(s32[2]{0:T(128)S(1)} %bitcast.24, s32[2]{0:T(128)S(1)} %collective-permute-done.offset_ref.refs_1_, s32[2]{0:T(128)S(1)} %pad_add_fusion.refs_2_, ...), custom_call_target="tpu_custom_call" | custom-call | bytes 1703936 | tf_op jit(solution)/shard_map/wave_gradients/pallas_call | solution.py:224
  18.6 0.2 collective-permute-start.4
  18.8 1.2 %collective-permute-done.4 = f32[2,128,128]{2,1,0:T(8,128)S(1)} collective-permute-done((f32[2,128,128]{2,1,0:T(8,128)S(1)}, f32[2,128,128]{2,1,0:T(8,128)S(1)}, u32[]{:S(2)}, u32[]{:S(2)}) %collective-permute-start.4) | collective-permute-done | bytes 131104 | tf_op jit(solution)/shard_map/ppermute | solution.py:29
  20.1 0.2 collective-permute-start.5
  20.3 2.8 %collective-permute-start.7 = (f32[2,128,128]{2,1,0:T(8,128)S(1)}, f32[2,128,128]{2,1,0:T(8,128)S(1)}, u32[]{:S(2)}, u32[]{:S(2)}) collective-permute-start(f32[2,128,128]{2,1,0:T(8,128)S(1)} %add.26), channel_id=1, source_target_pairs={{0,16},{1,5},{2,18},{3,7},{4,20},{5,1},{6,22},{7,3},{8,24},{9,13},... | collective-permute-start | bytes 393224 | tf_op jit(solution)/shard_map/ppermute | solution.py:309
  23.2 4.4 %collective-permute-done.7 = f32[2,128,128]{2,1,0:T(8,128)S(1)} collective-permute-done((f32[2,128,128]{2,1,0:T(8,128)S(1)}, f32[2,128,128]{2,1,0:T(8,128)S(1)}, u32[]{:S(2)}, u32[]{:S(2)}) %collective-permute-start.7) | collective-permute-done | bytes 131104 | tf_op jit(solution)/shard_map/ppermute | solution.py:309
  27.6 2.8 %collective-permute-start.8 = (f32[2,128,128]{2,1,0:T(8,128)S(1)}, f32[2,128,128]{2,1,0:T(8,128)S(1)}, u32[]{:S(2)}, u32[]{:S(2)}) collective-permute-start(f32[2,128,128]{2,1,0:T(8,128)S(1)} %add.29), channel_id=1, source_target_pairs={{0,4},{1,9},{2,6},{3,11},{4,0},{5,13},{6,2},{7,15},{8,12},{9,1},{1... | collective-permute-start | bytes 393224 | tf_op jit(solution)/shard_map/ppermute | solution.py:309
  30.4 1.9 %collective-permute-start.6 = (f32[2,2,64,128]{3,2,1,0:T(8,128)S(1)}, f32[2,2,64,128]{3,2,1,0:T(8,128)S(1)}, u32[]{:S(2)}, u32[]{:S(2)}) collective-permute-start(f32[2,2,64,128]{3,2,1,0:T(8,128)S(1)} %slice.41), channel_id=1, source_target_pairs={{0,4},{4,8},{8,12},{12,16},{16,20},{20,24},{24,28},{1,5},{5,9},{9,... | collective-permute-start | bytes 393224 | tf_op jit(solution)/shard_map/ppermute | solution.py:25
  32.3 1.0 %collective-permute-done.8 = f32[2,128,128]{2,1,0:T(8,128)S(1)} collective-permute-done((f32[2,128,128]{2,1,0:T(8,128)S(1)}, f32[2,128,128]{2,1,0:T(8,128)S(1)}, u32[]{:S(2)}, u32[]{:S(2)}) %collective-permute-start.8) | collective-permute-done | bytes 131104 | tf_op jit(solution)/shard_map/ppermute | solution.py:309
  33.3 1.7 %collective-permute-start.9 = (f32[2,128,128]{2,1,0:T(8,128)S(1)}, f32[2,128,128]{2,1,0:T(8,128)S(1)}, u32[]{:S(2)}, u32[]{:S(2)}) collective-permute-start(f32[2,128,128]{2,1,0:T(8,128)S(1)} %add.30), channel_id=1, source_target_pairs={{0,8},{1,17},{2,10},{3,19},{4,12},{5,21},{6,14},{7,23},{8,0},{9,25... | collective-permute-start | bytes 393224 | tf_op jit(solution)/shard_map/ppermute | solution.py:309
  35.0 3.3 %collective-permute-done.9 = f32[2,128,128]{2,1,0:T(8,128)S(1)} collective-permute-done((f32[2,128,128]{2,1,0:T(8,128)S(1)}, f32[2,128,128]{2,1,0:T(8,128)S(1)}, u32[]{:S(2)}, u32[]{:S(2)}) %collective-permute-start.9) | collective-permute-done | bytes 131104 | tf_op jit(solution)/shard_map/ppermute | solution.py:309
  38.5 1.3 %collective-permute-done.10 = f32[2,128,128]{2,1,0:T(8,128)S(1)} collective-permute-done((f32[2,128,128]{2,1,0:T(8,128)S(1)}, f32[2,128,128]{2,1,0:T(8,128)S(1)}, u32[]{:S(2)}, u32[]{:S(2)}) %collective-permute-start.10) | collective-permute-done | bytes 131104 | tf_op jit(solution)/shard_map/ppermute | solution.py:29
  39.9 0.7 %copy.8 = f32[2,2,128,128]{3,2,1,0:T(8,128)} copy(f32[2,2,128,128]{3,2,0,1:T(8,128)S(1)} %pad_maximum_fusion) | data formatting | bytes 524288
  (30 shorter events, 0.3 us)
Async XLA Ops:
  0.6 2.4 %copy-start.5 = (f32[1,1,128,128]{3,2,1,0:T(8,128)S(1)}, f32[1,1,128,128]{3,2,1,0:T(8,128)}, u32[]{:S(2)}) copy-start(f32[1,1,128,128]{3,2,1,0:T(8,128)} %param.12) | copy-start | bytes 196612
  0.6 6.0 %copy-start.2 = (f32[2,2,128,128]{3,2,1,0:T(8,128)S(1)}, f32[2,2,128,128]{3,2,1,0:T(8,128)}, u32[]{:S(2)}) copy-start(f32[2,2,128,128]{3,2,1,0:T(8,128)} %probe_in_ref.1) | copy-start | bytes 786436
  0.7 6.0 %copy-start.3 = (bf16[2,2,128,128]{3,2,1,0:T(8,128)(2,1)S(1)}, bf16[2,2,128,128]{3,2,1,0:T(8,128)(2,1)}, u32[]{:S(2)}) copy-start(bf16[2,2,128,128]{3,2,1,0:T(8,128)(2,1)} %constant.48.clone.table_in_ref) | copy-start | bytes 393220
  0.7 6.0 %copy-start.4 = (f32[128,128]{1,0:T(8,128)S(1)}, f32[128,128]{1,0:T(8,128)}, u32[]{:S(2)}) copy-start(f32[128,128]{1,0:T(8,128)} %phase_ref.1) | copy-start | bytes 196612
  1.7 11.1 %collective-permute-start.2 = (f32[2,2,128,128]{3,2,1,0:T(8,128)S(1)}, f32[2,2,128,128]{3,2,1,0:T(8,128)S(1)}, u32[]{:S(2)}, u32[]{:S(2)}) collective-permute-start(f32[2,2,128,128]{3,2,1,0:T(8,128)S(1)} %dynamic-slice_bitcast_fusion), channel_id=1, source_target_pairs={{4,0},{8,4},{12,8},{16,12},{20,16},{24,20},{28,24},{5,1},{9,5},{13... | collective-permute-start | bytes 786440 | tf_op jit(solution)/shard_map/ppermute | solution.py:25
  3.0 3.0 %copy-start.6 = (s32[1,1,2]{2,1,0:T(1,128)S(1)}, s32[1,1,2]{2,1,0:T(1,128)}, u32[]{:S(2)}) copy-start(s32[1,1,2]{2,1,0:T(1,128)} %param.11) | copy-start | bytes 28
  3.0 7.4 %collective-permute-start.1 = (f32[128,128]{1,0:T(8,128)S(1)}, f32[128,128]{1,0:T(8,128)S(1)}, u32[]{:S(2)}, u32[]{:S(2)}) collective-permute-start(f32[128,128]{1,0:T(8,128)S(1)} %bitcast.20), channel_id=1, source_target_pairs={{0,2},{1,3},{2,0},{3,1},{4,6},{5,7},{6,4},{7,5},{8,10},{9,11},{10,... | collective-permute-start | bytes 196616 | tf_op jit(solution)/shard_map/ppermute | solution.py:29
  6.1 3.5 %collective-permute-start = (s32[2]{0:T(128)S(1)}, s32[2]{0:T(128)S(1)}, u32[]{:S(2)}, u32[]{:S(2)}) collective-permute-start(s32[2]{0:T(128)S(1)} %bitcast.22), channel_id=1, source_target_pairs={{0,2},{1,3},{2,0},{3,1},{4,6},{5,7},{6,4},{7,5},{8,10},{9,11},{10,... | collective-permute-start | bytes 32 | tf_op jit(solution)/shard_map/ppermute | solution.py:29
  6.7 1.2 %copy-start = (f32[1,2,2,256,256]{4,3,2,1,0:T(8,128)S(1)}, f32[1,2,2,256,256]{4,3,2,1,0:T(8,128)}, u32[]{:S(2)}) copy-start(f32[1,2,2,256,256]{4,3,2,1,0:T(8,128)} %param.8) | copy-start | bytes 3145732
  7.9 1.7 %copy-start.1 = (f32[1,2,2,256,256]{4,3,2,1,0:T(8,128)S(1)}, f32[1,2,2,256,256]{4,3,2,1,0:T(8,128)}, u32[]{:S(2)}) copy-start(f32[1,2,2,256,256]{4,3,2,1,0:T(8,128)} %param.8) | copy-start | bytes 3145732
  12.9 1.5 %collective-permute-start.3 = (f32[2,2,128,128]{3,2,1,0:T(8,128)S(1)}, f32[2,2,128,128]{3,2,1,0:T(8,128)S(1)}, u32[]{:S(2)}, u32[]{:S(2)}) collective-permute-start(f32[2,2,128,128]{3,2,1,0:T(8,128)S(1)} %collective-permute-done.2.refs_10_), channel_id=1, source_target_pairs={{0,1},{1,0},{2,3},{3,2},{4,5},{5,4},{6,7},{7,6},{8,9},{9,8},{10,11... | collective-permute-start | bytes 786440 | tf_op jit(solution)/shard_map/ppermute | solution.py:29
  18.6 1.4 %collective-permute-start.4 = (f32[2,128,128]{2,1,0:T(8,128)S(1)}, f32[2,128,128]{2,1,0:T(8,128)S(1)}, u32[]{:S(2)}, u32[]{:S(2)}) collective-permute-start(f32[2,128,128]{2,1,0:T(8,128)S(1)} %get-tuple-element.35), channel_id=1, source_target_pairs={{0,1},{1,0},{2,3},{3,2},{4,5},{5,4},{6,7},{7,6},{8,9},{9,8},{10,11... | collective-permute-start | bytes 393224 | tf_op jit(solution)/shard_map/ppermute | solution.py:29
  20.1 3.0 %collective-permute-start.5 = (f32[2,2,64,384]{3,2,1,0:T(8,128)S(1)}, f32[2,2,64,384]{3,2,1,0:T(8,128)S(1)}, u32[]{:S(2)}, u32[]{:S(2)}) collective-permute-start(f32[2,2,64,384]{3,2,1,0:T(8,128)S(1)} %get-tuple-element.36), channel_id=1, source_target_pairs={{0,1},{1,0},{2,3},{3,2},{4,5},{5,4},{6,7},{7,6},{8,9},{9,8},{10,11... | collective-permute-start | bytes 1179656 | tf_op jit(solution)/shard_map/ppermute | solution.py:29
  20.3 7.3 %collective-permute-start.7 = (f32[2,128,128]{2,1,0:T(8,128)S(1)}, f32[2,128,128]{2,1,0:T(8,128)S(1)}, u32[]{:S(2)}, u32[]{:S(2)}) collective-permute-start(f32[2,128,128]{2,1,0:T(8,128)S(1)} %add.26), channel_id=1, source_target_pairs={{0,16},{1,5},{2,18},{3,7},{4,20},{5,1},{6,22},{7,3},{8,24},{9,13},... | collective-permute-start | bytes 393224 | tf_op jit(solution)/shard_map/ppermute | solution.py:309
  27.6 5.7 %collective-permute-start.8 = (f32[2,128,128]{2,1,0:T(8,128)S(1)}, f32[2,128,128]{2,1,0:T(8,128)S(1)}, u32[]{:S(2)}, u32[]{:S(2)}) collective-permute-start(f32[2,128,128]{2,1,0:T(8,128)S(1)} %add.29), channel_id=1, source_target_pairs={{0,4},{1,9},{2,6},{3,11},{4,0},{5,13},{6,2},{7,15},{8,12},{9,1},{1... | collective-permute-start | bytes 393224 | tf_op jit(solution)/shard_map/ppermute | solution.py:309
  30.4 8.1 %collective-permute-start.6 = (f32[2,2,64,128]{3,2,1,0:T(8,128)S(1)}, f32[2,2,64,128]{3,2,1,0:T(8,128)S(1)}, u32[]{:S(2)}, u32[]{:S(2)}) collective-permute-start(f32[2,2,64,128]{3,2,1,0:T(8,128)S(1)} %slice.41), channel_id=1, source_target_pairs={{0,4},{4,8},{8,12},{12,16},{16,20},{20,24},{24,28},{1,5},{5,9},{9,... | collective-permute-start | bytes 393224 | tf_op jit(solution)/shard_map/ppermute | solution.py:25
  33.3 5.0 %collective-permute-start.9 = (f32[2,128,128]{2,1,0:T(8,128)S(1)}, f32[2,128,128]{2,1,0:T(8,128)S(1)}, u32[]{:S(2)}, u32[]{:S(2)}) collective-permute-start(f32[2,128,128]{2,1,0:T(8,128)S(1)} %add.30), channel_id=1, source_target_pairs={{0,8},{1,17},{2,10},{3,19},{4,12},{5,21},{6,14},{7,23},{8,0},{9,25... | collective-permute-start | bytes 393224 | tf_op jit(solution)/shard_map/ppermute | solution.py:309
  38.4 1.4 %collective-permute-start.10 = (f32[2,128,128]{2,1,0:T(8,128)S(1)}, f32[2,128,128]{2,1,0:T(8,128)S(1)}, u32[]{:S(2)}, u32[]{:S(2)}) collective-permute-start(f32[2,128,128]{2,1,0:T(8,128)S(1)} %add_multiply_fusion), channel_id=1, source_target_pairs={{0,1},{1,0},{2,3},{3,2},{4,5},{5,4},{6,7},{7,6},{8,9},{9,8},{10,11... | collective-permute-start | bytes 393224 | tf_op jit(solution)/shard_map/ppermute | solution.py:29
  38.5 1.3 %copy-start.7 = (f32[1,2,2,64,256]{4,3,2,1,0:T(8,128)}, f32[1,2,2,64,256]{4,3,2,1,0:T(8,128)S(1)}, u32[]{:S(2)}) copy-start(f32[1,2,2,64,256]{4,3,2,1,0:T(8,128)S(1)} %fusion.1) | copy-start | bytes 786436
